TPU v7x, 32 devices: a whole 2x2x4 slice. The times are simulated.
32 devices in a mesh: seq: 4 (over y, x), wide: 8 (over z, core).
Axes of the slice: x: 2, y: 2, z: 4, core: 2. Of those that a mesh axis runs over, the one named last changes fastest.
Arguments:
- inputs: bfloat16 [8, 1024, 2048], P('seq', 'wide'), may hold values from -9 to 9
- lengths: int32 [8], P('seq'), may hold values from 256 to 1024, as said below
- norm_gain: bfloat16 [2048], P('wide'), may hold values from 0.5 to 1.5
- gelu_weight: bfloat16 [2048, 2560], P('wide'), may hold values from -0.125 to 0.125
- branch_weight: bfloat16 [2048, 2560], P('wide'), may hold values from -0.125 to 0.125
- forget_gates: bfloat16 [2560, 256], P('wide'), may hold values from -0.375 to 0.375
- admit_gates: bfloat16 [2560, 256], P('wide'), may hold values from -0.375 to 0.375
- forget_bias: bfloat16 [2560], P('wide'), may hold values from -4 to 4
- admit_bias: bfloat16 [2560], P('wide'), may hold values from -4 to 4
- decay_rate: bfloat16 [2560], P('wide'), may hold values from 3.6478043e-05 to 0.019897461
- conv_weight: bfloat16 [4, 2560], P(None, 'wide'), may hold values from -3 to 3
- conv_bias: bfloat16 [2560], P('wide'), may hold values from -3 to 3
- out_weight: bfloat16 [2560, 2048], P('wide'), may hold values from -0.5 to 0.5
- mlp_gain: bfloat16 [2048], P('wide'), may hold values from 0.5 to 1.5
- gate_weight: bfloat16 [2048, 6144], P('wide', 'seq'), may hold values from -0.125 to 0.125
- up_weight: bfloat16 [2048, 6144], P('wide', 'seq'), may hold values from -0.125 to 0.125
- down_weight: bfloat16 [6144, 2048], P('seq', 'wide'), may hold values from -0.15625 to 0.15625
- cotangent: bfloat16 [8, 1024, 2048], P('seq', 'wide'), may hold values from -6 to 6
Outputs:
- output: bfloat16 [8, 1024, 2048], P('seq', 'wide')
- inputs_grad: float32 [8, 1024, 2048], P('seq', 'wide')
- norm_gain_grad: float32 [2048], P('wide')
- gelu_weight_grad: float32 [2048, 2560], P('wide')
- branch_weight_grad: float32 [2048, 2560], P('wide')
- forget_gates_grad: float32 [2560, 256], P('wide')
- admit_gates_grad: float32 [2560, 256], P('wide')
- forget_bias_grad: float32 [2560], P('wide')
- admit_bias_grad: float32 [2560], P('wide')
- decay_rate_grad: float32 [2560], P('wide')
- conv_weight_grad: float32 [4, 2560], P(None, 'wide')
- conv_bias_grad: float32 [2560], P('wide')
- out_weight_grad: float32 [2560, 2048], P('wide')
- mlp_gain_grad: float32 [2048], P('wide')
- gate_weight_grad: float32 [2048, 6144], P('wide', 'seq')
- up_weight_grad: float32 [2048, 6144], P('wide', 'seq')
- down_weight_grad: float32 [6144, 2048], P('seq', 'wide')
- statistics: float32 [3], replicated
Inputs may be any that keep to these rules, and one draw needn't show every extreme that they name: `lengths`: in each group of 2 consecutive sequences one, drawn from the seed, has all 1024 tokens valid.
All inputs are finite; a program needn't handle non-finite values.
Results may differ from a plain program's by a relative error of at most 0.011.
Values may be sent and summed in bfloat16 or wider, within the bound.
A program may use at most 320 MiB of HBM per device.

v0:
```python
import math

import jax
import jax.numpy as jnp
from jax import lax
from jax.sharding import PartitionSpec as P

R = 2560
NBLK = 10
BW = 256
CONV = 4


def rms_norm(values, gain):
    return values * lax.rsqrt(jnp.mean(values * values, axis=-1, keepdims=True) + 1e-06) * gain


def contract_last(left, right):
    return lax.dot_general(
        left, right, (((1,), (1,)), ((), ())), preferred_element_type=jnp.float32
    )


def contract_rows(left, right):
    return lax.dot_general(
        left, right, (((0,), (0,)), ((), ())), preferred_element_type=jnp.float32
    )


def combine_pairs(earlier, later):
    return (earlier[0] * later[0], later[0] * earlier[1] + later[1])


def block_gates(values, weight, bias):
    count = values.shape[0]
    blocks = values.reshape(count, NBLK, BW)
    mixed = jnp.einsum(
        "tki,kij->tkj", blocks, weight.reshape(NBLK, BW, BW), preferred_element_type=jnp.float32
    )
    return (mixed.reshape(count, R) + bias).astype(jnp.bfloat16)


def causal_conv(conv_in, taps_weight, taps_bias, before):
    taps = taps_weight.shape[0]
    steps = conv_in.shape[1]
    padded = jnp.concatenate([before, conv_in], axis=1)
    conv_out = taps_bias
    for offset in range(taps):
        conv_out = (
            conv_out
            + taps_weight[offset] * padded[:, taps - 1 - offset : taps - 1 - offset + steps, :]
        )
    return conv_out


def local_recurrence(
    conv_in, forget_logits, admit_logits, decay_values, taps_weight, taps_bias, before
):
    seqs, steps, width = conv_in.shape
    conv_out = causal_conv(conv_in, taps_weight, taps_bias, before)
    log_rate = -8.0 * decay_values * (0.1 + 0.9 * jax.nn.sigmoid(forget_logits))
    drive = jnp.sqrt(-jnp.expm1(2.0 * log_rate)) * jax.nn.sigmoid(admit_logits) * conv_out
    block_len = math.gcd(steps, 128)
    count = steps // block_len
    rate_blocks = log_rate.reshape(seqs, count, block_len, width)
    drive_blocks = drive.reshape(seqs, count, block_len, width)
    within = jnp.cumsum(rate_blocks, axis=2)
    inner = jnp.exp(within) * jnp.cumsum(jnp.exp(-within) * drive_blocks, axis=2)
    ends = within[:, :, -1, :]
    unused_decays, end_states = lax.associative_scan(
        combine_pairs, (jnp.exp(ends), inner[:, :, -1, :]), axis=1
    )
    carry_in = jnp.concatenate(
        [jnp.zeros((seqs, 1, width), jnp.float32), end_states[:, :-1, :]], axis=1
    )
    offsets = jnp.cumsum(ends, axis=1) - ends
    carried = inner + jnp.exp(within) * carry_in[:, :, None, :]
    products = jnp.exp(within + offsets[:, :, None, :])
    return (carried.reshape(seqs, steps, width), products.reshape(seqs, steps, width))


def body(
    inputs,
    lengths,
    norm_gain,
    gelu_weight,
    branch_weight,
    forget_gates,
    admit_gates,
    forget_bias,
    admit_bias,
    decay_rate,
    conv_weight,
    conv_bias,
    out_weight,
    mlp_gain,
    gate_weight,
    up_weight,
    down_weight,
    cotangent,
):
    gathered = (
        lax.all_gather(norm_gain, "wide", axis=0, tiled=True),
        lax.all_gather(gelu_weight, "wide", axis=0, tiled=True),
        lax.all_gather(branch_weight, "wide", axis=0, tiled=True),
        lax.all_gather(forget_gates, "wide", axis=0, tiled=True),
        lax.all_gather(admit_gates, "wide", axis=0, tiled=True),
        lax.all_gather(forget_bias, "wide", axis=0, tiled=True),
        lax.all_gather(admit_bias, "wide", axis=0, tiled=True),
        lax.all_gather(decay_rate, "wide", axis=0, tiled=True),
        lax.all_gather(conv_weight, "wide", axis=1, tiled=True),
        lax.all_gather(conv_bias, "wide", axis=0, tiled=True),
        lax.all_gather(out_weight, "wide", axis=0, tiled=True),
        lax.all_gather(mlp_gain, "wide", axis=0, tiled=True),
        lax.all_gather(gate_weight, "wide", axis=0, tiled=True),
        lax.all_gather(up_weight, "wide", axis=0, tiled=True),
        lax.all_gather(down_weight, "wide", axis=1, tiled=True),
    )
    (
        gain_one,
        gelu_full,
        branch_full,
        forget_full,
        admit_full,
        forget_shift,
        admit_shift,
        decay_full,
        taps_full,
        taps_bias_full,
        out_full,
        gain_two,
        gate_full,
        up_full,
        down_full,
    ) = gathered
    seqs, tokens, width = inputs.shape
    rows = seqs * tokens
    flat = inputs.reshape(rows, width).astype(jnp.float32)
    gain_one = gain_one.astype(jnp.float32)
    gain_two = gain_two.astype(jnp.float32)
    decay_values = decay_full.astype(jnp.float32)
    taps_weight = taps_full.astype(jnp.float32)
    taps_bias = taps_bias_full.astype(jnp.float32)
    normed_low = rms_norm(flat, gain_one).astype(jnp.bfloat16)
    branch_y = jnp.dot(normed_low, gelu_full, preferred_element_type=jnp.float32)
    branch_x = jnp.dot(normed_low, branch_full, preferred_element_type=jnp.float32).astype(
        jnp.bfloat16
    )
    forget_logits = block_gates(branch_x, forget_full, forget_shift.astype(jnp.float32))
    admit_logits = block_gates(branch_x, admit_full, admit_shift.astype(jnp.float32))
    conv_seq = branch_x.reshape(seqs, tokens, R)
    forget_seq = forget_logits.reshape(seqs, tokens, R)
    admit_seq = admit_logits.reshape(seqs, tokens, R)
    share = R // lax.axis_size("wide")
    start = lax.axis_index("wide") * share
    conv_ch, forget_ch, admit_ch = (
        lax.all_to_all(conv_seq, "wide", split_axis=2, concat_axis=1, tiled=True),
        lax.all_to_all(forget_seq, "wide", split_axis=2, concat_axis=1, tiled=True),
        lax.all_to_all(admit_seq, "wide", split_axis=2, concat_axis=1, tiled=True),
    )
    decay_ch = lax.dynamic_slice_in_dim(decay_values, start, share, 0)
    taps_ch = lax.dynamic_slice_in_dim(taps_weight, start, share, 1)
    taps_bias_ch = lax.dynamic_slice_in_dim(taps_bias, start, share, 0)
    before = jnp.zeros((seqs, CONV - 1, share), jnp.float32)
    (carried_ch, products), pullback = jax.vjp(
        local_recurrence,
        conv_ch.astype(jnp.float32),
        forget_ch.astype(jnp.float32),
        admit_ch.astype(jnp.float32),
        decay_ch,
        taps_ch,
        taps_bias_ch,
        before,
    )
    state_low = lax.all_to_all(
        carried_ch.astype(jnp.bfloat16), "wide", split_axis=1, concat_axis=2, tiled=True
    )
    state_values = state_low.reshape(rows, R).astype(jnp.float32)
    gelu_y = jax.nn.gelu(branch_y)
    mixed_low = (state_values * gelu_y).astype(jnp.bfloat16)
    temporal = jnp.dot(mixed_low, out_full, preferred_element_type=jnp.float32)
    stream = flat + temporal
    normed_two = rms_norm(stream, gain_two).astype(jnp.bfloat16)
    normed_all, upstream_all = (
        lax.all_gather(normed_two.reshape(seqs, tokens, width), "seq", axis=0, tiled=True),
        lax.all_gather(cotangent, "seq", axis=0, tiled=True),
    )
    group_rows = normed_all.shape[0] * tokens
    normed_all = normed_all.reshape(group_rows, width)
    upstream_all = upstream_all.reshape(group_rows, width)
    gate = jnp.dot(normed_all, gate_full, preferred_element_type=jnp.float32)
    up_values = jnp.dot(normed_all, up_full, preferred_element_type=jnp.float32)
    gelu_gate = jax.nn.gelu(gate)
    hidden_low = (gelu_gate * up_values).astype(jnp.bfloat16)
    feed = lax.psum_scatter(
        jnp.dot(hidden_low, down_full, preferred_element_type=jnp.float32),
        "seq",
        scatter_dimension=0,
        tiled=True,
    )
    result = stream + feed
    output = result.astype(jnp.bfloat16).reshape(seqs, tokens, width)
    position = lax.axis_index("wide") * tokens + jnp.arange(tokens, dtype=jnp.int32)
    valid = (position[None, :] < lengths[:, None]).astype(jnp.float32).reshape(rows, 1)
    partial_sums = jnp.stack(
        [
            jnp.sum(valid * result * result),
            jnp.sum(valid * temporal * temporal),
            jnp.sum(valid * feed * feed),
            jnp.sum(valid),
        ]
    )
    upstream = cotangent.reshape(rows, width)
    hidden_grad = contract_last(upstream_all, down_full)
    down_grad = contract_rows(hidden_low, upstream_all)
    unused_gelu, gelu_gate_pull = jax.vjp(jax.nn.gelu, gate)
    (gate_pre,) = gelu_gate_pull(hidden_grad * up_values)
    gate_rows = gate_pre.astype(jnp.bfloat16)
    up_rows = (hidden_grad * gelu_gate).astype(jnp.bfloat16)
    gate_grad = contract_rows(normed_all, gate_rows)
    up_grad = contract_rows(normed_all, up_rows)
    normed_two_grad = lax.psum_scatter(
        contract_last(gate_rows, gate_full) + contract_last(up_rows, up_full),
        "seq",
        scatter_dimension=0,
        tiled=True,
    )
    unused_norm, norm_two_pull = jax.vjp(rms_norm, stream, gain_two)
    stream_part, gain_two_grad = norm_two_pull(normed_two_grad)
    stream_grad = upstream.astype(jnp.float32) + stream_part
    stream_low = stream_grad.astype(jnp.bfloat16)
    mixed_grad = contract_last(stream_low, out_full)
    out_grad = contract_rows(mixed_low, stream_low)
    state_grad = (mixed_grad * gelu_y).astype(jnp.bfloat16)
    unused_branch, gelu_y_pull = jax.vjp(jax.nn.gelu, branch_y)
    (branch_pre,) = gelu_y_pull(mixed_grad * state_values)
    y_rows = branch_pre.astype(jnp.bfloat16)
    state_grad_ch = lax.all_to_all(
        state_grad.reshape(seqs, tokens, R), "wide", split_axis=2, concat_axis=1, tiled=True
    )
    (
        conv_grad_ch,
        forget_grad_ch,
        admit_grad_ch,
        decay_grad_ch,
        taps_grad_ch,
        taps_bias_grad_ch,
        unused_edge,
    ) = pullback((state_grad_ch.astype(jnp.float32), jnp.zeros_like(products)))
    conv_low, forget_low, admit_low = (
        lax.all_to_all(
            conv_grad_ch.astype(jnp.bfloat16), "wide", split_axis=1, concat_axis=2, tiled=True
        ),
        lax.all_to_all(
            forget_grad_ch.astype(jnp.bfloat16), "wide", split_axis=1, concat_axis=2, tiled=True
        ),
        lax.all_to_all(
            admit_grad_ch.astype(jnp.bfloat16), "wide", split_axis=1, concat_axis=2, tiled=True
        ),
    )
    decay_grad = lax.dynamic_update_slice_in_dim(
        jnp.zeros((R,), jnp.float32), decay_grad_ch, start, 0
    )
    taps_grad = lax.dynamic_update_slice_in_dim(
        jnp.zeros((CONV, R), jnp.float32), taps_grad_ch, start, 1
    )
    taps_bias_grad = lax.dynamic_update_slice_in_dim(
        jnp.zeros((R,), jnp.float32), taps_bias_grad_ch, start, 0
    )
    forget_rows = forget_low.reshape(rows, NBLK, BW)
    admit_rows = admit_low.reshape(rows, NBLK, BW)
    branch_blocks = branch_x.reshape(rows, NBLK, BW)
    forget_grad = jnp.einsum(
        "tki,tkj->kij", branch_blocks, forget_rows, preferred_element_type=jnp.float32
    ).reshape(R, BW)
    admit_grad = jnp.einsum(
        "tki,tkj->kij", branch_blocks, admit_rows, preferred_element_type=jnp.float32
    ).reshape(R, BW)
    forget_bias_grad = jnp.sum(forget_low.reshape(rows, R).astype(jnp.float32), axis=0)
    admit_bias_grad = jnp.sum(admit_low.reshape(rows, R).astype(jnp.float32), axis=0)
    branch_back = jnp.einsum(
        "tkj,kij->tki",
        forget_rows,
        forget_full.reshape(NBLK, BW, BW),
        preferred_element_type=jnp.float32,
    )
    branch_back = branch_back + jnp.einsum(
        "tkj,kij->tki",
        admit_rows,
        admit_full.reshape(NBLK, BW, BW),
        preferred_element_type=jnp.float32,
    )
    branch_rows = (
        branch_back.reshape(rows, R) + conv_low.reshape(rows, R).astype(jnp.float32)
    ).astype(jnp.bfloat16)
    normed_grad = contract_last(branch_rows, branch_full) + contract_last(y_rows, gelu_full)
    branch_grad = contract_rows(normed_low, branch_rows)
    gelu_grad = contract_rows(normed_low, y_rows)
    unused_first, norm_one_pull = jax.vjp(rms_norm, flat, gain_one)
    flat_part, gain_one_grad = norm_one_pull(normed_grad)
    inputs_grad = (stream_grad + flat_part).reshape(seqs, tokens, width)
    stat_terms = jnp.tile(partial_sums, lax.axis_size("wide"))
    wide_parts = (
        lax.psum_scatter(gain_one_grad, "wide", scatter_dimension=0, tiled=True),
        lax.psum_scatter(gelu_grad, "wide", scatter_dimension=0, tiled=True),
        lax.psum_scatter(branch_grad, "wide", scatter_dimension=0, tiled=True),
        lax.psum_scatter(forget_grad, "wide", scatter_dimension=0, tiled=True),
        lax.psum_scatter(admit_grad, "wide", scatter_dimension=0, tiled=True),
        lax.psum_scatter(forget_bias_grad, "wide", scatter_dimension=0, tiled=True),
        lax.psum_scatter(admit_bias_grad, "wide", scatter_dimension=0, tiled=True),
        lax.psum_scatter(decay_grad, "wide", scatter_dimension=0, tiled=True),
        lax.psum_scatter(taps_grad, "wide", scatter_dimension=1, tiled=True),
        lax.psum_scatter(taps_bias_grad, "wide", scatter_dimension=0, tiled=True),
        lax.psum_scatter(out_grad, "wide", scatter_dimension=0, tiled=True),
        lax.psum_scatter(gain_two_grad, "wide", scatter_dimension=0, tiled=True),
        lax.psum_scatter(gate_grad, "wide", scatter_dimension=0, tiled=True),
        lax.psum_scatter(up_grad, "wide", scatter_dimension=0, tiled=True),
        lax.psum_scatter(down_grad, "wide", scatter_dimension=1, tiled=True),
        lax.psum_scatter(stat_terms, "wide", scatter_dimension=0, tiled=True),
    )
    seq_parts = lax.psum(
        (
            wide_parts[0],
            wide_parts[1],
            wide_parts[2],
            wide_parts[3],
            wide_parts[4],
            wide_parts[5],
            wide_parts[6],
            wide_parts[7],
            wide_parts[8],
            wide_parts[9],
            wide_parts[10],
            wide_parts[11],
            wide_parts[15],
        ),
        "seq",
    )
    totals = seq_parts[12]
    statistics = jnp.sqrt(totals[0:3] / (totals[3] * width))
    return (
        output,
        inputs_grad,
        seq_parts[0],
        seq_parts[1],
        seq_parts[2],
        seq_parts[3],
        seq_parts[4],
        seq_parts[5],
        seq_parts[6],
        seq_parts[7],
        seq_parts[8],
        seq_parts[9],
        seq_parts[10],
        seq_parts[11],
        wide_parts[12],
        wide_parts[13],
        wide_parts[14],
        statistics,
    )


def solution(mesh):
    in_specs = (
        P("seq", "wide", None),
        P("seq"),
        P("wide"),
        P("wide", None),
        P("wide", None),
        P("wide", None),
        P("wide", None),
        P("wide"),
        P("wide"),
        P("wide"),
        P(None, "wide"),
        P("wide"),
        P("wide", None),
        P("wide"),
        P("wide", "seq"),
        P("wide", "seq"),
        P("seq", "wide"),
        P("seq", "wide", None),
    )
    out_specs = (
        P("seq", "wide", None),
        P("seq", "wide", None),
        P("wide"),
        P("wide", None),
        P("wide", None),
        P("wide", None),
        P("wide", None),
        P("wide"),
        P("wide"),
        P("wide"),
        P(None, "wide"),
        P("wide"),
        P("wide", None),
        P("wide"),
        P("wide", "seq"),
        P("wide", "seq"),
        P("seq", "wide"),
        P(),
    )
    return jax.shard_map(body, mesh=mesh, in_specs=in_specs, out_specs=out_specs, check_vma=False)
```

profile of v0, /device:TPU:0, one launch (start us, length us, event | category | flops | bytes accessed | tf_op | source)
XLA Modules:
  0.0 2542.3 jit_solution(6336902962082683540)
XLA Ops:
  13.0 31.3 %all-reduce.52 = (bf16[2560]{0:T(1024)(128)(2,1)S(1)}, bf16[2560]{0:T(1024)(128)(2,1)S(1)}, bf16[2560]{0:T(1024)(128)(2,1)S(1)}, bf16[2560]{0:T(1024)(128)(2,1)S(1)}) all-reduce(bf16[2560]{0:T(1024)(128)(2,1)S(1)} %dynamic-update-slice.1, bf16[2560]{0:T(1024)(128)(2,1)S(1)} %dynamic-update-slice, ...), channel_id=1, replica_groups=mesh['seq'=4,'wide'=8] {'wide'}, use_global_device_ids=true, to_apply=%add.39 | all-reduce | flops 10240 | bytes 40960
  54.2 58.0 %all-gather.14.cloned.1.call-done = bf16[2048,2560]{1,0:T(8,128)(2,1)} async-done(((bf16[256,2560]{1,0:T(8,128)(2,1)}), bf16[2048,2560]{1,0:T(8,128)(2,1)}) %all-gather.14.cloned.1.call-update) | async-done | bytes 10485776 | tf_op jit(solution)/shard_map/all_gather | solution.py:105
  178.3 40.5 %all-to-all-done = bf16[2,128,2560]{1,0,2:T(2,128)(2,1)} async-done(((bf16[2,128,2560]{1,0,2:T(2,128)(2,1)}), bf16[2,128,2560]{1,0,2:T(2,128)(2,1)}, u32[]{:S(2)}, u32[]{:S(2)}) %all-to-all-start) | async-done | bytes 1310752 | tf_op jit(solution)/shard_map/all_to_all | solution.py:158
  223.4 73.1 %all-gather.1 = bf16[8,320,4]{1,2,0:T(4,128)(2,1)S(1)} all-gather(bf16[1,320,4]{1,2,0:T(4,128)(2,1)S(1)} %bitcast.359), channel_id=1, replica_groups=mesh['seq'=4,'wide'=8] {'wide'}, dimensions={0}, use_global_device_ids=true | all-gather | bytes 23040 | tf_op jit(solution)/shard_map/all_gather | solution.py:111
  337.7 31.9 %all-to-all-done.2 = bf16[2,128,2560]{1,0,2:T(2,128)(2,1)} async-done(((bf16[2,128,2560]{1,0,2:T(2,128)(2,1)}), bf16[2,128,2560]{1,0,2:T(2,128)(2,1)}, u32[]{:S(2)}, u32[]{:S(2)}) %all-to-all-start.2) | async-done | bytes 1310752 | tf_op jit(solution)/shard_map/all_to_all | solution.py:157
  414.6 33.3 %all-gather.2 = bf16[8,1,256]{2,1,0:T(2,128)(2,1)S(1)} all-gather(bf16[1,1,256]{2,1,0:T(2,128)(2,1)S(1)} %reshape.389), channel_id=1, replica_groups=mesh['seq'=4,'wide'=8] {'wide'}, dimensions={0}, use_global_device_ids=true | all-gather | bytes 4608 | tf_op jit(solution)/shard_map/all_gather | solution.py:114
  516.5 53.8 %all-gather.24.cloned.1.call-done = bf16[8,128,2048]{2,1,0:T(8,128)(2,1)} async-done(((bf16[2,128,2048]{2,1,0:T(8,128)(2,1)}), bf16[8,128,2048]{2,1,0:T(8,128)(2,1)}) %all-gather.24.cloned.1.call-update) | async-done | bytes 4194320 | tf_op jit(solution)/shard_map/all_gather | solution.py:185
  582.1 54.7 %all-gather.28.cloned.1.call-done = bf16[2048,1536]{1,0:T(8,128)(2,1)} async-done(((bf16[256,1536]{1,0:T(8,128)(2,1)}), bf16[2048,1536]{1,0:T(8,128)(2,1)}) %all-gather.28.cloned.1.call-update) | async-done | bytes 6291472 | tf_op jit(solution)/shard_map/all_gather | solution.py:116
  648.4 41.5 %all-gather.32.cloned.1.call-done = bf16[8,128,2048]{2,1,0:T(8,128)(2,1)} async-done(((bf16[2,128,2048]{2,1,0:T(8,128)(2,1)}), bf16[8,128,2048]{2,1,0:T(8,128)(2,1)}) %all-gather.32.cloned.1.call-update) | async-done | bytes 4194320 | tf_op jit(solution)/shard_map/all_gather | solution.py:186
  690.0 66.6 %all-gather.30.cloned.1.call-done = bf16[1536,2048]{1,0:T(8,128)(2,1)} async-done(((bf16[1536,256]{1,0:T(8,128)(2,1)}), bf16[1536,2048]{1,0:T(8,128)(2,1)}) %all-gather.30.cloned.1.call-update) | async-done | bytes 6291472 | tf_op jit(solution)/shard_map/all_gather | solution.py:117
  808.4 72.3 %reduce-scatter.16.cloned.1.call-done = f32[256,2048]{1,0:T(8,128)} async-done(((f32[1024,2048]{1,0:T(8,128)}), f32[256,2048]{1,0:T(8,128)}) %reduce-scatter.16.cloned.1.call-update) | async-done | bytes 2097168 | tf_op jit(solution)/shard_map/reduce_scatter | solution.py:222
  880.7 89.6 %reduce-scatter.14.cloned.1.call-done = f32[256,2048]{1,0:T(8,128)} async-done(((f32[1024,2048]{1,0:T(8,128)}), f32[256,2048]{1,0:T(8,128)}) %reduce-scatter.14.cloned.1.call-update) | async-done | bytes 2097168 | tf_op jit(solution)/shard_map/reduce_scatter | solution.py:195
  996.1 37.2 %all_to_all.86 = bf16[2,128,2560]{1,0,2:T(2,128)(2,1)S(1)} all-to-all(bf16[2,128,2560]{1,0,2:T(2,128)(2,1)} %copy.482), channel_id=1, replica_groups=mesh['seq'=4,'wide'=8] {'wide'}, dimensions={2} | all-to-all | bytes 2621440 | tf_op jit(solution)/shard_map/all_to_all | solution.py:238
  1112.3 40.3 %all_to_all.84 = bf16[2,1024,320]{2,0,1:T(2,128)(2,1)S(1)} all-to-all(bf16[2,1024,320]{2,0,1:T(2,128)(2,1)S(1)} %copy.494), channel_id=1, replica_groups=mesh['seq'=4,'wide'=8] {'wide'}, dimensions={1} | all-to-all | bytes 2621440 | tf_op jit(solution)/shard_map/all_to_all | solution.py:254
  1166.2 59.9 %all_to_all.85 = bf16[2,1024,320]{2,0,1:T(2,128)(2,1)} all-to-all(bf16[2,1024,320]{2,0,1:T(2,128)(2,1)S(1)} %copy.497), channel_id=1, replica_groups=mesh['seq'=4,'wide'=8] {'wide'}, dimensions={1} | all-to-all | bytes 2621440 | tf_op jit(solution)/shard_map/all_to_all | solution.py:257
  1270.8 55.8 %all-to-all-done.7 = bf16[2,1024,320]{2,0,1:T(2,128)(2,1)S(1)} async-done(((bf16[2,1024,320]{2,0,1:T(2,128)(2,1)}), bf16[2,1024,320]{2,0,1:T(2,128)(2,1)S(1)}, u32[]{:S(2)}, u32[]{:S(2)}) %all-to-all-start.7) | async-done | bytes 1310752 | tf_op jit(solution)/shard_map/all_to_all | solution.py:251
  1394.7 103.1 %reduce-scatter.26.cloned.1.call-done = f32[320,2048]{1,0:T(8,128)} async-done(((f32[2560,2048]{1,0:T(8,128)}), f32[320,2048]{1,0:T(8,128)}) %reduce-scatter.26.cloned.1.call-update) | async-done | bytes 2621456 | tf_op jit(solution)/shard_map/reduce_scatter | solution.py:314
  1497.9 214.8 %reduce-scatter.18.cloned.1.call-done = f32[256,2560]{1,0:T(8,128)} async-done(((f32[2048,2560]{1,0:T(8,128)}), f32[256,2560]{1,0:T(8,128)}) %reduce-scatter.18.cloned.1.call-update) | async-done | bytes 2621456 | tf_op jit(solution)/shard_map/reduce_scatter | solution.py:305
  1712.7 208.3 %reduce-scatter.20.cloned.1.call-done = f32[256,2560]{1,0:T(8,128)} async-done(((f32[2048,2560]{1,0:T(8,128)}), f32[256,2560]{1,0:T(8,128)}) %reduce-scatter.20.cloned.1.call-update) | async-done | bytes 2621456 | tf_op jit(solution)/shard_map/reduce_scatter | solution.py:306
  1982.8 30.0 %all-reduce.49 = (f32[2048]{0:T(1024)S(1)}, f32[2560]{0:T(1024)S(1)}, f32[2560]{0:T(1024)S(1)}, f32[2560]{0:T(1024)S(1)}, f32[2560]{0:T(1024)S(1)}, /*index=5*/f32[2048]{0:T(1024)S(1)}, f32[32]{0:T(128)S(1)}) all-reduce(f32[2048]{0:T(1024)S(1)} %get-tuple-element.23, ...), channel_id=4, replica_groups=mesh['seq'=4,'wide'=8] {'wide'}, use_global_device_ids=true, to_apply=%region_15.16.clone | all-reduce | flops 14368 | bytes 114944
  2035.4 51.5 %reduce-scatter.28.cloned.1.call-done = f32[256,1536]{1,0:T(8,128)} async-done(((f32[2048,1536]{1,0:T(8,128)}), f32[256,1536]{1,0:T(8,128)}) %reduce-scatter.28.cloned.1.call-update) | async-done | bytes 1572880 | tf_op jit(solution)/shard_map/reduce_scatter | solution.py:316
  2086.9 130.3 %reduce-scatter.30.cloned.1.call-done = f32[256,1536]{1,0:T(8,128)} async-done(((f32[2048,1536]{1,0:T(8,128)}), f32[256,1536]{1,0:T(8,128)}) %reduce-scatter.30.cloned.1.call-update) | async-done | bytes 1572880 | tf_op jit(solution)/shard_map/reduce_scatter | solution.py:317
  2217.2 130.5 %reduce-scatter.32.cloned.1.call-done = f32[1536,256]{1,0:T(8,128)} async-done(((f32[1536,2048]{1,0:T(8,128)}), f32[1536,256]{1,0:T(8,128)}) %reduce-scatter.32.cloned.1.call-update) | async-done | bytes 1572880 | tf_op jit(solution)/shard_map/reduce_scatter | solution.py:318
  2347.7 179.2 %all-reduce.55.cloned.1.call-done = (f32[256,2560]{1,0:T(8,128)}, f32[256,2560]{1,0:T(8,128)}, f32[320,256]{1,0:T(8,128)}, f32[320,256]{1,0:T(8,128)}, f32[320,2048]{1,0:T(8,128)}) async-done(((f32[256,2560]{1,0:T(8,128)}, f32[256,2560]{1,0:T(8,128)}, f32[320,256]{1,0:T(8,128)}, f32[320,256]{1,0:T(8,128)}, f32[320,2048]{1,0:T(8,128)}), (f32[256,2560]{1,0:T(8,128)}, f32[256,2560]{1,0:T(8,128)}, ...) | async-done | bytes 8519696 | tf_op jit(solution)/shard_map/psum | solution.py:321
  (425 shorter events, 635.4 us)
Async XLA Ops:
  7.3 104.9 %all-gather.14.cloned.1.call-start = ((), (), s32[]{:S(2)}) async-start(), calls=%async_computation.19 | async-start | bytes 11796480 | tf_op jit(solution)/shard_map/all_gather | solution.py:105
  8.0 127.8 %all-gather.16.cloned.1.call-start = ((), (), s32[]{:S(2)}) async-start(), calls=%async_computation.20 | async-start | bytes 1474560 | tf_op jit(solution)/shard_map/all_gather | solution.py:106
  8.7 151.7 %all-gather.18.cloned.1.call-start = ((), (), s32[]{:S(2)}) async-start(), calls=%async_computation.21 | async-start | bytes 1474560 | tf_op jit(solution)/shard_map/all_gather | solution.py:107
  9.5 466.7 %all-gather.20.cloned.1.call-start = ((), (), s32[]{:S(2)}) async-start(), calls=%async_computation.22 | async-start | bytes 11796480 | tf_op jit(solution)/shard_map/all_gather | solution.py:104
  10.1 476.4 %all-gather.22.cloned.1.call-start = ((), (), s32[]{:S(2)}) async-start(), calls=%async_computation.23 | async-start | bytes 11796480 | tf_op jit(solution)/shard_map/all_gather | solution.py:113
  218.8 85.1 %all-to-all-start.1 = ((bf16[2,128,2560]{1,0,2:T(2,128)(2,1)}), bf16[2,128,2560]{1,0,2:T(2,128)(2,1)S(1)}, u32[]{:S(2)}, u32[]{:S(2)}) async-start(bf16[2,128,2560]{1,0,2:T(2,128)(2,1)} %add_convert_fusion.1), calls=%async_computation.1 | async-start | bytes 2621440 | tf_op jit(solution)/shard_map/all_to_all | solution.py:159
  222.8 293.7 %all-gather.26.cloned.1.call-start = ((), (), s32[]{:S(2)}) async-start(), calls=%async_computation.25 | async-start | bytes 7077888 | tf_op jit(solution)/shard_map/all_gather | solution.py:115
  305.0 64.7 %all-to-all-start.2 = ((bf16[2,128,2560]{1,0,2:T(2,128)(2,1)}), bf16[2,128,2560]{1,0,2:T(2,128)(2,1)}, u32[]{:S(2)}, u32[]{:S(2)}) async-start(bf16[2,128,2560]{1,0,2:T(2,128)(2,1)} %copy.470), calls=%async_computation.2 | async-start | bytes 2621440 | tf_op jit(solution)/shard_map/all_to_all | solution.py:157
  414.6 155.7 %all-gather.24.cloned.1.call-start = ((), (), s32[]{:S(2)}) async-start(), calls=%async_computation.24 | async-start | bytes 5242880 | tf_op jit(solution)/shard_map/all_gather | solution.py:185
  498.0 138.8 %all-gather.28.cloned.1.call-start = ((), (), s32[]{:S(2)}) async-start(), calls=%async_computation.26 | async-start | bytes 7077888 | tf_op jit(solution)/shard_map/all_gather | solution.py:116
  498.7 191.2 %all-gather.32.cloned.1.call-start = ((), (), s32[]{:S(2)}) async-start(), calls=%async_computation.29 | async-start | bytes 5242880 | tf_op jit(solution)/shard_map/all_gather | solution.py:186
  499.5 257.1 %all-gather.30.cloned.1.call-start = ((), (), s32[]{:S(2)}) async-start(), calls=%async_computation.27 | async-start | bytes 7077888 | tf_op jit(solution)/shard_map/all_gather | solution.py:117
  500.0 380.7 %reduce-scatter.16.cloned.1.call-start = ((), (), s32[]{:S(2)}) async-start(), calls=%async_computation.30 | async-start | bytes 10485760 | tf_op jit(solution)/shard_map/reduce_scatter | solution.py:222
  795.9 174.4 %reduce-scatter.14.cloned.1.call-start = ((), (), s32[]{:S(2)}) async-start(), calls=%async_computation.28 | async-start | bytes 10485760 | tf_op jit(solution)/shard_map/reduce_scatter | solution.py:195
  807.7 587.0 %reduce-scatter.22.cloned.1.call-start = ((), (), s32[]{:S(2)}) async-start(), calls=%async_computation.33 | async-start | bytes 2949120 | tf_op jit(solution)/shard_map/reduce_scatter | solution.py:307
  1161.9 232.8 %reduce-scatter.24.cloned.1.call-start = ((), (), s32[]{:S(2)}) async-start(), calls=%async_computation.34 | async-start | bytes 2949120 | tf_op jit(solution)/shard_map/reduce_scatter | solution.py:308
  1236.1 261.7 %reduce-scatter.26.cloned.1.call-start = ((), (), s32[]{:S(2)}) async-start(), calls=%async_computation.35 | async-start | bytes 23592960 | tf_op jit(solution)/shard_map/reduce_scatter | solution.py:314
  1247.8 464.9 %reduce-scatter.18.cloned.1.call-start = ((), (), s32[]{:S(2)}) async-start(), calls=%async_computation.31 | async-start | bytes 23592960 | tf_op jit(solution)/shard_map/reduce_scatter | solution.py:305
  1269.5 651.5 %reduce-scatter.20.cloned.1.call-start = ((), (), s32[]{:S(2)}) async-start(), calls=%async_computation.32 | async-start | bytes 23592960 | tf_op jit(solution)/shard_map/reduce_scatter | solution.py:306
  1352.1 602.7 %reduce-scatter.34.cloned.1.call-start = ((), (), s32[]{:S(2)}) async-start(), calls=%async_computation.39 | async-start | bytes 1474560
  1356.7 730.2 %reduce-scatter.28.cloned.1.call-start = ((), (), s32[]{:S(2)}) async-start(), calls=%async_computation.36 | async-start | bytes 14155776 | tf_op jit(solution)/shard_map/reduce_scatter | solution.py:316
  1369.3 847.9 %reduce-scatter.30.cloned.1.call-start = ((), (), s32[]{:S(2)}) async-start(), calls=%async_computation.37 | async-start | bytes 14155776 | tf_op jit(solution)/shard_map/reduce_scatter | solution.py:317
  1382.2 965.5 %reduce-scatter.32.cloned.1.call-start = ((), (), s32[]{:S(2)}) async-start(), calls=%async_computation.38 | async-start | bytes 14155776 | tf_op jit(solution)/shard_map/reduce_scatter | solution.py:318
  1394.6 1132.3 %all-reduce.55.cloned.1.call-start = ((), (), s32[]{:S(2)}) async-start(), calls=%async_computation.40 | async-start | bytes 17039360 | tf_op jit(solution)/shard_map/psum | solution.py:321
  (75 other events, 1303.5 us)
Sparse Core Ops, SparseCore 0:
  9.7 102.4 all-gather.13
  113.8 21.9 all-gather.15
  137.5 22.9 all-gather.17
  161.9 144.4 all-gather.19
  307.9 143.5 all-gather.21
  453.0 63.4 all-gather.25
  518.9 51.3 all-gather.23
  571.9 64.7 all-gather.27
  638.6 51.3 all-gather.31
  691.4 65.1 all-gather.29
  796.0 84.6 reduce-scatter.15
  883.9 86.3 reduce-scatter.13
  1162.0 56.4 reduce-scatter.21
  1236.3 35.6 reduce-scatter.23
  1274.1 223.7 reduce-scatter.25
  1500.1 212.5 reduce-scatter.17
  1714.9 206.0 reduce-scatter.19
  1923.1 31.7 reduce-scatter.33
  1957.7 129.1 reduce-scatter.27
  2089.6 127.5 reduce-scatter.29
  2220.1 127.5 reduce-scatter.31
  2352.1 174.7 all-reduce.54
where the time goes:
time: 2550 us; the launch traced here: 2540 us
  waiting for transfers between devices  1660 us (65%)
  blocking collectives  330 us (13%)
  matrix products  208 us (8%)
  local copies, waits for them, and re-layouts  160 us (6%)
  other arithmetic  138 us (5%)
    reduce_scatter x1, waiting for transfers between devices, body(): lax.psum_scatter(gelu_grad, 'wide', scatter_dimension=0, tiled=True)  215 us
    reduce_scatter x1, waiting for transfers between devices, body(): lax.psum_scatter(branch_grad, 'wide', scatter_dimension=0, tiled=True)  208 us
    psum x1, waiting for transfers between devices, body(): lax.psum((wide_parts[0], wide_parts[1], wide_parts[2], wide_parts[3], wid...  179 us
    reduce_scatter x1, waiting for transfers between devices, body(): lax.psum_scatter(down_grad, 'wide', scatter_dimension=1, tiled=True)  131 us
    reduce_scatter x1, waiting for transfers between devices, body(): lax.psum_scatter(up_grad, 'wide', scatter_dimension=0, tiled=True)  130 us
    reduce_scatter x1, waiting for transfers between devices, body(): lax.psum_scatter(out_grad, 'wide', scatter_dimension=0, tiled=True)  103 us
    reduce_scatter x1, waiting for transfers between devices, body(): lax.psum_scatter(jnp.dot(hidden_low, down_full, preferred_element_type=jn...  89.6 us
    all_gather x1, blocking collectives, body(): lax.all_gather(conv_weight, 'wide', axis=1, tiled=True)  73.1 us
  transfers between devices with their start and end apart: 27, of which 22 were waited for; matrix products, arithmetic and copies ran while one was open for 13% of the time, Pallas kernels for 0%

commit v1 on v0

v1 whole, which is shorter than its diff:
```python
import jax
import jax.numpy as jnp
from jax import lax
from jax.sharding import PartitionSpec as P

BW = 256
CONV = 4
HALO = 8
BF = jnp.bfloat16
F32 = jnp.float32


def dot(left, right):
    return jnp.dot(left, right, preferred_element_type=F32)


def contract_last(left, right):
    return lax.dot_general(left, right, (((1,), (1,)), ((), ())), preferred_element_type=F32)


def contract_rows(left, right):
    return lax.dot_general(left, right, (((0,), (0,)), ((), ())), preferred_element_type=F32)


def swap(values, mask):
    return lax.ppermute(values, "seq", [(i, i ^ mask) for i in range(lax.axis_size("seq"))])


def gather_seq(values):
    half = values.shape[0] // 2
    near = swap(values, 1)
    side = swap(values, 2)
    first = swap(near[:half], 2)
    second = swap(side[half:], 1)
    return [values, near, side, jnp.concatenate([first, second], axis=0)]


def reduce_seq(block_of):
    far = block_of(3).astype(BF)
    half = far.shape[0] // 2
    to_side = swap(far[:half], 1)
    to_near = swap(far[half:], 2)
    near = block_of(1)
    near = jnp.concatenate([near[:half], near[half:] + to_near.astype(F32)], axis=0).astype(BF)
    near = swap(near, 1)
    side = block_of(2)
    side = jnp.concatenate([side[:half] + to_side.astype(F32), side[half:]], axis=0).astype(BF)
    side = swap(side, 2)
    return block_of(0) + near.astype(F32) + side.astype(F32)


def inverse_rms(values):
    return lax.rsqrt(jnp.mean(values * values, axis=-1, keepdims=True) + 1e-06)


def rms_norm(values, gain):
    return values * inverse_rms(values) * gain


def rms_back(values, gain, grad):
    inv = inverse_rms(values)
    inner = jnp.mean(values * gain * grad, axis=-1, keepdims=True)
    return inv * gain * grad - values * (inv * inv * inv) * inner


def gelu_grad_of(values):
    c = 0.7978845608028654
    sq = values * values
    t = jnp.tanh(c * values * (1.0 + 0.044715 * sq))
    return 0.5 * (1.0 + t) + 0.5 * values * (1.0 - t * t) * c * (1.0 + 3.0 * 0.044715 * sq)


def body(
    inputs,
    lengths,
    norm_gain,
    gelu_weight,
    branch_weight,
    forget_gates,
    admit_gates,
    forget_bias,
    admit_bias,
    decay_rate,
    conv_weight,
    conv_bias,
    out_weight,
    mlp_gain,
    gate_weight,
    up_weight,
    down_weight,
    cotangent,
):
    groups = lax.axis_size("seq")
    wide = lax.axis_size("wide")
    s = lax.axis_index("seq")
    w = lax.axis_index("wide")
    seqs, tokens, width = inputs.shape
    rows = seqs * tokens
    total = groups * rows
    all_seqs = groups * seqs
    channels = gelu_weight.shape[1]
    share = channels // groups
    window = (share + BW - 1) // BW * BW
    blocks = window // BW

    def base_of(index):
        return jnp.minimum(index * share // BW * BW, channels - window)

    base = base_of(s)
    off = s * share - base
    quarter = width // groups
    gate_cols = 2 * BW // groups

    small = jnp.concatenate(
        [norm_gain, mlp_gain, forget_bias, admit_bias, decay_rate, conv_bias, conv_weight.reshape(-1)]
    )
    small = lax.all_gather(small, "wide").astype(F32)
    dw, rw = width // wide, channels // wide
    gain_one = small[:, :dw].reshape(1, width)
    gain_two = small[:, dw : 2 * dw].reshape(1, width)
    per_channel = small[:, 2 * dw :].reshape(wide, 8, rw).transpose(1, 0, 2).reshape(8, channels)
    per_channel = lax.dynamic_slice_in_dim(per_channel, s * share, share, 1)
    forget_shift, admit_shift, decay, taps_bias = (per_channel[i : i + 1] for i in range(4))
    taps = per_channel[4:8]

    branch_cols = lax.all_gather(
        lax.dynamic_slice_in_dim(branch_weight, base, window, 1), "wide", axis=0, tiled=True
    )
    gate_quarter = lax.all_gather(
        lax.dynamic_slice_in_dim(
            jnp.concatenate([forget_gates, admit_gates], axis=1), s * gate_cols, gate_cols, 1
        ),
        "wide",
        axis=0,
        tiled=True,
    )
    gelu_cols = lax.all_gather(
        lax.dynamic_slice_in_dim(gelu_weight, s * share, share, 1), "wide", axis=0, tiled=True
    )
    out_quarter = lax.all_gather(
        lax.dynamic_slice_in_dim(out_weight, s * quarter, quarter, 1), "wide", axis=0, tiled=True
    )
    mlp_full = lax.all_gather(
        jnp.concatenate([gate_weight, up_weight], axis=1), "wide", axis=0, tiled=True
    )
    down_full = lax.all_gather(down_weight, "wide", axis=1, tiled=True)
    hidden_units = gate_weight.shape[1]

    gates = jnp.zeros((window, groups * gate_cols), BF)
    out_rows = jnp.zeros((share, width), BF)
    for k in range(groups):
        other = s ^ k
        part = lax.dynamic_slice_in_dim(gate_quarter, base_of(other), window, 0)
        part = swap(part, k) if k else part
        gates = lax.dynamic_update_slice_in_dim(gates, part, other * gate_cols, 1)
    for k in range(groups):
        other = s ^ k
        part = lax.dynamic_slice_in_dim(out_quarter, other * share, share, 0)
        part = swap(part, k) if k else part
        out_rows = lax.dynamic_update_slice_in_dim(out_rows, part, other * quarter, 1)
    forget_blocks = gates[:, :BW].reshape(blocks, BW, BW)
    admit_blocks = gates[:, BW:].reshape(blocks, BW, BW)

    flat_low = inputs.reshape(rows, width)
    upstream = cotangent.reshape(rows, width)
    edge = lax.ppermute(
        inputs[:, tokens - HALO :, :].reshape(seqs * HALO, width),
        "wide",
        [(i, i + 1) for i in range(wide - 1)],
    )
    token_blocks = gather_seq(jnp.concatenate([flat_low, edge], axis=0))
    all_low = jnp.concatenate(
        [b[:rows] for b in token_blocks] + [b[rows:] for b in token_blocks], axis=0
    )
    upstream_all = jnp.concatenate(gather_seq(upstream), axis=0)
    normed_ext = rms_norm(all_low.astype(F32), gain_one).astype(BF)
    normed_all = normed_ext[:total]

    x_ext = dot(normed_ext, branch_cols).astype(BF)
    x_win = x_ext[:total]
    x_blocks = x_win.reshape(total, blocks, BW)

    def logits_of(weight, shift):
        mixed = jnp.einsum("tki,kij->tkj", x_blocks, weight, preferred_element_type=F32)
        mixed = lax.dynamic_slice_in_dim(mixed.reshape(total, window), off, share, 1)
        return (mixed + shift).astype(BF).reshape(all_seqs, tokens, share)

    forget_sig = jax.nn.sigmoid(logits_of(forget_blocks, forget_shift).astype(F32))
    admit_sig = jax.nn.sigmoid(logits_of(admit_blocks, admit_shift).astype(F32))
    x_own = lax.dynamic_slice_in_dim(x_ext, off, share, 1)
    before = x_own[total:].reshape(all_seqs, HALO, share)[:, HALO - (CONV - 1) :]
    padded = jnp.concatenate([before, x_own[:total].reshape(all_seqs, tokens, share)], axis=1)

    def shifted(k):
        return padded[:, CONV - 1 - k : CONV - 1 - k + tokens, :].astype(F32)

    conv_out = taps_bias
    for k in range(CONV):
        conv_out = conv_out + taps[k] * shifted(k)
    span = 0.1 + 0.9 * forget_sig
    log_rate = -8.0 * decay * span
    rate = jnp.exp(log_rate)
    scale = jnp.sqrt(-jnp.expm1(2.0 * log_rate))
    drive = scale * admit_sig * conv_out
    within = jnp.cumsum(log_rate, axis=1)
    grow = jnp.exp(within)
    inner = grow * jnp.cumsum(jnp.exp(-within) * drive, axis=1)
    ends = lax.all_gather(jnp.stack([grow[:, -1], inner[:, -1]]), "wide")
    carry = jnp.zeros((all_seqs, share), F32)
    for j in range(wide - 1):
        carry = jnp.where(j < w, ends[j, 0] * carry + ends[j, 1], carry)
    carried = inner + grow * carry[:, None, :]
    carried_before = jnp.concatenate([carry[:, None, :], carried[:, :-1]], axis=1)
    state = carried.astype(BF).astype(F32).reshape(total, share)

    branch_y = dot(normed_all, gelu_cols)
    gelu_y = jax.nn.gelu(branch_y)
    mixed_low = (state * gelu_y).astype(BF)
    temporal = reduce_seq(lambda k: dot(mixed_low[k * rows : (k + 1) * rows], out_rows))
    flat = flat_low.astype(F32)
    stream = flat + temporal
    normed_two = rms_norm(stream, gain_two).astype(BF)
    normed_two_all = jnp.concatenate(gather_seq(normed_two), axis=0)

    gate_up = dot(normed_two_all, mlp_full)
    gate, up_values = gate_up[:, :hidden_units], gate_up[:, hidden_units:]
    gelu_gate = jax.nn.gelu(gate)
    hidden_low = (gelu_gate * up_values).astype(BF)
    hidden_grad = contract_last(upstream_all, down_full)
    gate_rows = (hidden_grad * up_values * gelu_grad_of(gate)).astype(BF)
    up_rows = (hidden_grad * gelu_gate).astype(BF)
    mlp_rows = jnp.concatenate([gate_rows, up_rows], axis=1)
    normed_two_grad = reduce_seq(
        lambda k: contract_last(mlp_rows[k * rows : (k + 1) * rows], mlp_full)
    )
    mlp_grad = lax.psum_scatter(
        contract_rows(normed_two_all, mlp_rows).astype(BF), "wide", scatter_dimension=0, tiled=True
    ).astype(F32)
    down_grad = lax.psum_scatter(
        contract_rows(hidden_low, upstream_all).astype(BF), "wide", scatter_dimension=1, tiled=True
    ).astype(F32)
    feed = reduce_seq(lambda k: dot(hidden_low[k * rows : (k + 1) * rows], down_full))
    result = stream + feed
    output = result.astype(BF).reshape(seqs, tokens, width)
    position = w * tokens + jnp.arange(tokens, dtype=jnp.int32)
    valid = (position[None, :] < lengths[:, None]).astype(F32).reshape(rows, 1)
    partial_sums = jnp.stack(
        [
            jnp.sum(valid * result * result),
            jnp.sum(valid * temporal * temporal),
            jnp.sum(valid * feed * feed),
            jnp.sum(valid),
        ]
    )

    gain_two_grad = jnp.sum(normed_two_grad * stream * inverse_rms(stream), axis=0)
    stream_grad = upstream.astype(F32) + rms_back(stream, gain_two, normed_two_grad)
    stream_low_all = jnp.concatenate(gather_seq(stream_grad.astype(BF)), axis=0)

    mixed_grad = contract_last(stream_low_all, out_rows)
    state_grad = (mixed_grad * gelu_y).astype(BF).astype(F32).reshape(all_seqs, tokens, share)
    y_rows = (mixed_grad * state * gelu_grad_of(branch_y)).astype(BF)
    gathered_back = lax.cumsum(grow * state_grad, axis=1, reverse=True)
    adjoint_local = jnp.exp(-within) * gathered_back
    gelu_part = lax.psum_scatter(
        contract_rows(normed_all, y_rows).astype(BF), "wide", scatter_dimension=0, tiled=True
    )
    heads = lax.all_gather(gathered_back[:, 0], "wide")
    reach = jnp.exp(within[:, -1:] - within)
    later = jnp.zeros((all_seqs, share), F32)
    for j in range(wide - 1, 0, -1):
        later = jnp.where(j > w, ends[j, 0] * later + heads[j], later)
    adjoint = adjoint_local + reach * later[:, None, :]
    drive_part = scale * admit_sig
    conv_out_grad = adjoint * drive_part
    after = lax.ppermute(
        conv_out_grad[:, : CONV - 1], "wide", [(i + 1, i) for i in range(wide - 1)]
    )
    grad_padded = jnp.concatenate([conv_out_grad, after], axis=1)
    conv_rows = sum(taps[k] * grad_padded[:, k : k + tokens] for k in range(CONV)).astype(BF)
    log_rate_grad = adjoint * (
        rate * carried_before - rate * rate / scale * admit_sig * conv_out
    )
    forget_rows = (
        log_rate_grad * (-7.2) * decay * forget_sig * (1.0 - forget_sig)
    ).astype(BF)
    admit_rows = (adjoint * scale * conv_out * admit_sig * (1.0 - admit_sig)).astype(BF)
    channel_grads = jnp.stack(
        [
            jnp.sum(forget_rows.astype(F32), axis=(0, 1)),
            jnp.sum(admit_rows.astype(F32), axis=(0, 1)),
            jnp.sum(log_rate_grad * (-8.0) * span, axis=(0, 1)),
            jnp.sum(conv_out_grad, axis=(0, 1)),
        ]
        + [jnp.sum(conv_out_grad * shifted(k), axis=(0, 1)) for k in range(CONV)]
    )

    def in_window(values):
        return lax.dynamic_update_slice_in_dim(
            jnp.zeros((total, window), BF), values.reshape(total, share), off, 1
        )

    forget_win = in_window(forget_rows).reshape(total, blocks, BW)
    admit_win = in_window(admit_rows).reshape(total, blocks, BW)
    branch_back = jnp.einsum(
        "tkj,kij->tki", forget_win, forget_blocks, preferred_element_type=F32
    ) + jnp.einsum("tkj,kij->tki", admit_win, admit_blocks, preferred_element_type=F32)
    branch_rows = (
        branch_back.reshape(total, window) + in_window(conv_rows).astype(F32)
    ).astype(BF)
    normed_grad = reduce_seq(
        lambda k: contract_last(branch_rows[k * rows : (k + 1) * rows], branch_cols)
        + contract_last(y_rows[k * rows : (k + 1) * rows], gelu_cols)
    )
    branch_part = lax.psum_scatter(
        contract_rows(normed_all, branch_rows).astype(BF), "wide", scatter_dimension=0, tiled=True
    )
    gate_grads = jnp.concatenate(
        [
            jnp.einsum("tki,tkj->kij", x_blocks, rows_win, preferred_element_type=F32).reshape(
                window, BW
            )
            for rows_win in (forget_win, admit_win)
        ],
        axis=1,
    )
    out_grad = contract_rows(mixed_low, stream_low_all).astype(BF)

    gate_cols_grad = jnp.zeros((channels, gate_cols), F32)
    out_cols_grad = jnp.zeros((channels, quarter), BF)
    for k in range(groups):
        other = s ^ k
        part = lax.dynamic_slice_in_dim(gate_grads, other * gate_cols, gate_cols, 1)
        part = swap(part.astype(BF), k).astype(F32) if k else part
        start = base_of(other)
        part = part + lax.dynamic_slice_in_dim(gate_cols_grad, start, window, 0)
        gate_cols_grad = lax.dynamic_update_slice_in_dim(gate_cols_grad, part, start, 0)
        part = lax.dynamic_slice_in_dim(out_grad, other * quarter, quarter, 1)
        part = swap(part, k) if k else part
        out_cols_grad = lax.dynamic_update_slice_in_dim(out_cols_grad, part, other * share, 0)
    late_part = lax.psum_scatter(
        jnp.concatenate([out_cols_grad, gate_cols_grad.astype(BF)], axis=1),
        "wide",
        scatter_dimension=0,
        tiled=True,
    )
    out_whole = jnp.zeros((channels // wide, width), F32)
    gates_whole = jnp.zeros((channels // wide, 2 * BW), F32)
    gelu_whole = jnp.zeros((width // wide, channels), F32)
    branch_whole = jnp.zeros((width // wide, channels), F32)
    for k in range(groups):
        other = s ^ k
        part = swap(late_part, k) if k else late_part
        out_whole = lax.dynamic_update_slice_in_dim(
            out_whole, part[:, :quarter].astype(F32), other * quarter, 1
        )
        gates_whole = lax.dynamic_update_slice_in_dim(
            gates_whole, part[:, quarter:].astype(F32), other * gate_cols, 1
        )
        part = swap(gelu_part, k) if k else gelu_part
        gelu_whole = lax.dynamic_update_slice_in_dim(
            gelu_whole, part.astype(F32), other * share, 1
        )
        part = (swap(branch_part, k) if k else branch_part).astype(F32)
        start = base_of(other)
        part = part + lax.dynamic_slice_in_dim(branch_whole, start, window, 1)
        branch_whole = lax.dynamic_update_slice_in_dim(branch_whole, part, start, 1)

    gain_one_grad = jnp.sum(normed_grad * flat * inverse_rms(flat), axis=0)
    inputs_grad = (stream_grad + rms_back(flat, gain_one, normed_grad)).reshape(
        seqs, tokens, width
    )
    channel_all = lax.dynamic_update_slice_in_dim(
        jnp.zeros((8, channels), F32), channel_grads, s * share, 1
    )
    sums = lax.psum(
        jnp.concatenate(
            [channel_all.reshape(-1), gain_one_grad, gain_two_grad, partial_sums]
        ),
        ("seq", "wide"),
    )
    channel_sums = lax.dynamic_slice_in_dim(
        sums[: 8 * channels].reshape(8, channels), w * rw, rw, 1
    )
    gain_sums = lax.dynamic_slice_in_dim(
        sums[8 * channels : 8 * channels + 2 * width].reshape(2, width), w * dw, dw, 1
    )
    totals = sums[8 * channels + 2 * width :]
    statistics = jnp.sqrt(totals[0:3] / (totals[3] * width))
    return (
        output,
        inputs_grad,
        gain_sums[0],
        gelu_whole,
        branch_whole,
        gates_whole[:, :BW],
        gates_whole[:, BW:],
        channel_sums[0],
        channel_sums[1],
        channel_sums[2],
        channel_sums[4:8],
        channel_sums[3],
        out_whole,
        gain_sums[1],
        mlp_grad[:, :hidden_units],
        mlp_grad[:, hidden_units:],
        down_grad,
        statistics,
    )


def solution(mesh):
    in_specs = (
        P("seq", "wide", None),
        P("seq"),
        P("wide"),
        P("wide", None),
        P("wide", None),
        P("wide", None),
        P("wide", None),
        P("wide"),
        P("wide"),
        P("wide"),
        P(None, "wide"),
        P("wide"),
        P("wide", None),
        P("wide"),
        P("wide", "seq"),
        P("wide", "seq"),
        P("seq", "wide"),
        P("seq", "wide", None),
    )
    out_specs = (
        P("seq", "wide", None),
        P("seq", "wide", None),
        P("wide"),
        P("wide", None),
        P("wide", None),
        P("wide", None),
        P("wide", None),
        P("wide"),
        P("wide"),
        P("wide"),
        P(None, "wide"),
        P("wide"),
        P("wide", None),
        P("wide"),
        P("wide", "seq"),
        P("wide", "seq"),
        P("seq", "wide"),
        P(),
    )
    return jax.shard_map(body, mesh=mesh, in_specs=in_specs, out_specs=out_specs, check_vma=False)
```

time: 2550 us -> 1130 us (0.44)
  waiting for transfers between devices: 1660 us -> 502 us
  blocking collectives: 330 us -> 67.5 us
  starting transfers between devices: 25.4 us -> 63.5 us
  other arithmetic: 138 us -> 109 us
    reduce_scatter x10 -> x5, waiting for transfers between devices: 1000 us -> 247 us  [the longest x1 128 us: body(): lax.psum_scatter(contract_rows(normed_two_all, mlp_rows).astype(BF), 'wid...]
    all_gather x10 -> x5, waiting for transfers between devices: 308 us -> 0.03 us  [the longest x1 0.02 us: body(): lax.all_gather(lax.dynamic_slice_in_dim(out_weight, s * quarter, quarter,...]
    ppermute x0 -> x55, waiting for transfers between devices: none -> 247 us  [the longest x53 247 us: swap(): lax.ppermute(values, 'seq', [(i, i ^ mask) for i in range(lax.axis_size('...]
    psum x1, waiting for transfers between devices: 179 us -> 7.61 us  [body(): lax.psum(jnp.concatenate([channel_all.reshape(-1), gain_one_grad, gain_tw...]
    all_to_all x5 -> x0, waiting for transfers between devices: 140 us -> none  [the longest x1 55.8 us: body(): lax.all_to_all(conv_grad_ch.astype(jnp.bfloat16), 'wide', split_axis=1, c...]
    all_to_all x3 -> x0, blocking collectives: 137 us -> none  [the longest x1 59.9 us: body(): lax.all_to_all(admit_grad_ch.astype(jnp.bfloat16), 'wide', split_axis=1,...]
    dynamic_update_slice x2 -> x21, local copies, waits for them, and re-layouts: 0.54 us -> 65.3 us  [the longest x4 26.3 us: body(): branch_whole = lax.dynamic_update_slice_in_dim(branch_whole, part, start, 1)]
    ppermute x0 -> x55, starting transfers between devices: none -> 62.4 us  [the longest x53 58.7 us: swap(): lax.ppermute(values, 'seq', [(i, i ^ mask) for i in range(lax.axis_size('...]
  transfers between devices with their start and end apart: 27 -> 66, of which waited for: 22 -> 37; matrix products, arithmetic and copies ran while one was open for 13% -> 32% of each run, Pallas kernels for 0% -> 0%
where the time goes in v1:
time: 1130 us; the launch traced here: 1120 us
  waiting for transfers between devices  502 us (44%)
  matrix products  197 us (17%)
  local copies, waits for them, and re-layouts  165 us (15%)
  other arithmetic  109 us (10%)
  blocking collectives  67.5 us (6%)
  starting transfers between devices  63.5 us (6%)
  between operations  17.2 us (2%)
    ppermute x53, waiting for transfers between devices, swap(): lax.ppermute(values, 'seq', [(i, i ^ mask) for i in range(lax.axis_size('...  247 us
    reduce_scatter x1, waiting for transfers between devices, body(): lax.psum_scatter(contract_rows(normed_two_all, mlp_rows).astype(BF), 'wid...  128 us
    dot_general x14, matrix products, contract_last(): lax.dot_general(left, right, (((1,), (1,)), ((), ())), preferred_element_...  74.8 us
    dot_general x11, matrix products, dot(): return jnp.dot(left, right, preferred_element_type=F32)  64.4 us
    ppermute x53, starting transfers between devices, swap(): lax.ppermute(values, 'seq', [(i, i ^ mask) for i in range(lax.axis_size('...  58.7 us
    reduce_scatter x1, waiting for transfers between devices, body(): lax.psum_scatter(contract_rows(hidden_low, upstream_all).astype(BF), 'wid...  48 us
    dot_general x5, matrix products, contract_rows(): lax.dot_general(left, right, (((0,), (0,)), ((), ())), preferred_element_...  47.3 us
    unnamed x238, local copies, waits for them, and re-layouts  40.9 us
  transfers between devices with their start and end apart: 66, of which 37 were waited for; matrix products, arithmetic and copies ran while one was open for 32% of the time, Pallas kernels for 0%

profile of v1, /device:TPU:0, one launch (start us, length us, event | category | flops | bytes accessed | tf_op | source)
XLA Modules:
  0.0 1121.8 jit_solution(11784390200646281825)
XLA Ops:
  16.0 19.9 %all_gather.35 = bf16[2560,128]{1,0:T(8,128)(2,1)S(1)} all-gather(bf16[320,128]{1,0:T(8,128)(2,1)S(1)} %fusion.134), channel_id=1, replica_groups=mesh['seq'=4,'wide'=8] {'wide'}, dimensions={0}, use_global_device_ids=true | all-gather | bytes 737280 | tf_op jit(solution)/shard_map/all_gather | solution.py:129
  43.9 14.0 %all-gather = bf16[24576]{0:T(1024)(128)(2,1)S(1)} all-gather(bf16[3072]{0:T(1024)(128)(2,1)S(1)} %concatenate.80), channel_id=2, replica_groups=mesh['seq'=4,'wide'=8] {'wide'}, dimensions={0}, use_global_device_ids=true | all-gather | bytes 55296 | tf_op jit(solution)/shard_map/all_gather | solution.py:117
  107.1 11.0 collective-permute-done.8
  118.9 10.7 collective-permute-done.9
  165.5 10.7 fusion.180
  177.7 19.6 %all-gather.1 = f32[16,8,640]{2,1,0:T(8,128)S(1)} all-gather(f32[2,8,640]{2,1,0:T(8,128)S(1)} %pad_maximum_fusion.15), channel_id=3, replica_groups=mesh['seq'=4,'wide'=8] {'wide'}, dimensions={0}, use_global_device_ids=true | all-gather | bytes 368640 | tf_op jit(solution)/shard_map/all_gather | solution.py:208
  238.9 18.5 %collective-permute-done.12 = bf16[256,2048]{1,0:T(8,128)(2,1)} collective-permute-done((bf16[256,2048]{1,0:T(8,128)(2,1)}, bf16[256,2048]{1,0:T(8,128)(2,1)}, u32[]{:S(2)}, u32[]{:S(2)}) %collective-permute-start.12) | collective-permute-done | bytes 1048608 | tf_op jit(solution)/shard_map/ppermute | solution.py:26
  268.4 11.4 %collective-permute-done.23 = bf16[256,2048]{1,0:T(8,128)(2,1)} collective-permute-done((bf16[256,2048]{1,0:T(8,128)(2,1)}, bf16[256,2048]{1,0:T(8,128)(2,1)}, u32[]{:S(2)}, u32[]{:S(2)}) %collective-permute-start.23) | collective-permute-done | bytes 1048608 | tf_op jit(solution)/shard_map/ppermute | solution.py:26
  302.5 9.6 collective-permute-done.26
  328.5 19.3 %fusion.191 = f32[1024,3072]{1,0:T(8,128)} fusion(bf16[1024,2048]{1,0:T(8,128)(2,1)} %constant_dynamic-update-slice_fusion.3, bf16[2048,3072]{1,0:T(8,128)(2,1)} %all-gather.15.cloned.1.call-done), kind=kOutput, calls=%fused_computation.442 | convolution fusion | flops 12884901888 | bytes 29360128 | tf_op jit(solution)/shard_map/dot_general | solution.py:14
  347.8 18.8 %multiply_convert_fusion = (bf16[1024,1536]{1,0:T(8,128)(2,1)S(1)}, bf16[1024,1536]{1,0:T(8,128)(2,1)S(1)}, bf16[1024,1536]{1,0:T(8,128)(2,1)}) fusion(f32[1024,3072]{1,0:T(8,128)} %fusion.191, bf16[1024,2048]{1,0:T(8,128)(2,1)} %copy-done.63, bf16[1536,2048]{1,0:T(8,128)(2,1)} %all-gather.17.cloned.1.call-done), kind=kOutput, calls=%fused_computation.34 | convolution fusion | flops 6489636864 | bytes 32505856 | tf_op jit(solution)/shard_map/dot_general | solution.py:18
  366.6 10.4 convolution_convert_fusion.7
  423.0 20.0 %collective-permute-done.28 = bf16[256,2048]{1,0:T(8,128)(2,1)S(1)} collective-permute-done((bf16[256,2048]{1,0:T(8,128)(2,1)S(1)}, bf16[256,2048]{1,0:T(8,128)(2,1)S(1)}, u32[]{:S(2)}, u32[]{:S(2)}) %collective-permute-start.28) | collective-permute-done | bytes 1048608 | tf_op jit(solution)/shard_map/ppermute | solution.py:26
  474.9 15.7 %collective-permute-done.31 = bf16[256,2048]{1,0:T(8,128)(2,1)} collective-permute-done((bf16[256,2048]{1,0:T(8,128)(2,1)}, bf16[256,2048]{1,0:T(8,128)(2,1)}, u32[]{:S(2)}, u32[]{:S(2)}) %collective-permute-start.31) | collective-permute-done | bytes 1048608 | tf_op jit(solution)/shard_map/ppermute | solution.py:26
  523.3 14.1 %all-gather.2 = f32[64,1,640]{2,0,1:T(8,128)S(1)} all-gather(f32[8,1,640]{2,0,1:T(8,128)S(1)} %slice.658), channel_id=4, replica_groups=mesh['seq'=4,'wide'=8] {'wide'}, dimensions={0}, use_global_device_ids=true | all-gather | bytes 184320 | tf_op jit(solution)/shard_map/all_gather | solution.py:268
  608.6 10.2 collective-permute-done.36
  630.5 15.2 %collective-permute-done.37 = bf16[256,2048]{1,0:T(8,128)(2,1)} collective-permute-done((bf16[256,2048]{1,0:T(8,128)(2,1)}, bf16[256,2048]{1,0:T(8,128)(2,1)}, u32[]{:S(2)}, u32[]{:S(2)}) %collective-permute-start.37) | collective-permute-done | bytes 1048608 | tf_op jit(solution)/shard_map/ppermute | solution.py:26
  693.4 28.5 %collective-permute-done.50 = bf16[768,128]{1,0:T(8,128)(2,1)} collective-permute-done((bf16[768,128]{1,0:T(8,128)(2,1)S(1)}, bf16[768,128]{1,0:T(8,128)(2,1)}, u32[]{:S(2)}, u32[]{:S(2)}) %collective-permute-start.50) | collective-permute-done | bytes 196640 | tf_op jit(solution)/shard_map/ppermute | solution.py:26
  739.3 10.8 convolution_convert_fusion.1
  752.0 18.7 %convolution_convert_fusion = bf16[2048,3072]{1,0:T(8,128)(2,1)} fusion(bf16[1024,2048]{1,0:T(8,128)(2,1)} %constant_dynamic-update-slice_fusion.3, bf16[1024,1536]{1,0:T(8,128)(2,1)S(1)} %copy-done.101, bf16[1024,1536]{1,0:T(8,128)(2,1)} %copy-done.102), kind=kOutput, calls=%fused_computation | convolution fusion | flops 12903776256 | bytes 23068672 | tf_op jit(solution)/shard_map/dot_general | solution.py:22
  790.8 35.2 %reduce-scatter.6.cloned.1.call-done = bf16[256,640]{1,0:T(8,128)(2,1)} async-done(((bf16[2048,640]{1,0:T(8,128)(2,1)}), bf16[256,640]{1,0:T(8,128)(2,1)}) %reduce-scatter.6.cloned.1.call-update) | async-done | bytes 327696 | tf_op jit(solution)/shard_map/reduce_scatter | solution.py:265
  836.7 31.0 %reduce-scatter.8.cloned.1.call-done = bf16[256,768]{1,0:T(8,128)(2,1)} async-done(((bf16[2048,768]{1,0:T(8,128)(2,1)}), bf16[256,768]{1,0:T(8,128)(2,1)}) %reduce-scatter.8.cloned.1.call-update) | async-done | bytes 393232 | tf_op jit(solution)/shard_map/reduce_scatter | solution.py:315
  933.4 48.0 %reduce-scatter.14.cloned.1.call-done = bf16[1536,256]{1,0:T(8,128)(2,1)} async-done(((bf16[1536,2048]{1,0:T(8,128)(2,1)}), bf16[1536,256]{1,0:T(8,128)(2,1)}) %reduce-scatter.14.cloned.1.call-update) | async-done | bytes 786448 | tf_op jit(solution)/shard_map/reduce_scatter | solution.py:239
  983.9 127.5 %reduce-scatter.12.cloned.1.call-done = bf16[256,3072]{1,0:T(8,128)(2,1)} async-done(((bf16[2048,3072]{1,0:T(8,128)(2,1)}), bf16[256,3072]{1,0:T(8,128)(2,1)}) %reduce-scatter.12.cloned.1.call-update) | async-done | bytes 1572880 | tf_op jit(solution)/shard_map/reduce_scatter | solution.py:236
  (592 shorter events, 555.7 us)
Async XLA Ops:
  7.2 89.4 %all-gather.13.cloned.1.call-start = ((), (), s32[]{:S(2)}) async-start(), calls=%async_computation.7 | async-start | bytes 2949120 | tf_op jit(solution)/shard_map/all_gather | solution.py:140
  9.2 122.2 %all-gather.9.cloned.1.call-start = ((), (), s32[]{:S(2)}) async-start(), calls=%async_computation.5 | async-start | bytes 3538944 | tf_op jit(solution)/shard_map/all_gather | solution.py:126
  10.2 192.8 %all-gather.11.cloned.1.call-start = ((), (), s32[]{:S(2)}) async-start(), calls=%async_computation.6 | async-start | bytes 2949120 | tf_op jit(solution)/shard_map/all_gather | solution.py:137
  12.0 316.4 %all-gather.15.cloned.1.call-start = ((), (), s32[]{:S(2)}) async-start(), calls=%async_computation.8 | async-start | bytes 14155776 | tf_op jit(solution)/shard_map/all_gather | solution.py:143
  13.5 334.3 %all-gather.17.cloned.1.call-start = ((), (), s32[]{:S(2)}) async-start(), calls=%async_computation.9 | async-start | bytes 7077888 | tf_op jit(solution)/shard_map/all_gather | solution.py:146
  37.0 39.8 %collective-permute-start.4 = (bf16[272,2048]{1,0:T(8,128)(2,1)}, bf16[272,2048]{1,0:T(8,128)(2,1)}, u32[]{:S(2)}, u32[]{:S(2)}) collective-permute-start(bf16[272,2048]{1,0:T(8,128)(2,1)} %pad_maximum_fusion.5), channel_id=1, source_target_pairs={{0,8},{8,0},{16,24},{24,16},{1,9},{9,1},{17,25},{25,17},{2,10},{10... | collective-permute-start | bytes 3342344 | tf_op jit(solution)/shard_map/ppermute | solution.py:26
  38.1 36.1 %collective-permute-start.5 = (bf16[272,2048]{1,0:T(8,128)(2,1)}, bf16[272,2048]{1,0:T(8,128)(2,1)}, u32[]{:S(2)}, u32[]{:S(2)}) collective-permute-start(bf16[272,2048]{1,0:T(8,128)(2,1)} %pad_maximum_fusion.5), channel_id=1, source_target_pairs={{0,16},{8,24},{16,0},{24,8},{1,17},{9,25},{17,1},{25,9},{2,18},{10... | collective-permute-start | bytes 3342344 | tf_op jit(solution)/shard_map/ppermute | solution.py:26
  43.6 741.1 %all-reduce.2.cloned.1.call-start = ((), (), s32[]{:S(2)}) async-start(), calls=%async_computation.10 | async-start | bytes 204800 | tf_op jit(solution)/shard_map/psum | solution.py:376
  235.9 43.9 %collective-permute-start.23 = (bf16[256,2048]{1,0:T(8,128)(2,1)}, bf16[256,2048]{1,0:T(8,128)(2,1)}, u32[]{:S(2)}, u32[]{:S(2)}) collective-permute-start(bf16[256,2048]{1,0:T(8,128)(2,1)} %bitcast.32), channel_id=1, source_target_pairs={{0,8},{8,0},{16,24},{24,16},{1,9},{9,1},{17,25},{25,17},{2,10},{10... | collective-permute-start | bytes 3145736 | tf_op jit(solution)/shard_map/ppermute | solution.py:26
  237.5 45.6 %collective-permute-start.24 = (bf16[256,2048]{1,0:T(8,128)(2,1)}, bf16[256,2048]{1,0:T(8,128)(2,1)}, u32[]{:S(2)}, u32[]{:S(2)}) collective-permute-start(bf16[256,2048]{1,0:T(8,128)(2,1)} %bitcast.32), channel_id=1, source_target_pairs={{0,16},{8,24},{16,0},{24,8},{1,17},{9,25},{17,1},{25,9},{2,18},{10... | collective-permute-start | bytes 3145736 | tf_op jit(solution)/shard_map/ppermute | solution.py:26
  281.2 37.1 %collective-permute-start.16 = (bf16[256,2048]{1,0:T(8,128)(2,1)S(1)}, bf16[256,2048]{1,0:T(8,128)(2,1)S(1)}, u32[]{:S(2)}, u32[]{:S(2)}) collective-permute-start(bf16[256,2048]{1,0:T(8,128)(2,1)S(1)} %get-tuple-element.56), channel_id=1, source_target_pairs={{0,16},{8,24},{16,0},{24,8},{1,17},{9,25},{17,1},{25,9},{2,18},{10... | collective-permute-start | bytes 3145736 | tf_op jit(solution)/shard_map/ppermute | solution.py:26
  417.8 43.2 %collective-permute-start.20 = (bf16[256,2048]{1,0:T(8,128)(2,1)}, bf16[256,2048]{1,0:T(8,128)(2,1)}, u32[]{:S(2)}, u32[]{:S(2)}) collective-permute-start(bf16[256,2048]{1,0:T(8,128)(2,1)} %pad_maximum_fusion.9), channel_id=1, source_target_pairs={{0,8},{8,0},{16,24},{24,16},{1,9},{9,1},{17,25},{25,17},{2,10},{10... | collective-permute-start | bytes 3145736 | tf_op jit(solution)/shard_map/ppermute | solution.py:26
  421.8 39.2 %collective-permute-start.22 = (bf16[256,2048]{1,0:T(8,128)(2,1)}, bf16[256,2048]{1,0:T(8,128)(2,1)}, u32[]{:S(2)}, u32[]{:S(2)}) collective-permute-start(bf16[256,2048]{1,0:T(8,128)(2,1)} %pad_maximum_fusion.10), channel_id=1, source_target_pairs={{0,16},{8,24},{16,0},{24,8},{1,17},{9,25},{17,1},{25,9},{2,18},{10... | collective-permute-start | bytes 3145736 | tf_op jit(solution)/shard_map/ppermute | solution.py:26
  544.9 39.7 %collective-permute-start.35 = (f32[8,3,640]{2,0,1:T(8,128)}, f32[8,3,640]{2,0,1:T(8,128)}, u32[]{:S(2)}, u32[]{:S(2)}) collective-permute-start(f32[8,3,640]{2,0,1:T(8,128)} %slice.667), channel_id=1, source_target_pairs={{1,0},{2,1},{3,2},{4,3},{5,4},{6,5},{7,6},{9,8},{10,9},{11,10},{12... | collective-permute-start | bytes 184328 | tf_op jit(solution)/shard_map/ppermute | solution.py:276
  655.7 170.3 %reduce-scatter.6.cloned.1.call-start = ((), (), s32[]{:S(2)}) async-start(), calls=%async_computation.11 | async-start | bytes 2949120 | tf_op jit(solution)/shard_map/reduce_scatter | solution.py:265
  663.2 204.5 %reduce-scatter.8.cloned.1.call-start = ((), (), s32[]{:S(2)}) async-start(), calls=%async_computation.12 | async-start | bytes 3538944 | tf_op jit(solution)/shard_map/reduce_scatter | solution.py:315
  672.0 238.5 %reduce-scatter.10.cloned.1.call-start = ((), (), s32[]{:S(2)}) async-start(), calls=%async_computation.13 | async-start | bytes 3686400 | tf_op jit(solution)/shard_map/reduce_scatter | solution.py:341
  682.6 45.2 %collective-permute-start.46 = (bf16[640,512]{1,0:T(8,128)(2,1)}, bf16[640,512]{1,0:T(8,128)(2,1)}, u32[]{:S(2)}, u32[]{:S(2)}) collective-permute-start(bf16[640,512]{1,0:T(8,128)(2,1)} %get-tuple-element.71), channel_id=1, source_target_pairs={{0,8},{8,0},{16,24},{24,16},{1,9},{9,1},{17,25},{25,17},{2,10},{10... | collective-permute-start | bytes 1966088 | tf_op jit(solution)/shard_map/ppermute | solution.py:26
  683.5 46.3 %collective-permute-start.47 = (bf16[640,512]{1,0:T(8,128)(2,1)S(1)}, bf16[640,512]{1,0:T(8,128)(2,1)}, u32[]{:S(2)}, u32[]{:S(2)}) collective-permute-start(bf16[640,512]{1,0:T(8,128)(2,1)S(1)} %get-tuple-element.70), channel_id=1, source_target_pairs={{0,16},{8,24},{16,0},{24,8},{1,17},{9,25},{17,1},{25,9},{2,18},{10... | collective-permute-start | bytes 1966088 | tf_op jit(solution)/shard_map/ppermute | solution.py:26
  685.2 46.5 %collective-permute-start.48 = (bf16[640,512]{1,0:T(8,128)(2,1)S(1)}, bf16[640,512]{1,0:T(8,128)(2,1)}, u32[]{:S(2)}, u32[]{:S(2)}) collective-permute-start(bf16[640,512]{1,0:T(8,128)(2,1)S(1)} %get-tuple-element.69), channel_id=1, source_target_pairs={{0,24},{8,16},{16,8},{24,0},{1,25},{9,17},{17,9},{25,1},{2,26},{10... | collective-permute-start | bytes 1966088 | tf_op jit(solution)/shard_map/ppermute | solution.py:26
  737.4 243.9 %reduce-scatter.14.cloned.1.call-start = ((), (), s32[]{:S(2)}) async-start(), calls=%async_computation.15 | async-start | bytes 7077888 | tf_op jit(solution)/shard_map/reduce_scatter | solution.py:239
  750.2 361.2 %reduce-scatter.12.cloned.1.call-start = ((), (), s32[]{:S(2)}) async-start(), calls=%async_computation.14 | async-start | bytes 14155776 | tf_op jit(solution)/shard_map/reduce_scatter | solution.py:236
  828.1 41.1 %collective-permute-start.41 = (bf16[256,640]{1,0:T(8,128)(2,1)}, bf16[256,640]{1,0:T(8,128)(2,1)}, u32[]{:S(2)}, u32[]{:S(2)}) collective-permute-start(bf16[256,640]{1,0:T(8,128)(2,1)} %reduce-scatter.6.cloned.1.call-done), channel_id=1, source_target_pairs={{0,16},{8,24},{16,0},{24,8},{1,17},{9,25},{17,1},{25,9},{2,18},{10... | collective-permute-start | bytes 983048 | tf_op jit(solution)/shard_map/ppermute | solution.py:26
  829.5 42.3 %collective-permute-start.42 = (bf16[256,640]{1,0:T(8,128)(2,1)}, bf16[256,640]{1,0:T(8,128)(2,1)S(1)}, u32[]{:S(2)}, u32[]{:S(2)}) collective-permute-start(bf16[256,640]{1,0:T(8,128)(2,1)} %reduce-scatter.6.cloned.1.call-done), channel_id=1, source_target_pairs={{0,24},{8,16},{16,8},{24,0},{1,25},{9,17},{17,9},{25,1},{2,26},{10... | collective-permute-start | bytes 983048 | tf_op jit(solution)/shard_map/ppermute | solution.py:26
  (150 other events, 2646.2 us)
Sparse Core Ops, SparseCore 0:
  10.3 40.5 all-gather.12
  53.1 38.0 all-gather.8
  93.5 32.7 all-gather.10
  128.3 118.2 all-gather.14
  248.1 63.3 all-gather.16
  655.8 128.7 all-reduce.1
  787.5 38.4 reduce-scatter.5
  828.3 39.3 reduce-scatter.7
  870.0 40.4 reduce-scatter.9
  912.8 68.5 reduce-scatter.13
  983.8 127.5 reduce-scatter.11

commit v2 on v1

v2 whole, which is shorter than its diff:
```python
import jax
import jax.numpy as jnp
from jax import lax
from jax.experimental import pallas as pl
from jax.experimental.pallas import tpu as pltpu
from jax.sharding import PartitionSpec as P

BW = 256
CONV = 4
HALO = 8
BF = jnp.bfloat16
F32 = jnp.float32
LANES = 128
ROWS16 = 16
MESH = pl.DeviceIdType.MESH


def dot(left, right):
    return jnp.dot(left, right, preferred_element_type=F32)


def contract_last(left, right):
    return lax.dot_general(left, right, (((1,), (1,)), ((), ())), preferred_element_type=F32)


def contract_rows(left, right):
    return lax.dot_general(left, right, (((0,), (0,)), ((), ())), preferred_element_type=F32)


def swap(values, mask):
    return lax.ppermute(values, "seq", [(i, i ^ mask) for i in range(lax.axis_size("seq"))])


def gather_seq(values):
    half = values.shape[0] // 2
    near = swap(values, 1)
    side = swap(values, 2)
    first = swap(near[:half], 2)
    second = swap(side[half:], 1)
    return [values, near, side, jnp.concatenate([first, second], axis=0)]


def inverse_rms(values):
    return lax.rsqrt(jnp.mean(values * values, axis=-1, keepdims=True) + 1e-06)


def rms_norm(values, gain):
    return values * inverse_rms(values) * gain


def sigmoid(values):
    return 0.5 * jnp.tanh(0.5 * values) + 0.5


def gelu_parts(values):
    c = 0.7978845608028654
    sq = values * values
    t = jnp.tanh(c * values * (1.0 + 0.044715 * sq))
    half = 0.5 * (1.0 + t)
    return values * half, half + 0.5 * values * (1.0 - t * t) * (c * (1.0 + 3.0 * 0.044715 * sq))


def drop_of(rate_log):
    u = 2.0 * rate_log
    series = 1.0 + u * (1.0 / 8.0)
    for n in (7, 6, 5, 4, 3, 2):
        series = 1.0 + u * series * (1.0 / n)
    return jnp.where(u > -0.4, -u * series, 1.0 - jnp.exp(u))


def scan_rows(rate, drive, reverse):
    rows, lanes = rate.shape
    count = rows // 8
    rate = rate.reshape(count, 8, lanes)
    drive = drive.reshape(count, 8, lanes)
    row = lax.broadcasted_iota(jnp.int32, (count, 8, lanes), 1)
    for step in (1, 2, 4):
        shift = 8 - step if reverse else step
        keep = row < 8 - step if reverse else row >= step
        drive = drive + rate * jnp.where(keep, pltpu.roll(drive, shift, 1), 0.0)
        rate = rate * jnp.where(keep, pltpu.roll(rate, shift, 1), 1.0)
    state, reach = jnp.zeros((1, lanes), F32), jnp.ones((1, lanes), F32)
    states, reaches = [None] * count, [None] * count
    last = 0 if reverse else 7
    for i in reversed(range(count)) if reverse else range(count):
        states[i] = drive[i] + rate[i] * state
        reaches[i] = rate[i] * reach
        state = states[i][last : last + 1]
        reach = reaches[i][last : last + 1]
    return jnp.concatenate(states, axis=0), jnp.concatenate(reaches, axis=0)


def forward_kernel(
    off_ref, x_ref, edge_ref, gates_ref, chan_ref,
    forget_out, admit_out, conv_out_ref, rate_out, local_out, reach_out, ends_out,
    logits,
):
    q = pl.program_id(0)
    tokens = x_ref.shape[0]
    share = chan_ref.shape[1]
    blocks = x_ref.shape[1] // BW
    off = pl.multiple_of(off_ref[0], LANES)
    for b in range(blocks):
        cols = slice(b * BW, (b + 1) * BW)
        mixed = jnp.dot(x_ref[:, cols], gates_ref[cols, :], preferred_element_type=F32)
        logits[0, :, cols] = mixed[:, :BW]
        logits[1, :, cols] = mixed[:, BW:]
    for j in range(share // LANES):
        lanes = slice(j * LANES, (j + 1) * LANES)
        here = pl.ds(pl.multiple_of(off + j * LANES, LANES), LANES)
        chan = [chan_ref[i : i + 1, lanes] for i in range(8)]
        forget = (logits[0, :, here] + chan[0]).astype(BF)
        admit = (logits[1, :, here] + chan[1]).astype(BF)
        forget_out[:, lanes] = forget
        admit_out[:, lanes] = admit
        edge = edge_ref[pl.ds(pl.multiple_of(q * HALO, HALO), HALO), here]
        padded = jnp.concatenate([edge, x_ref[:, here].astype(F32)], axis=0)
        conv = chan[3] + chan[4] * padded[HALO:]
        for k in range(1, CONV):
            conv = conv + chan[4 + k] * pltpu.roll(padded, k, 0)[HALO:]
        conv_out_ref[:, lanes] = conv
        rate_log = -8.0 * chan[2] * (0.1 + 0.9 * sigmoid(forget.astype(F32)))
        rate = jnp.exp(rate_log)
        drive = jnp.sqrt(drop_of(rate_log)) * sigmoid(admit.astype(F32)) * conv
        state, reach = scan_rows(rate, drive, False)
        rate_out[:, lanes] = rate
        local_out[:, lanes] = state
        reach_out[:, lanes] = reach
        ends_out[0, 0, :, lanes] = reach[tokens - 1 :]
        ends_out[0, 1, :, lanes] = state[tokens - 1 :]


def whole(shape):
    return pl.BlockSpec(shape, lambda q: (0,) * len(shape))


def per_seq(width):
    return pl.BlockSpec((1, 1, width), lambda q: (q, 0, 0))


def temporal_forward(off, x_win, edge, gates, chan, tokens):
    total, window = x_win.shape
    share = chan.shape[1]
    seqs = total // tokens
    part = lambda width: pl.BlockSpec((tokens, width), lambda q: (q, 0))
    return pl.pallas_call(
        forward_kernel,
        grid=(seqs,),
        in_specs=[
            pl.BlockSpec(memory_space=pltpu.SMEM),
            part(window),
            whole(edge.shape),
            whole(gates.shape),
            whole(chan.shape),
        ],
        out_specs=[
            part(share), part(share), part(share), part(share), part(share), part(share),
            pl.BlockSpec((1, 2, 1, share), lambda q: (q, 0, 0, 0)),
        ],
        out_shape=[
            jax.ShapeDtypeStruct((total, share), BF),
            jax.ShapeDtypeStruct((total, share), BF),
            jax.ShapeDtypeStruct((total, share), F32),
            jax.ShapeDtypeStruct((total, share), F32),
            jax.ShapeDtypeStruct((total, share), F32),
            jax.ShapeDtypeStruct((total, share), F32),
            jax.ShapeDtypeStruct((seqs, 2, 1, share), F32),
        ],
        scratch_shapes=[
            pltpu.VMEM((2, tokens, window), F32),
        ],
        compiler_params=pltpu.CompilerParams(vmem_limit_bytes=48 * 1024 * 1024),
        cost_estimate=pl.CostEstimate(flops=1000, bytes_accessed=1000, transcendentals=0),
        name="temporal_forward",
    )(off, x_win, edge, gates, chan)


def backward_scan_kernel(
    grad_ref, y_ref, local_ref, reach_ref, carry_ref, rate_ref,
    y_rows_out, adjoint_out, later_out, heads_out,
):
    tokens, share = grad_ref.shape
    row = lax.broadcasted_iota(jnp.int32, (tokens, LANES), 0)
    for j in range(share // LANES):
        lanes = slice(j * LANES, (j + 1) * LANES)
        grad = grad_ref[:, lanes]
        value, slope = gelu_parts(y_ref[:, lanes])
        state = (local_ref[:, lanes] + reach_ref[:, lanes] * carry_ref[0, :, lanes]).astype(BF)
        y_rows_out[:, lanes] = (grad * state.astype(F32) * slope).astype(BF)
        state_grad = (grad * value).astype(BF).astype(F32)
        rate = rate_ref[:, lanes]
        ahead = jnp.where(row == tokens - 1, 1.0, pltpu.roll(rate, tokens - 1, 0))
        adjoint, later = scan_rows(ahead, state_grad, True)
        adjoint_out[:, lanes] = adjoint
        later_out[:, lanes] = later
        heads_out[0, :, lanes] = rate[:1] * adjoint[:1]


def backward_scan(grad, y, local, reach, carry, rate, tokens):
    total, share = grad.shape
    seqs = total // tokens
    part = pl.BlockSpec((tokens, share), lambda q: (q, 0))
    return pl.pallas_call(
        backward_scan_kernel,
        grid=(seqs,),
        in_specs=[part, part, part, part, per_seq(share), part],
        out_specs=[part, part, part, per_seq(share)],
        out_shape=[
            jax.ShapeDtypeStruct((total, share), BF),
            jax.ShapeDtypeStruct((total, share), F32),
            jax.ShapeDtypeStruct((total, share), F32),
            jax.ShapeDtypeStruct((seqs, 1, share), F32),
        ],
        compiler_params=pltpu.CompilerParams(vmem_limit_bytes=48 * 1024 * 1024),
        cost_estimate=pl.CostEstimate(flops=1000, bytes_accessed=1000, transcendentals=0),
        name="backward_scan",
    )(grad, y, local, reach, carry[:, None, :], rate)


def backward_rows_kernel(
    off_ref, adjoint_ref, later_ref, local_ref, reach_ref, rate_ref, conv_ref,
    forget_ref, admit_ref, x_ref, edge_ref, gates_ref, chan_ref, carry_ref, tail_ref, after_ref,
    branch_out, forget_out, admit_out, sums_out,
    conv_rows,
):
    q = pl.program_id(0)
    tokens = adjoint_ref.shape[0]
    share = chan_ref.shape[1]
    window = x_ref.shape[1]
    off = pl.multiple_of(off_ref[0], LANES)
    forget_out[...] = jnp.zeros_like(forget_out)
    admit_out[...] = jnp.zeros_like(admit_out)
    conv_rows[...] = jnp.zeros_like(conv_rows)

    @pl.when(q == 0)
    def _():
        sums_out[...] = jnp.zeros_like(sums_out)

    row = lax.broadcasted_iota(jnp.int32, (tokens, LANES), 0)
    for j in range(share // LANES):
        lanes = slice(j * LANES, (j + 1) * LANES)
        here = pl.ds(pl.multiple_of(off + j * LANES, LANES), LANES)
        chan = [chan_ref[i : i + 1, lanes] for i in range(8)]
        reach = reach_ref[:, lanes]
        carry = carry_ref[0, :, lanes]
        carried = local_ref[:, lanes] + reach * carry
        before = jnp.where(row == 0, carry, pltpu.roll(carried, 1, 0))
        adjoint = adjoint_ref[:, lanes] + later_ref[:, lanes] * tail_ref[0, :, lanes]
        forget_sig = sigmoid(forget_ref[:, lanes].astype(F32))
        admit_sig = sigmoid(admit_ref[:, lanes].astype(F32))
        span = 0.1 + 0.9 * forget_sig
        rate_log = -8.0 * chan[2] * span
        rate = rate_ref[:, lanes]
        scale = jnp.sqrt(drop_of(rate_log))
        conv = conv_ref[:, lanes]
        gated = admit_sig * conv
        log_grad = adjoint * (rate * before - rate * rate / scale * gated)
        conv_grad = adjoint * scale * admit_sig
        forget_rows = (
            log_grad * (-7.2) * chan[2] * forget_sig * (1.0 - forget_sig)
        ).astype(BF)
        admit_rows = (adjoint * scale * gated * (1.0 - admit_sig)).astype(BF)
        forget_out[:, here] = forget_rows
        admit_out[:, here] = admit_rows
        after = after_ref[pl.ds(pl.multiple_of(q * HALO, HALO), HALO), lanes]
        ahead = jnp.concatenate([conv_grad, after], axis=0)
        back = chan[4] * conv_grad
        for k in range(1, CONV):
            back = back + chan[4 + k] * pltpu.roll(ahead, tokens + HALO - k, 0)[:tokens]
        conv_rows[:, here] = back.astype(BF).astype(F32)
        edge = edge_ref[pl.ds(pl.multiple_of(q * HALO, HALO), HALO), here]
        padded = jnp.concatenate([edge, x_ref[:, here].astype(F32)], axis=0)
        sums = [
            forget_rows.astype(F32),
            admit_rows.astype(F32),
            log_grad * (-8.0) * span,
            conv_grad,
            conv_grad * padded[HALO:],
        ] + [conv_grad * pltpu.roll(padded, k, 0)[HALO:] for k in range(1, CONV)]
        sums_out[:, lanes] += jnp.concatenate(
            [jnp.sum(v, axis=0, keepdims=True) for v in sums], axis=0
        )
    for b in range(window // BW):
        cols = slice(b * BW, (b + 1) * BW)
        back = conv_rows[:, cols]
        for source, at in ((forget_out, 0), (admit_out, BW)):
            back = back + lax.dot_general(
                source[:, cols],
                gates_ref[cols, at : at + BW],
                (((1,), (1,)), ((), ())),
                preferred_element_type=F32,
            )
        branch_out[:, cols] = back.astype(BF)


def backward_rows(off, adjoint, later, local, reach, rate, conv, forget, admit, x_win, edge, gates, chan, carry, tail, after, tokens):
    total, window = x_win.shape
    share = chan.shape[1]
    seqs = total // tokens
    part = lambda width: pl.BlockSpec((tokens, width), lambda q: (q, 0))
    return pl.pallas_call(
        backward_rows_kernel,
        grid=(seqs,),
        in_specs=[pl.BlockSpec(memory_space=pltpu.SMEM)]
        + [part(share)] * 8
        + [part(window)]
        + [whole(v.shape) for v in (edge, gates, chan)]
        + [per_seq(share), per_seq(share), whole(after.shape)],
        out_specs=[part(window), part(window), part(window), whole((8, share))],
        out_shape=[jax.ShapeDtypeStruct((total, window), BF)] * 3
        + [jax.ShapeDtypeStruct((8, share), F32)],
        scratch_shapes=[pltpu.VMEM((tokens, window), F32)],
        compiler_params=pltpu.CompilerParams(vmem_limit_bytes=48 * 1024 * 1024),
        cost_estimate=pl.CostEstimate(flops=1000, bytes_accessed=1000, transcendentals=0),
        name="backward_rows",
    )(off, adjoint, later, local, reach, rate, conv, forget, admit, x_win, edge, gates, chan, carry[:, None, :], tail[:, None, :], after)


def partner(mask):
    s = lax.axis_index("seq")
    if mask == 1:
        other = s + 1 - 2 * (s % 2)
    else:
        other = (s + 2) % 4
    return {"seq": other}


def greet():
    barrier = pltpu.get_barrier_semaphore()
    for mask in (1, 2):
        pl.semaphore_signal(barrier, inc=1, device_id=partner(mask), device_id_type=MESH)
    pl.semaphore_wait(barrier, 2)


def sender(sends, recvs):
    def send(slot, source, target, mask):
        copy = pltpu.make_async_remote_copy(
            src_ref=source,
            dst_ref=target,
            send_sem=sends.at[slot],
            recv_sem=recvs.at[slot],
            device_id=partner(mask),
            device_id_type=MESH,
        )
        copy.start()
        return copy

    return send


def over_chunks(rows, run):
    def step(i, carry):
        run(pl.ds(pl.multiple_of(i * ROWS16, ROWS16), ROWS16))
        return carry

    lax.fori_loop(0, rows // ROWS16, step, 0)


def reduce_phase(product, send, first_slot, acc, sent, got):
    rows = acc.shape[1]
    half = rows // 2
    low, high = pl.ds(0, half), pl.ds(half, half)
    product(3, lambda cols, value: sent.__setitem__((0, slice(None), cols), value.astype(BF)))
    far_near = send(first_slot, sent.at[0, low], got.at[0, low], 1)
    far_side = send(first_slot + 1, sent.at[0, high], got.at[0, high], 2)
    product(1, lambda cols, value: acc.__setitem__((1, slice(None), cols), value))
    over_chunks(half, lambda r: sent.__setitem__((1, r), acc[1, r].astype(BF)))
    near_low = send(first_slot + 2, sent.at[1, low], got.at[1, low], 1)
    product(2, lambda cols, value: acc.__setitem__((2, slice(None), cols), value))

    def tail(k):
        def run(r):
            r = pl.ds(pl.multiple_of(r.start + half, ROWS16), ROWS16)
            sent[k, r] = acc[k, r].astype(BF)

        return run

    over_chunks(half, tail(2))
    side_high = send(first_slot + 3, sent.at[2, high], got.at[2, high], 2)
    far_side.wait_recv()

    def add_high(r):
        r = pl.ds(pl.multiple_of(r.start + half, ROWS16), ROWS16)
        sent[1, r] = (acc[1, r] + got[0, r].astype(F32)).astype(BF)

    over_chunks(half, add_high)
    near_high = send(first_slot + 4, sent.at[1, high], got.at[1, high], 1)
    far_near.wait_recv()

    def add_low(r):
        sent[2, r] = (acc[2, r] + got[0, r].astype(F32)).astype(BF)

    over_chunks(half, add_low)
    side_low = send(first_slot + 5, sent.at[2, low], got.at[2, low], 2)
    product(0, lambda cols, value: acc.__setitem__((0, slice(None), cols), value))
    arriving = [near_low, side_high, near_high, side_low]
    for copy in arriving:
        copy.wait_recv()
    return [far_near, far_side] + arriving


def gather_phase(send, first_slot, out):
    half = out.shape[1] // 2
    low, high = pl.ds(0, half), pl.ds(half, half)
    near_low = send(first_slot, out.at[0, low], out.at[1, low], 1)
    side_high = send(first_slot + 1, out.at[0, high], out.at[2, high], 2)
    near_high = send(first_slot + 2, out.at[0, high], out.at[1, high], 1)
    side_low = send(first_slot + 3, out.at[0, low], out.at[2, low], 2)
    near_low.wait_recv()
    far_low = send(first_slot + 4, out.at[1, low], out.at[3, low], 2)
    side_high.wait_recv()
    far_high = send(first_slot + 5, out.at[2, high], out.at[3, high], 1)
    for copy in (near_high, side_low, far_low, far_high):
        copy.wait_recv()
    return [near_low, side_high, near_high, side_low, far_low, far_high]


def product_of(left, right, contract, rows, tile):
    def product(k, store):
        def step(c, carry):
            cols = pl.ds(pl.multiple_of(c * tile, tile), tile)
            total = None
            for a, b in zip(left, right):
                part = b[cols, :] if contract else b[:, cols]
                value = lax.dot_general(
                    a[k * rows : (k + 1) * rows, :],
                    part,
                    (((1,), (1 if contract else 0,)), ((), ())),
                    preferred_element_type=F32,
                )
                total = value if total is None else total + value
            store(cols, total)
            return carry

        width = right[0].shape[0 if contract else 1]
        lax.fori_loop(0, width // tile, step, 0)

    return product


def rms_parts(values):
    return lax.rsqrt(jnp.mean(values * values, axis=-1, keepdims=True) + 1e-06)


def stream_kernel(
    mixed_ref, weight_ref, flat_ref, gain_ref,
    stream_out, temporal_out, normed_out,
    acc, sent, got, sends, recvs,
):
    rows = flat_ref.shape[0]
    greet()
    send = sender(sends, recvs)
    copies = reduce_phase(
        product_of([mixed_ref], [weight_ref], False, rows, 512), send, 0, acc, sent, got
    )

    def finish(r):
        temporal = acc[0, r] + got[1, r].astype(F32) + got[2, r].astype(F32)
        temporal_out[r] = temporal
        stream = flat_ref[r].astype(F32) + temporal
        stream_out[r] = stream
        normed_out[0, r] = (stream * rms_parts(stream) * gain_ref[...]).astype(BF)

    over_chunks(rows, finish)
    copies += gather_phase(send, 6, normed_out)
    for copy in copies:
        copy.wait_send()


def exchange_scratch(rows, width, copies):
    return [
        pltpu.VMEM((3, rows, width), F32),
        pltpu.VMEM((3, rows, width), BF),
        pltpu.VMEM((3, rows, width), BF),
        pltpu.SemaphoreType.DMA((copies,)),
        pltpu.SemaphoreType.DMA((copies,)),
    ]


def remote_call(kernel, name, ident, outs, operands, scratch):
    return pl.pallas_call(
        kernel,
        in_specs=[pl.BlockSpec(memory_space=pltpu.VMEM)] * len(operands),
        out_specs=[pl.BlockSpec(memory_space=pltpu.VMEM)] * len(outs),
        out_shape=[jax.ShapeDtypeStruct(shape, kind) for shape, kind in outs],
        scratch_shapes=scratch,
        compiler_params=pltpu.CompilerParams(
            collective_id=ident, has_side_effects=True, vmem_limit_bytes=60 * 1024 * 1024
        ),
        cost_estimate=pl.CostEstimate(flops=1000, bytes_accessed=1000, transcendentals=0),
        name=name,
    )(*operands)


def stream_and_norm(mixed, weight, flat, gain):
    rows, width = flat.shape
    groups = mixed.shape[0] // rows
    return remote_call(
        stream_kernel,
        "stream_and_norm",
        1,
        [((rows, width), F32), ((rows, width), F32), ((groups, rows, width), BF)],
        (mixed, weight, flat, gain),
        exchange_scratch(rows, width, 12),
    )


def stream_back_kernel(
    rows_ref, weight_ref, stream_ref, gain_ref, upstream_ref,
    grad_out, low_out, gain_out,
    acc, sent, got, sends, recvs,
):
    rows, width = stream_ref.shape
    greet()
    send = sender(sends, recvs)
    copies = reduce_phase(
        product_of([rows_ref], [weight_ref], True, rows, 512), send, 0, acc, sent, got
    )
    gain_out[...] = jnp.zeros_like(gain_out)

    def finish(r):
        grad = acc[0, r] + got[1, r].astype(F32) + got[2, r].astype(F32)
        stream = stream_ref[r]
        inv = rms_parts(stream)
        scaled = grad * gain_ref[...]
        inner = jnp.mean(stream * scaled, axis=-1, keepdims=True)
        total = upstream_ref[r].astype(F32) + inv * scaled - stream * (inv * inv * inv * inner)
        grad_out[r] = total
        low_out[0, r] = total.astype(BF)
        gained = grad * stream * inv
        gain_out[...] += gained[:8] + gained[8:]

    over_chunks(rows, finish)
    copies += gather_phase(send, 6, low_out)
    for copy in copies:
        copy.wait_send()


def stream_back(rows_all, weight, stream, gain, upstream):
    rows, width = stream.shape
    groups = rows_all.shape[0] // rows
    return remote_call(
        stream_back_kernel,
        "stream_back",
        2,
        [((rows, width), F32), ((groups, rows, width), BF), ((8, width), F32)],
        (rows_all, weight, stream, gain, upstream),
        exchange_scratch(rows, width, 12),
    )


def inputs_back_kernel(
    branch_ref, y_ref, weight_ref, flat_ref, gain_ref, stream_grad_ref,
    grad_out, gain_out,
    acc, sent, got, sends, recvs,
):
    rows, width = flat_ref.shape
    greet()
    send = sender(sends, recvs)
    window = branch_ref.shape[1]
    weights = [weight_ref.at[:, :window], weight_ref.at[:, window:]]
    copies = reduce_phase(
        product_of([branch_ref, y_ref], weights, True, rows, 512), send, 0, acc, sent, got
    )
    gain_out[...] = jnp.zeros_like(gain_out)

    def finish(r):
        grad = acc[0, r] + got[1, r].astype(F32) + got[2, r].astype(F32)
        values = flat_ref[r].astype(F32)
        inv = rms_parts(values)
        scaled = grad * gain_ref[...]
        inner = jnp.mean(values * scaled, axis=-1, keepdims=True)
        grad_out[r] = stream_grad_ref[r] + inv * scaled - values * (inv * inv * inv * inner)
        gained = grad * values * inv
        gain_out[...] += gained[:8] + gained[8:]

    over_chunks(rows, finish)
    for copy in copies:
        copy.wait_send()


def inputs_back(branch_rows, y_rows, weight, flat, gain, stream_grad):
    rows, width = flat.shape
    return remote_call(
        inputs_back_kernel,
        "inputs_back",
        3,
        [((rows, width), F32), ((8, width), F32)],
        (branch_rows, y_rows, weight, flat, gain, stream_grad),
        exchange_scratch(rows, width, 6),
    )


def result_kernel(
    hidden_ref, weight_ref, stream_ref, temporal_ref, valid_ref,
    result_out, sums_out,
    acc, sent, got, sends, recvs,
):
    rows = stream_ref.shape[0]
    greet()
    send = sender(sends, recvs)
    copies = reduce_phase(
        product_of([hidden_ref], [weight_ref], False, rows, 512), send, 0, acc, sent, got
    )
    sums_out[...] = jnp.zeros_like(sums_out)

    def finish(r):
        feed = acc[0, r] + got[1, r].astype(F32) + got[2, r].astype(F32)
        result = stream_ref[r] + feed
        result_out[r] = result.astype(BF)
        valid = valid_ref[r]
        for i, values in enumerate((result, temporal_ref[r], feed)):
            square = valid * values * values
            sums_out[i] += square[:8] + square[8:]

    over_chunks(rows, finish)
    for copy in copies:
        copy.wait_send()


def result_of(hidden, weight, stream, temporal, valid):
    rows, width = stream.shape
    return remote_call(
        result_kernel,
        "result_of",
        4,
        [((rows, width), BF), ((3, 8, width), F32)],
        (hidden, weight, stream, temporal, valid),
        exchange_scratch(rows, width, 6),
    )


def body(
    inputs,
    lengths,
    norm_gain,
    gelu_weight,
    branch_weight,
    forget_gates,
    admit_gates,
    forget_bias,
    admit_bias,
    decay_rate,
    conv_weight,
    conv_bias,
    out_weight,
    mlp_gain,
    gate_weight,
    up_weight,
    down_weight,
    cotangent,
):
    groups = lax.axis_size("seq")
    wide = lax.axis_size("wide")
    s = lax.axis_index("seq")
    w = lax.axis_index("wide")
    seqs, tokens, width = inputs.shape
    rows = seqs * tokens
    total = groups * rows
    all_seqs = groups * seqs
    channels = gelu_weight.shape[1]
    share = channels // groups
    window = (share + BW - 1) // BW * BW
    blocks = window // BW

    def base_of(index):
        return jnp.minimum(index * share // BW * BW, channels - window)

    base = base_of(s)
    off = s * share - base
    quarter = width // groups
    gate_cols = 2 * BW // groups

    flat_low = inputs.reshape(rows, width)
    upstream = cotangent.reshape(rows, width)
    edge = lax.ppermute(
        inputs[:, tokens - HALO :, :].reshape(seqs * HALO, width),
        "wide",
        [(i, i + 1) for i in range(wide - 1)],
    )
    token_blocks = gather_seq(flat_low)
    edge_blocks = [swap(edge, k) if k else edge for k in range(groups)]

    x_y_cols = lax.all_gather(
        jnp.concatenate(
            [
                lax.dynamic_slice_in_dim(branch_weight, base, window, 1),
                lax.dynamic_slice_in_dim(gelu_weight, s * share, share, 1),
            ],
            axis=1,
        ),
        "wide",
        axis=0,
        tiled=True,
    )
    dw, rw = width // wide, channels // wide
    small = jnp.concatenate(
        [norm_gain, mlp_gain, forget_bias, admit_bias, decay_rate, conv_bias, conv_weight.reshape(-1)]
    ).reshape(-1, gate_cols)
    gates_quarter = jnp.concatenate([forget_gates, admit_gates], axis=1)
    small = jnp.concatenate(
        [lax.dynamic_slice_in_dim(gates_quarter, s * gate_cols, gate_cols, 1), small], axis=0
    )
    small, token_blocks[1] = lax.optimization_barrier((small, token_blocks[1]))
    small = lax.all_gather(small, "wide")
    gates_quarter = small[:, :rw].reshape(channels, gate_cols)
    small = small[:, rw:].reshape(wide, -1).astype(F32)
    gain_one = small[:, :dw].reshape(1, width)
    gain_two = small[:, dw : 2 * dw].reshape(1, width)
    per_channel = small[:, 2 * dw :].reshape(wide, 8, rw).transpose(1, 0, 2).reshape(8, channels)
    per_channel = lax.dynamic_slice_in_dim(per_channel, s * share, share, 1)

    out_quarter = lax.all_gather(
        lax.dynamic_slice_in_dim(out_weight, s * quarter, quarter, 1), "wide", axis=0, tiled=True
    )
    mlp_full = lax.all_gather(
        jnp.concatenate([gate_weight, up_weight], axis=1), "wide", axis=0, tiled=True
    )
    down_full = lax.all_gather(down_weight, "wide", axis=1, tiled=True)
    hidden_units = gate_weight.shape[1]

    def in_order(parts):
        near = [jnp.where(s % 2 == 1, parts[k ^ 1], parts[k]) for k in range(groups)]
        return [jnp.where(s // 2 == 1, near[k ^ 2], near[k]) for k in range(groups)]

    gate_parts, out_parts = [], []
    for k in range(groups):
        other = s ^ k
        part = lax.dynamic_slice_in_dim(gates_quarter, base_of(other), window, 0)
        gate_parts.append(swap(part, k) if k else part)
        part = lax.dynamic_slice_in_dim(out_quarter, other * share, share, 0)
        out_parts.append(swap(part, k) if k else part)
    gates = jnp.concatenate(in_order(gate_parts), axis=1)
    out_rows = jnp.concatenate(in_order(out_parts), axis=1)

    all_low = jnp.concatenate(token_blocks + edge_blocks, axis=0)
    normed_ext = rms_norm(all_low.astype(F32), gain_one).astype(BF)
    normed_all = normed_ext[:total]

    x_y = dot(normed_all, x_y_cols)
    x_win = x_y[:, :window].astype(BF)
    branch_y = x_y[:, window:]
    edge_win = dot(normed_ext[total:], x_y_cols[:, :window]).astype(BF).astype(F32)
    offset = off.reshape(1)
    forget, admit, conv_out, rate, local, reach, ends = temporal_forward(
        offset, x_win, edge_win, gates, per_channel, tokens
    )
    ends, later_upstream = lax.optimization_barrier((ends, upstream))
    upstream_all = jnp.concatenate(gather_seq(later_upstream), axis=0)
    ends = lax.all_gather(ends, "wide")[:, :, :, 0]
    carry = jnp.zeros((all_seqs, share), F32)
    for j in range(wide - 1):
        carry = jnp.where(j < w, ends[j, :, 0] * carry + ends[j, :, 1], carry)
    carried = local.reshape(all_seqs, tokens, share) + reach.reshape(
        all_seqs, tokens, share
    ) * carry[:, None, :]
    state = carried.astype(BF).astype(F32).reshape(total, share)

    gelu_y = jax.nn.gelu(branch_y)
    mixed_low = (state * gelu_y).astype(BF)
    stream, temporal, normed_two_all = stream_and_norm(mixed_low, out_rows, flat_low, gain_two)
    normed_two_all = normed_two_all.reshape(total, width)

    gate_up = dot(normed_two_all, mlp_full)
    gate, up_values = gate_up[:, :hidden_units], gate_up[:, hidden_units:]
    gelu_gate = jax.nn.gelu(gate)
    hidden_low = (gelu_gate * up_values).astype(BF)
    down_part = contract_rows(hidden_low, upstream_all).astype(BF)
    hidden_low, down_part, upstream_low = lax.optimization_barrier(
        (hidden_low, down_part, upstream_all)
    )
    down_grad = lax.psum_scatter(down_part, "wide", scatter_dimension=1, tiled=True)
    hidden_grad = contract_last(upstream_low, down_full)
    gate_rows = (hidden_grad * up_values * gelu_parts(gate)[1]).astype(BF)
    up_rows = (hidden_grad * gelu_gate).astype(BF)
    mlp_rows = jnp.concatenate([gate_rows, up_rows], axis=1)
    mlp_part = contract_rows(normed_two_all, mlp_rows).astype(BF)
    mlp_rows, mlp_part = lax.optimization_barrier((mlp_rows, mlp_part))
    mlp_grad = lax.psum_scatter(mlp_part, "wide", scatter_dimension=0, tiled=True)
    stream_grad, stream_low_all, gain_two_grad = stream_back(
        mlp_rows, mlp_full, stream, gain_two, upstream
    )
    gain_two_grad = jnp.sum(gain_two_grad, axis=0)
    stream_low_all = stream_low_all.reshape(total, width)
    stream_low_all, down_grad = lax.optimization_barrier((stream_low_all, down_grad))
    position = w * tokens + jnp.arange(tokens, dtype=jnp.int32)
    valid = (position[None, :] < lengths[:, None]).astype(F32).reshape(rows, 1)
    mixed_grad = contract_last(stream_low_all, out_rows)
    y_rows, adjoint, later, heads = backward_scan(
        mixed_grad, branch_y, local, reach, carry, rate, tokens
    )
    heads = lax.all_gather(heads, "wide")[:, :, 0]

    def firsts(values):
        return values.reshape(all_seqs, tokens, share)[:, :HALO].astype(F32)

    first_rate = -8.0 * per_channel[2] * (0.1 + 0.9 * jax.nn.sigmoid(firsts(forget)))
    gain = jnp.sqrt(-jnp.expm1(2.0 * first_rate)) * jax.nn.sigmoid(firsts(admit))
    after = lax.ppermute(
        jnp.stack([firsts(adjoint) * gain, firsts(later) * gain]),
        "wide",
        [(i + 1, i) for i in range(wide - 1)],
    )
    tail = jnp.zeros((all_seqs, share), F32)
    next_tail = tail
    for j in range(wide - 1, 0, -1):
        stepped = ends[j, :, 0] * tail + heads[j]
        next_tail = jnp.where(j > w + 1, stepped, next_tail)
        tail = jnp.where(j > w, stepped, tail)
    after = (after[0] + after[1] * next_tail[:, None, :]).reshape(all_seqs * HALO, share)
    branch_rows, forget_win, admit_win, channel_grads = backward_rows(
        offset, adjoint, later, local, reach, rate, conv_out, forget, admit,
        x_win, edge_win, gates, per_channel, carry, tail, after, tokens,
    )
    bases = [min(j * share // BW * BW, channels - window) for j in range(groups)]

    def placed(parts, axis):
        rest = [
            tuple(
                (bases[j], channels - window - bases[j]) if d == axis else (0, 0) for d in range(2)
            )
            for j in range(groups)
        ]
        return sum(jnp.pad(p.astype(F32), r) for p, r in zip(parts, rest))

    def swapped(part_of):
        return [swap(part_of(s ^ k), k) if k else part_of(s) for k in range(groups)]

    def stack(values):
        values = values.reshape(wide, values.shape[0] // wide, values.shape[1])
        tiles = values.shape[2] // LANES
        return jnp.concatenate(
            [values[:, :, i * LANES : (i + 1) * LANES] for i in range(tiles)], axis=1
        )

    def unstack(values, count, columns):
        return jnp.concatenate(
            [values[i * count : (i + 1) * count] for i in range(columns // LANES)], axis=1
        )

    out_grad = contract_rows(mixed_low, stream_low_all).astype(BF)
    out_cols = jnp.concatenate(
        in_order(
            swapped(lambda j: lax.dynamic_slice_in_dim(out_grad, j * quarter, quarter, 1))
        ),
        axis=0,
    )
    gelu_part = contract_rows(normed_all, y_rows).astype(BF)

    gate_grads = jnp.concatenate(
        [
            jnp.einsum(
                "tki,tkj->kij",
                x_win.reshape(total, blocks, BW),
                rows_win.reshape(total, blocks, BW),
                preferred_element_type=F32,
            ).reshape(window, BW)
            for rows_win in (forget_win, admit_win)
        ],
        axis=1,
    ).astype(BF)
    gate_cols_grad = placed(
        in_order(
            swapped(lambda j: lax.dynamic_slice_in_dim(gate_grads, j * gate_cols, gate_cols, 1))
        ),
        0,
    ).astype(BF)
    branch_part = contract_rows(normed_all, branch_rows).astype(BF)
    first_pieces = [(gelu_part, share), (out_cols, quarter)]
    second_pieces = [(branch_part, window), (gate_cols_grad, gate_cols)]
    first = jnp.concatenate([stack(values) for values, _unused in first_pieces], axis=1)
    second = jnp.concatenate([stack(values) for values, _unused in second_pieces], axis=1)
    first, mlp_grad, branch_late = lax.optimization_barrier((first, mlp_grad, branch_rows))
    first = lax.psum_scatter(first, "wide", scatter_dimension=0, tiled=True)
    inputs_grad, gain_one_grad = inputs_back(
        branch_late, y_rows, x_y_cols, flat_low, gain_one, stream_grad
    )
    second = lax.psum_scatter(second, "wide", scatter_dimension=0, tiled=True)
    first, gain_one_grad, stream_late = lax.optimization_barrier((first, gain_one_grad, stream))
    output, square_sums = result_of(hidden_low, down_full, stream_late, temporal, valid)
    second, square_sums = lax.optimization_barrier((second, square_sums))

    def spread(summed, pieces):
        parts = in_order(swapped(lambda j: summed[0]))
        start, spread_pieces = 0, []
        for values, columns in pieces:
            count = values.shape[0] // wide
            size = count * columns // LANES
            spread_pieces.append([unstack(p[start : start + size], count, columns) for p in parts])
            start += size
        return spread_pieces

    gelu_parts_all, out_parts_all = spread(first, first_pieces)
    branch_parts_all, gate_parts_all = spread(second, second_pieces)
    gelu_whole = jnp.concatenate(gelu_parts_all, axis=1).astype(F32)
    out_whole = jnp.concatenate(out_parts_all, axis=1).astype(F32)
    branch_whole = placed(branch_parts_all, 1)
    gates_whole = jnp.concatenate(gate_parts_all, axis=1).astype(F32)
    partial_sums = jnp.concatenate([jnp.sum(square_sums, axis=(1, 2)), jnp.sum(valid).reshape(1)])
    inputs_grad = inputs_grad.reshape(seqs, tokens, width)
    output = output.reshape(seqs, tokens, width)
    channel_all = lax.dynamic_update_slice_in_dim(
        jnp.zeros((8, channels), F32), channel_grads, s * share, 1
    )
    sums = jnp.concatenate(
        [
            channel_all.reshape(8, wide, rw).transpose(1, 0, 2).reshape(wide, 8 * rw),
            jnp.sum(gain_one_grad, axis=0).reshape(wide, dw),
            gain_two_grad.reshape(wide, dw),
            jnp.tile(partial_sums[None, :], (wide, 1)),
        ],
        axis=1,
    )
    sums = jnp.sum(lax.all_to_all(sums, "wide", 0, 0), axis=0)
    sums = sums + swap(sums, 1)
    sums = sums + swap(sums, 2)
    channel_sums = sums[: 8 * rw].reshape(8, rw)
    gain_sums = sums[8 * rw : 8 * rw + 2 * dw].reshape(2, dw)
    totals = sums[8 * rw + 2 * dw :]
    statistics = jnp.sqrt(totals[0:3] / (totals[3] * width))
    return (
        output,
        inputs_grad,
        gain_sums[0],
        gelu_whole,
        branch_whole,
        gates_whole[:, :BW],
        gates_whole[:, BW:],
        channel_sums[0],
        channel_sums[1],
        channel_sums[2],
        channel_sums[4:8],
        channel_sums[3],
        out_whole,
        gain_sums[1],
        mlp_grad[:, :hidden_units].astype(F32),
        mlp_grad[:, hidden_units:].astype(F32),
        down_grad.astype(F32),
        statistics,
    )


def solution(mesh):
    in_specs = (
        P("seq", "wide", None),
        P("seq"),
        P("wide"),
        P("wide", None),
        P("wide", None),
        P("wide", None),
        P("wide", None),
        P("wide"),
        P("wide"),
        P("wide"),
        P(None, "wide"),
        P("wide"),
        P("wide", None),
        P("wide"),
        P("wide", "seq"),
        P("wide", "seq"),
        P("seq", "wide"),
        P("seq", "wide", None),
    )
    out_specs = (
        P("seq", "wide", None),
        P("seq", "wide", None),
        P("wide"),
        P("wide", None),
        P("wide", None),
        P("wide", None),
        P("wide", None),
        P("wide"),
        P("wide"),
        P("wide"),
        P(None, "wide"),
        P("wide"),
        P("wide", None),
        P("wide"),
        P("wide", "seq"),
        P("wide", "seq"),
        P("seq", "wide"),
        P(),
    )
    return jax.shard_map(body, mesh=mesh, in_specs=in_specs, out_specs=out_specs, check_vma=False)
```

time: 1130 us -> 727 us (0.64)
  waiting for transfers between devices: 502 us -> 81.6 us
  Pallas kernels: 0 us -> 296 us
  matrix products: 197 us -> 100 us
  local copies, waits for them, and re-layouts: 165 us -> 71.6 us
  other arithmetic: 109 us -> 45.4 us
  starting transfers between devices: 63.5 us -> 43.7 us
    pallas_call x0 -> x7, Pallas kernels: none -> 296 us  [the longest x4 256 us: remote_call(): pl.pallas_call(kernel, in_specs=[pl.BlockSpec(memory_space=pltpu.VMEM)] *...]
    reduce_scatter x5 -> x4, waiting for transfers between devices: 247 us -> 1.78 us  [the longest x1 1.72 us: body(): lax.psum_scatter(mlp_part, 'wide', scatter_dimension=0, tiled=True)]
    ppermute x53 -> x31, waiting for transfers between devices: 247 us -> 77.7 us  [swap(): lax.ppermute(values, 'seq', [(i, i ^ mask) for i in range(lax.axis_size('...]
    dynamic_update_slice x20 -> x0, local copies, waits for them, and re-layouts: 65.3 us -> none  [the longest x4 26.3 us: body(): branch_whole = lax.dynamic_update_slice_in_dim(branch_whole, part, start, 1)]
    dot_general x14 -> x2, matrix products: 74.8 us -> 25.4 us  [contract_last(): lax.dot_general(left, right, (((1,), (1,)), ((), ())), preferred_element_...]
    dot_general x11 -> x3, matrix products: 64.4 us -> 29.5 us  [dot(): return jnp.dot(left, right, preferred_element_type=F32)]
    reduce_sum x6 -> x5, other arithmetic: 25.4 us -> 1.95 us  [the longest x1 1.16 us: body(): jnp.sum(square_sums, axis=(1, 2))]
    another operation x12 -> x2, other arithmetic: 22.1 us -> 1.36 us  [body(): jnp.stack([firsts(adjoint) * gain, firsts(later) * gain])]
  transfers between devices with their start and end apart: 66 -> 41, of which waited for: 37 -> 10; matrix products, arithmetic and copies ran while one was open for 32% -> 28% of each run, Pallas kernels for 0% -> 41%
where the time goes in v2:
time: 727 us; the launch traced here: 717 us
  Pallas kernels  296 us (41%)
  matrix products  100 us (14%)
  waiting for transfers between devices  81.6 us (11%)
  local copies, waits for them, and re-layouts  71.6 us (10%)
  blocking collectives  61.8 us (9%)
  other arithmetic  45.4 us (6%)
  starting transfers between devices  43.7 us (6%)
  between operations  17 us (2%)
    pallas_call x4, Pallas kernels, remote_call(): pl.pallas_call(kernel, in_specs=[pl.BlockSpec(memory_space=pltpu.VMEM)] *...  256 us
    ppermute x31, waiting for transfers between devices, swap(): lax.ppermute(values, 'seq', [(i, i ^ mask) for i in range(lax.axis_size('...  77.7 us
    unnamed x195, local copies, waits for them, and re-layouts  44.7 us
    dot_general x5, matrix products, contract_rows(): lax.dot_general(left, right, (((0,), (0,)), ((), ())), preferred_element_...  42.2 us
    ppermute x31, starting transfers between devices, swap(): lax.ppermute(values, 'seq', [(i, i ^ mask) for i in range(lax.axis_size('...  39.3 us
    dot_general x3, matrix products, dot(): return jnp.dot(left, right, preferred_element_type=F32)  29.5 us
    dot_general x2, matrix products, contract_last(): lax.dot_general(left, right, (((1,), (1,)), ((), ())), preferred_element_...  25.4 us
    all_gather x1, blocking collectives, body(): ends = lax.all_gather(ends, 'wide')[:, :, :, 0]  16.5 us
  transfers between devices with their start and end apart: 41, of which 10 were waited for; matrix products, arithmetic and copies ran while one was open for 28% of the time, Pallas kernels for 41%

profile of v2, /device:TPU:0, one launch (start us, length us, event | category | flops | bytes accessed | tf_op | source)
XLA Modules:
  0.0 717.3 jit_solution(3885905415599334511)
XLA Ops:
  21.6 18.4 %collective-permute-done = bf16[256,2048]{1,0:T(8,128)(2,1)} collective-permute-done((bf16[256,2048]{1,0:T(8,128)(2,1)S(1)}, bf16[256,2048]{1,0:T(8,128)(2,1)}, u32[]{:S(2)}, u32[]{:S(2)}) %collective-permute-start) | collective-permute-done | bytes 1048608 | tf_op jit(solution)/shard_map/ppermute | solution.py:31
  40.0 16.1 %all-gather = bf16[2752,128]{1,0:T(8,128)(2,1)S(1)} all-gather(bf16[344,128]{1,0:T(8,128)(2,1)S(1)} %pad_maximum_fusion.7), channel_id=2, replica_groups=mesh['seq'=4,'wide'=8] {'wide'}, dimensions={0}, use_global_device_ids=true | all-gather | bytes 792576 | tf_op jit(solution)/shard_map/all_gather | solution.py:705
  75.6 9.2 %collective-permute-done.2 = bf16[128,2048]{1,0:T(8,128)(2,1)} collective-permute-done((bf16[128,2048]{1,0:T(8,128)(2,1)S(1)}, bf16[128,2048]{1,0:T(8,128)(2,1)}, u32[]{:S(2)}, u32[]{:S(2)}) %collective-permute-start.2) | collective-permute-done | bytes 524320 | tf_op jit(solution)/shard_map/ppermute | solution.py:31
  95.1 5.5 fusion.2
  108.8 10.6 %fusion.22 = f32[1024,1408]{1,0:T(8,128)S(1)} fusion(bf16[2048,1408]{1,0:T(8,128)(2,1)} %all-gather.8.cloned.1.call-done.weight_ref, bf16[1088,2048]{1,0:T(8,128)(2,1)} %fusion.2), kind=kOutput, calls=%fused_computation.34 | convolution fusion | flops 5905580032 | bytes 15728640 | tf_op jit(solution)/shard_map/dot_general | solution.py:19
  122.2 12.7 %temporal_forward.1 = (bf16[1024,640]{1,0:T(8,128)(2,1)S(1)}, bf16[1024,640]{1,0:T(8,128)(2,1)S(1)}, f32[1024,640]{1,0:T(8,128)}, f32[1024,640]{1,0:T(8,128)}, f...) custom-call(s32[1]{0:T(128)} %bitcast.off_ref, bf16[1024,768]{1,0:T(8,128)(2,1)S(1)} %slice.1020.x_ref, ...), custom_call_target="tpu_custom_call" | custom-call | flops 1000 | bytes 1000 | tf_op jit(solution)/shard_map/temporal_forward/pallas_call | solution.py:146
  145.7 16.5 %all-gather.1 = f32[64,2,1,640]{3,1,2,0:T(2,128)S(1)} all-gather(f32[8,2,1,640]{3,1,2,0:T(2,128)S(1)} %copy.110), channel_id=3, replica_groups=mesh['seq'=4,'wide'=8] {'wide'}, dimensions={0}, use_global_device_ids=true | all-gather | bytes 368640 | tf_op jit(solution)/shard_map/all_gather | solution.py:750
  171.5 84.1 %stream_and_norm.1 = (f32[256,2048]{1,0:T(8,128)}, f32[256,2048]{1,0:T(8,128)}, bf16[4,256,2048]{2,1,0:T(8,128)(2,1)}) custom-call(bf16[1024,640]{1,0:T(8,128)(2,1)} %get-tuple-element.113.mixed_ref, bf16[640,2048]{1,0:T(8,128)(2,1)} %pad_maximum_fusion.1.weight_ref, bf16[256,2048]{1,0:T(8,128)(2,1)} %bitcast.508, f32[1,2048]{1,0:T(1,128)} %bitcast.561), custom_call_target="tpu_custom_call" | custom-call | flops 1000 | bytes 1000 | tf_op jit(solution)/shard_map/stream_and_norm/pallas_call | solution.py:481
  263.8 6.3 collective-permute-done.17
  271.0 17.0 %fusion.103 = f32[1024,3072]{1,0:T(8,128)S(1)} fusion(bf16[1024,2048]{1,0:T(8,128)(2,1)} %bitcast.567, bf16[2048,3072]{1,0:T(8,128)(2,1)} %all-gather.12.cloned.1.call-done.weight_ref), kind=kOutput, calls=%fused_computation.352 | convolution fusion | flops 12884901888 | bytes 29360128 | tf_op jit(solution)/shard_map/dot_general | solution.py:19
  295.5 8.7 %convolution_convert_fusion.1 = bf16[1536,2048]{1,0:T(8,128)(2,1)} fusion(bf16[1024,1536]{1,0:T(8,128)(2,1)S(1)} %multiply_convert_fusion.1.hidden_ref, bf16[1024,2048]{1,0:T(8,128)(2,1)S(1)} %copy-done.38), kind=kOutput, calls=%fused_computation.9 | convolution fusion | flops 6445596672 | bytes 13631488 | tf_op jit(solution)/shard_map/dot_general | solution.py:27
  304.7 17.9 %fusion.18 = (bf16[1024,1536]{1,0:T(8,128)(2,1)S(1)}, bf16[1024,1536]{1,0:T(8,128)(2,1)S(1)}) fusion(f32[1024,3072]{1,0:T(8,128)} %copy-done.14, bf16[1024,2048]{1,0:T(8,128)(2,1)} %constant_dynamic-update-slice_fusion.9, bf16[1536,2048]{1,0:T(8,128)(2,1)} %all-gather.14.cloned.1.call-done.weight_ref), kind=kOutput, calls=%fused_computation.25 | convolution fusion | flops 6486491136 | bytes 29360128 | tf_op jit(solution)/shard_map/dot_general | solution.py:23
  326.0 18.8 %convolution_convert_fusion = bf16[2048,3072]{1,0:T(8,128)(2,1)} fusion(bf16[1024,2048]{1,0:T(8,128)(2,1)} %bitcast.568, bf16[1024,1536]{1,0:T(8,128)(2,1)S(1)} %get-tuple-element.111, bf16[1024,1536]{1,0:T(8,128)(2,1)S(1)} %get-tuple-element.110), kind=kOutput, calls=%fused_computation | convolution fusion | flops 12903776256 | bytes 23068672 | tf_op jit(solution)/shard_map/dot_general | solution.py:27
  345.2 83.6 %stream_back.1 = (f32[256,2048]{1,0:T(8,128)}, bf16[4,256,2048]{2,1,0:T(8,128)(2,1)}, f32[8,2048]{1,0:T(8,128)}) custom-call(bf16[1024,3072]{1,0:T(8,128)(2,1)} %pad_maximum_fusion.rows_ref, bf16[2048,3072]{1,0:T(8,128)(2,1)} %all-gather.12.cloned.1.call-done.weight_ref, f32[256,2048]{1,0:T(8,128)} %get-tuple-element.91.stream_ref, f32[1,2048]{1,0:T(1,128)} %bitcast.562, ...), custom_call_target="tpu_custom_call" | custom-call | flops 1000 | bytes 1000 | tf_op jit(solution)/shard_map/stream_back/pallas_call | solution.py:481
  428.9 7.5 %fusion.96.grad_ref = f32[1024,640]{1,0:T(8,128)} fusion(bf16[1024,2048]{1,0:T(8,128)(2,1)} %bitcast.569, bf16[640,512]{1,0:T(8,128)(2,1)} %copy-done.24, bf16[640,512]{1,0:T(8,128)(2,1)} %copy-done.23, bf16[640,512]{1,0:T(8,128)(2,1)S(1)} %copy-done.22, bf16[640,512]{1,0:T(8,128)(2,1)S(1)} %get-tuple-element.118), kind=kOutput, calls=%fused_computation.347 | convolution fusion | flops 2694840320 | bytes 9437184 | tf_op jit(solution)/shard_map/dot_general | solution.py:23
  436.4 11.4 %backward_scan.1 = (bf16[1024,640]{1,0:T(8,128)(2,1)S(1)}, f32[1024,640]{1,0:T(8,128)S(1)}, f32[1024,640]{1,0:T(8,128)}, f32[8,1,640]{2,1,0:T(1,128)S(1)}) custom-call(f32[1024,640]{1,0:T(8,128)} %fusion.96.grad_ref, f32[1024,640]{1,0:T(8,128)} %get-tuple-element.112.y_ref, f32[1024,640]{1,0:T(8,128)} %get-tuple-element.64.local_ref, ...), custom_call_target="tpu_custom_call" | custom-call | flops 1000 | bytes 1000 | tf_op jit(solution)/shard_map/backward_scan/pallas_call | solution.py:203
  460.6 15.3 %all-gather.2 = f32[64,1,640]{2,0,1:T(8,128)S(1)} all-gather(f32[8,1,640]{2,0,1:T(8,128)S(1)} %copy.128), channel_id=4, replica_groups=mesh['seq'=4,'wide'=8] {'wide'}, dimensions={0}, use_global_device_ids=true | all-gather | bytes 184320 | tf_op jit(solution)/shard_map/all_gather | solution.py:792
  484.3 15.3 %backward_rows.1 = (bf16[1024,768]{1,0:T(8,128)(2,1)S(1)}, bf16[1024,768]{1,0:T(8,128)(2,1)}, bf16[1024,768]{1,0:T(8,128)(2,1)}, f32[8,640]{1,0:T(8,128)S(1)}) custom-call(s32[1]{0:T(128)} %bitcast.off_ref, f32[1024,640]{1,0:T(8,128)} %copy-done.4, f32[1024,640]{1,0:T(8,128)} %get-tuple-element.81.later_ref, f32[1024,640]{1,0:T(8,128)} %get-tuple-element.64.local_ref, ...), custom_call_target="tpu_custom_call" | custom-call | flops 1000 | bytes 1000 | tf_op jit(solution)/shard_map/backward_rows/pallas_call | solution.py:301
  521.4 5.8 convolution_convert_fusion.2
  536.4 45.5 %inputs_back.1 = (f32[256,2048]{1,0:T(8,128)}, f32[8,2048]{1,0:T(8,128)}) custom-call(bf16[1024,768]{1,0:T(8,128)(2,1)} %copy-done.5, bf16[1024,640]{1,0:T(8,128)(2,1)} %copy-done.11, bf16[2048,1408]{1,0:T(8,128)(2,1)} %all-gather.8.cloned.1.call-done.weight_ref, bf16[256,2048]{1,0:T(8,128)(2,1)} %bitcast.509, f32[1,2048]{1,0:T(1,128)} %bitcast.563, ...), custom_call_target="tpu_custom_call" | custom-call | flops 1000 | bytes 1000 | tf_op jit(solution)/shard_map/inputs_back/pallas_call | solution.py:481
  582.0 43.2 %result_of.1 = (bf16[256,2048]{1,0:T(8,128)(2,1)}, f32[3,8,2048]{2,1,0:T(8,128)}) custom-call(bf16[1024,1536]{1,0:T(8,128)(2,1)} %copy-done.15, bf16[1536,2048]{1,0:T(8,128)(2,1)} %all-gather.14.cloned.1.call-done.weight_ref, f32[256,2048]{1,0:T(8,128)} %get-tuple-element.91.stream_ref, f32[256,2048]{1,0:T(8,128)} %get-tuple-element.92.temporal_ref, ...), custom_call_target="tpu_custom_call" | custom-call | flops 1000 | bytes 1000 | tf_op jit(solution)/shard_map/result_of/pallas_call | solution.py:481
  627.3 13.9 %all_to_all.9 = f32[8,1,3076]{2,1,0:T(1,128)S(1)} all-to-all(f32[8,1,3076]{2,1,0:T(1,128)S(1)} %copy.141), channel_id=1, replica_groups=mesh['seq'=4,'wide'=8] {'wide'}, dimensions={0} | all-to-all | bytes 196864 | tf_op jit(solution)/shard_map/all_to_all | solution.py:914
  657.8 18.5 %collective-permute-done.30 = bf16[1856,128]{1,0:T(8,128)(2,1)S(1)} collective-permute-done((bf16[1856,128]{1,0:T(8,128)(2,1)S(1)}, bf16[1856,128]{1,0:T(8,128)(2,1)S(1)}, u32[]{:S(2)}, u32[]{:S(2)}) %collective-permute-start.30) | collective-permute-done | bytes 475168 | tf_op jit(solution)/shard_map/ppermute | solution.py:31
  677.9 20.0 %collective-permute-done.31 = bf16[1856,128]{1,0:T(8,128)(2,1)} collective-permute-done((bf16[1856,128]{1,0:T(8,128)(2,1)S(1)}, bf16[1856,128]{1,0:T(8,128)(2,1)}, u32[]{:S(2)}, u32[]{:S(2)}) %collective-permute-start.31) | collective-permute-done | bytes 475168 | tf_op jit(solution)/shard_map/ppermute | solution.py:31
  (390 shorter events, 178.6 us)
Async XLA Ops:
  7.2 93.3 %all-gather.10.cloned.1.call-start = ((), (), s32[]{:S(2)}) async-start(), calls=%async_computation.6 | async-start | bytes 2949120 | tf_op jit(solution)/shard_map/all_gather | solution.py:713
  9.2 99.6 %all-gather.8.cloned.1.call-start = ((), (), s32[]{:S(2)}) async-start(), calls=%async_computation.5 | async-start | bytes 6488064 | tf_op jit(solution)/shard_map/all_gather | solution.py:684
  11.5 259.6 %all-gather.12.cloned.1.call-start = ((), (), s32[]{:S(2)}) async-start(), calls=%async_computation.7 | async-start | bytes 14155776 | tf_op jit(solution)/shard_map/all_gather | solution.py:716
  12.9 291.7 %all-gather.14.cloned.1.call-start = ((), (), s32[]{:S(2)}) async-start(), calls=%async_computation.8 | async-start | bytes 7077888 | tf_op jit(solution)/shard_map/all_gather | solution.py:719
  13.0 27.0 %collective-permute-start = (bf16[256,2048]{1,0:T(8,128)(2,1)S(1)}, bf16[256,2048]{1,0:T(8,128)(2,1)}, u32[]{:S(2)}, u32[]{:S(2)}) collective-permute-start(bf16[256,2048]{1,0:T(8,128)(2,1)S(1)} %bitcast.510), channel_id=1, source_target_pairs={{0,8},{8,0},{16,24},{24,16},{1,9},{9,1},{17,25},{25,17},{2,10},{10... | collective-permute-start | bytes 3145736 | tf_op jit(solution)/shard_map/ppermute | solution.py:31
  16.0 48.0 %collective-permute-start.1 = (bf16[256,2048]{1,0:T(8,128)(2,1)S(1)}, bf16[256,2048]{1,0:T(8,128)(2,1)S(1)}, u32[]{:S(2)}, u32[]{:S(2)}) collective-permute-start(bf16[256,2048]{1,0:T(8,128)(2,1)S(1)} %bitcast.511), channel_id=1, source_target_pairs={{0,16},{8,24},{16,0},{24,8},{1,17},{9,25},{17,1},{25,9},{2,18},{10... | collective-permute-start | bytes 3145736 | tf_op jit(solution)/shard_map/ppermute | solution.py:31
  19.5 409.4 %reduce-scatter.5.cloned.1.call-start = ((), (), s32[]{:S(2)}) async-start(), calls=%async_computation.9 | async-start | bytes 7077888 | tf_op jit(solution)/shard_map/reduce_scatter | solution.py:772
  21.0 68.1 %collective-permute-start.5 = (bf16[16,2048]{1,0:T(8,128)(2,1)}, bf16[16,2048]{1,0:T(8,128)(2,1)}, u32[]{:S(2)}, u32[]{:S(2)}) collective-permute-start(bf16[16,2048]{1,0:T(8,128)(2,1)} %collective-permute-done.4), channel_id=1, source_target_pairs={{0,8},{8,0},{16,24},{24,16},{1,9},{9,1},{17,25},{25,17},{2,10},{10... | collective-permute-start | bytes 196616 | tf_op jit(solution)/shard_map/ppermute | solution.py:31
  103.4 37.3 %collective-permute-start.11 = (bf16[640,512]{1,0:T(8,128)(2,1)}, bf16[640,512]{1,0:T(8,128)(2,1)S(1)}, u32[]{:S(2)}, u32[]{:S(2)}) collective-permute-start(bf16[640,512]{1,0:T(8,128)(2,1)} %get-tuple-element.133), channel_id=1, source_target_pairs={{0,24},{8,16},{16,8},{24,0},{1,25},{9,17},{17,9},{25,1},{2,26},{10... | collective-permute-start | bytes 1966088 | tf_op jit(solution)/shard_map/ppermute | solution.py:31
  104.8 36.0 %collective-permute-start.12 = (bf16[640,512]{1,0:T(8,128)(2,1)}, bf16[640,512]{1,0:T(8,128)(2,1)}, u32[]{:S(2)}, u32[]{:S(2)}) collective-permute-start(bf16[640,512]{1,0:T(8,128)(2,1)} %get-tuple-element.132), channel_id=1, source_target_pairs={{0,16},{8,24},{16,0},{24,8},{1,17},{9,25},{17,1},{25,9},{2,18},{10... | collective-permute-start | bytes 1966088 | tf_op jit(solution)/shard_map/ppermute | solution.py:31
  106.4 35.2 %collective-permute-start.13 = (bf16[640,512]{1,0:T(8,128)(2,1)}, bf16[640,512]{1,0:T(8,128)(2,1)}, u32[]{:S(2)}, u32[]{:S(2)}) collective-permute-start(bf16[640,512]{1,0:T(8,128)(2,1)} %get-tuple-element.131), channel_id=1, source_target_pairs={{0,8},{8,0},{16,24},{24,16},{1,9},{9,1},{17,25},{25,17},{2,10},{10... | collective-permute-start | bytes 1966088 | tf_op jit(solution)/shard_map/ppermute | solution.py:31
  139.2 116.4 %collective-permute-start.15 = (bf16[256,2048]{1,0:T(8,128)(2,1)S(1)}, bf16[256,2048]{1,0:T(8,128)(2,1)}, u32[]{:S(2)}, u32[]{:S(2)}) collective-permute-start(bf16[256,2048]{1,0:T(8,128)(2,1)S(1)} %bitcast.522), channel_id=1, source_target_pairs={{0,16},{8,24},{16,0},{24,8},{1,17},{9,25},{17,1},{25,9},{2,18},{10... | collective-permute-start | bytes 3145736 | tf_op jit(solution)/shard_map/ppermute | solution.py:31
  165.2 97.8 %collective-permute-start.16 = (bf16[128,2048]{1,0:T(8,128)(2,1)}, bf16[128,2048]{1,0:T(8,128)(2,1)S(1)}, u32[]{:S(2)}, u32[]{:S(2)}) collective-permute-start(bf16[128,2048]{1,0:T(8,128)(2,1)} %slice.697), channel_id=1, source_target_pairs={{0,16},{8,24},{16,0},{24,8},{1,17},{9,25},{17,1},{25,9},{2,18},{10... | collective-permute-start | bytes 1572872 | tf_op jit(solution)/shard_map/ppermute | solution.py:31
  304.2 203.5 %reduce-scatter.7.cloned.1.call-start = ((), (), s32[]{:S(2)}) async-start(), calls=%async_computation.10 | async-start | bytes 14155776 | tf_op jit(solution)/shard_map/reduce_scatter | solution.py:779
  344.8 237.1 %reduce-scatter.9.cloned.1.call-start = ((), (), s32[]{:S(2)}) async-start(), calls=%async_computation.11 | async-start | bytes 5898240 | tf_op jit(solution)/shard_map/reduce_scatter | solution.py:874
  449.2 35.1 %collective-permute-start.21 = (f32[2,8,8,640]{3,2,1,0:T(8,128)S(1)}, f32[2,8,8,640]{3,2,1,0:T(8,128)S(1)}, u32[]{:S(2)}, u32[]{:S(2)}) collective-permute-start(f32[2,8,8,640]{3,2,1,0:T(8,128)S(1)} %pad_maximum_fusion.6), channel_id=1, source_target_pairs={{1,0},{2,1},{3,2},{4,3},{5,4},{6,5},{7,6},{9,8},{10,9},{11,10},{12... | collective-permute-start | bytes 983048 | tf_op jit(solution)/shard_map/ppermute | solution.py:799
  457.1 42.4 %collective-permute-start.18 = (bf16[640,512]{1,0:T(8,128)(2,1)}, bf16[640,512]{1,0:T(8,128)(2,1)S(1)}, u32[]{:S(2)}, u32[]{:S(2)}) collective-permute-start(bf16[640,512]{1,0:T(8,128)(2,1)} %get-tuple-element.130), channel_id=1, source_target_pairs={{0,24},{8,16},{16,8},{24,0},{1,25},{9,17},{17,9},{25,1},{2,26},{10... | collective-permute-start | bytes 1966088 | tf_op jit(solution)/shard_map/ppermute | solution.py:31
  458.4 41.1 %collective-permute-start.19 = (bf16[640,512]{1,0:T(8,128)(2,1)S(1)}, bf16[640,512]{1,0:T(8,128)(2,1)S(1)}, u32[]{:S(2)}, u32[]{:S(2)}) collective-permute-start(bf16[640,512]{1,0:T(8,128)(2,1)S(1)} %get-tuple-element.129), channel_id=1, source_target_pairs={{0,16},{8,24},{16,0},{24,8},{1,17},{9,25},{17,1},{25,9},{2,18},{10... | collective-permute-start | bytes 1966088 | tf_op jit(solution)/shard_map/ppermute | solution.py:31
  459.8 39.7 %collective-permute-start.20 = (bf16[640,512]{1,0:T(8,128)(2,1)S(1)}, bf16[640,512]{1,0:T(8,128)(2,1)S(1)}, u32[]{:S(2)}, u32[]{:S(2)}) collective-permute-start(bf16[640,512]{1,0:T(8,128)(2,1)S(1)} %get-tuple-element.128), channel_id=1, source_target_pairs={{0,8},{8,0},{16,24},{24,16},{1,9},{9,1},{17,25},{25,17},{2,10},{10... | collective-permute-start | bytes 1966088 | tf_op jit(solution)/shard_map/ppermute | solution.py:31
  507.8 117.5 %reduce-scatter.11.cloned.1.call-start = ((), (), s32[]{:S(2)}) async-start(), calls=%async_computation.12 | async-start | bytes 4276224 | tf_op jit(solution)/shard_map/reduce_scatter | solution.py:878
  647.5 55.3 %collective-permute-start.27 = (bf16[2560,128]{1,0:T(8,128)(2,1)S(1)}, bf16[2560,128]{1,0:T(8,128)(2,1)S(1)}, u32[]{:S(2)}, u32[]{:S(2)}) collective-permute-start(bf16[2560,128]{1,0:T(8,128)(2,1)S(1)} %bitcast.551), channel_id=1, source_target_pairs={{0,24},{8,16},{16,8},{24,0},{1,25},{9,17},{17,9},{25,1},{2,26},{10... | collective-permute-start | bytes 1966088 | tf_op jit(solution)/shard_map/ppermute | solution.py:31
  649.0 53.8 %collective-permute-start.28 = (bf16[2560,128]{1,0:T(8,128)(2,1)S(1)}, bf16[2560,128]{1,0:T(8,128)(2,1)S(1)}, u32[]{:S(2)}, u32[]{:S(2)}) collective-permute-start(bf16[2560,128]{1,0:T(8,128)(2,1)S(1)} %bitcast.552), channel_id=1, source_target_pairs={{0,16},{8,24},{16,0},{24,8},{1,17},{9,25},{17,1},{25,9},{2,18},{10... | collective-permute-start | bytes 1966088 | tf_op jit(solution)/shard_map/ppermute | solution.py:31
  652.1 45.8 %collective-permute-start.31 = (bf16[1856,128]{1,0:T(8,128)(2,1)S(1)}, bf16[1856,128]{1,0:T(8,128)(2,1)}, u32[]{:S(2)}, u32[]{:S(2)}) collective-permute-start(bf16[1856,128]{1,0:T(8,128)(2,1)S(1)} %bitcast.555), channel_id=1, source_target_pairs={{0,16},{8,24},{16,0},{24,8},{1,17},{9,25},{17,1},{25,9},{2,18},{10... | collective-permute-start | bytes 1425416 | tf_op jit(solution)/shard_map/ppermute | solution.py:31
  652.5 45.4 %collective-permute-start.32 = (bf16[1856,128]{1,0:T(8,128)(2,1)S(1)}, bf16[1856,128]{1,0:T(8,128)(2,1)}, u32[]{:S(2)}, u32[]{:S(2)}) collective-permute-start(bf16[1856,128]{1,0:T(8,128)(2,1)S(1)} %bitcast.556), channel_id=1, source_target_pairs={{0,8},{8,0},{16,24},{24,16},{1,9},{9,1},{17,25},{25,17},{2,10},{10... | collective-permute-start | bytes 1425416 | tf_op jit(solution)/shard_map/ppermute | solution.py:31
  (71 other events, 926.0 us)
Sparse Core Ops, SparseCore 0:
  10.3 36.8 all-gather.9
  49.3 59.4 all-gather.7
  111.0 117.9 all-gather.11
  230.5 63.3 all-gather.13
  304.3 68.7 reduce-scatter.4
  375.3 132.4 reduce-scatter.6
  510.0 58.0 reduce-scatter.8
  570.4 44.6 reduce-scatter.10

commit v3 on v2

--- a/solution.py
+++ b/solution.py
@@ -1,3 +1,5 @@
+import functools
+
 import jax
 import jax.numpy as jnp
 from jax import lax
@@ -29,15 +31,6 @@
 
 def swap(values, mask):
     return lax.ppermute(values, "seq", [(i, i ^ mask) for i in range(lax.axis_size("seq"))])
-
-
-def gather_seq(values):
-    half = values.shape[0] // 2
-    near = swap(values, 1)
-    side = swap(values, 2)
-    first = swap(near[:half], 2)
-    second = swap(side[half:], 1)
-    return [values, near, side, jnp.concatenate([first, second], axis=0)]
 
 
 def inverse_rms(values):
@@ -175,147 +168,6 @@
     )(off, x_win, edge, gates, chan)
 
 
-def backward_scan_kernel(
-    grad_ref, y_ref, local_ref, reach_ref, carry_ref, rate_ref,
-    y_rows_out, adjoint_out, later_out, heads_out,
-):
-    tokens, share = grad_ref.shape
-    row = lax.broadcasted_iota(jnp.int32, (tokens, LANES), 0)
-    for j in range(share // LANES):
-        lanes = slice(j * LANES, (j + 1) * LANES)
-        grad = grad_ref[:, lanes]
-        value, slope = gelu_parts(y_ref[:, lanes])
-        state = (local_ref[:, lanes] + reach_ref[:, lanes] * carry_ref[0, :, lanes]).astype(BF)
-        y_rows_out[:, lanes] = (grad * state.astype(F32) * slope).astype(BF)
-        state_grad = (grad * value).astype(BF).astype(F32)
-        rate = rate_ref[:, lanes]
-        ahead = jnp.where(row == tokens - 1, 1.0, pltpu.roll(rate, tokens - 1, 0))
-        adjoint, later = scan_rows(ahead, state_grad, True)
-        adjoint_out[:, lanes] = adjoint
-        later_out[:, lanes] = later
-        heads_out[0, :, lanes] = rate[:1] * adjoint[:1]
-
-
-def backward_scan(grad, y, local, reach, carry, rate, tokens):
-    total, share = grad.shape
-    seqs = total // tokens
-    part = pl.BlockSpec((tokens, share), lambda q: (q, 0))
-    return pl.pallas_call(
-        backward_scan_kernel,
-        grid=(seqs,),
-        in_specs=[part, part, part, part, per_seq(share), part],
-        out_specs=[part, part, part, per_seq(share)],
-        out_shape=[
-            jax.ShapeDtypeStruct((total, share), BF),
-            jax.ShapeDtypeStruct((total, share), F32),
-            jax.ShapeDtypeStruct((total, share), F32),
-            jax.ShapeDtypeStruct((seqs, 1, share), F32),
-        ],
-        compiler_params=pltpu.CompilerParams(vmem_limit_bytes=48 * 1024 * 1024),
-        cost_estimate=pl.CostEstimate(flops=1000, bytes_accessed=1000, transcendentals=0),
-        name="backward_scan",
-    )(grad, y, local, reach, carry[:, None, :], rate)
-
-
-def backward_rows_kernel(
-    off_ref, adjoint_ref, later_ref, local_ref, reach_ref, rate_ref, conv_ref,
-    forget_ref, admit_ref, x_ref, edge_ref, gates_ref, chan_ref, carry_ref, tail_ref, after_ref,
-    branch_out, forget_out, admit_out, sums_out,
-    conv_rows,
-):
-    q = pl.program_id(0)
-    tokens = adjoint_ref.shape[0]
-    share = chan_ref.shape[1]
-    window = x_ref.shape[1]
-    off = pl.multiple_of(off_ref[0], LANES)
-    forget_out[...] = jnp.zeros_like(forget_out)
-    admit_out[...] = jnp.zeros_like(admit_out)
-    conv_rows[...] = jnp.zeros_like(conv_rows)
-
-    @pl.when(q == 0)
-    def _():
-        sums_out[...] = jnp.zeros_like(sums_out)
-
-    row = lax.broadcasted_iota(jnp.int32, (tokens, LANES), 0)
-    for j in range(share // LANES):
-        lanes = slice(j * LANES, (j + 1) * LANES)
-        here = pl.ds(pl.multiple_of(off + j * LANES, LANES), LANES)
-        chan = [chan_ref[i : i + 1, lanes] for i in range(8)]
-        reach = reach_ref[:, lanes]
-        carry = carry_ref[0, :, lanes]
-        carried = local_ref[:, lanes] + reach * carry
-        before = jnp.where(row == 0, carry, pltpu.roll(carried, 1, 0))
-        adjoint = adjoint_ref[:, lanes] + later_ref[:, lanes] * tail_ref[0, :, lanes]
-        forget_sig = sigmoid(forget_ref[:, lanes].astype(F32))
-        admit_sig = sigmoid(admit_ref[:, lanes].astype(F32))
-        span = 0.1 + 0.9 * forget_sig
-        rate_log = -8.0 * chan[2] * span
-        rate = rate_ref[:, lanes]
-        scale = jnp.sqrt(drop_of(rate_log))
-        conv = conv_ref[:, lanes]
-        gated = admit_sig * conv
-        log_grad = adjoint * (rate * before - rate * rate / scale * gated)
-        conv_grad = adjoint * scale * admit_sig
-        forget_rows = (
-            log_grad * (-7.2) * chan[2] * forget_sig * (1.0 - forget_sig)
-        ).astype(BF)
-        admit_rows = (adjoint * scale * gated * (1.0 - admit_sig)).astype(BF)
-        forget_out[:, here] = forget_rows
-        admit_out[:, here] = admit_rows
-        after = after_ref[pl.ds(pl.multiple_of(q * HALO, HALO), HALO), lanes]
-        ahead = jnp.concatenate([conv_grad, after], axis=0)
-        back = chan[4] * conv_grad
-        for k in range(1, CONV):
-            back = back + chan[4 + k] * pltpu.roll(ahead, tokens + HALO - k, 0)[:tokens]
-        conv_rows[:, here] = back.astype(BF).astype(F32)
-        edge = edge_ref[pl.ds(pl.multiple_of(q * HALO, HALO), HALO), here]
-        padded = jnp.concatenate([edge, x_ref[:, here].astype(F32)], axis=0)
-        sums = [
-            forget_rows.astype(F32),
-            admit_rows.astype(F32),
-            log_grad * (-8.0) * span,
-            conv_grad,
-            conv_grad * padded[HALO:],
-        ] + [conv_grad * pltpu.roll(padded, k, 0)[HALO:] for k in range(1, CONV)]
-        sums_out[:, lanes] += jnp.concatenate(
-            [jnp.sum(v, axis=0, keepdims=True) for v in sums], axis=0
-        )
-    for b in range(window // BW):
-        cols = slice(b * BW, (b + 1) * BW)
-        back = conv_rows[:, cols]
-        for source, at in ((forget_out, 0), (admit_out, BW)):
-            back = back + lax.dot_general(
-                source[:, cols],
-                gates_ref[cols, at : at + BW],
-                (((1,), (1,)), ((), ())),
-                preferred_element_type=F32,
-            )
-        branch_out[:, cols] = back.astype(BF)
-
-
-def backward_rows(off, adjoint, later, local, reach, rate, conv, forget, admit, x_win, edge, gates, chan, carry, tail, after, tokens):
-    total, window = x_win.shape
-    share = chan.shape[1]
-    seqs = total // tokens
-    part = lambda width: pl.BlockSpec((tokens, width), lambda q: (q, 0))
-    return pl.pallas_call(
-        backward_rows_kernel,
-        grid=(seqs,),
-        in_specs=[pl.BlockSpec(memory_space=pltpu.SMEM)]
-        + [part(share)] * 8
-        + [part(window)]
-        + [whole(v.shape) for v in (edge, gates, chan)]
-        + [per_seq(share), per_seq(share), whole(after.shape)],
-        out_specs=[part(window), part(window), part(window), whole((8, share))],
-        out_shape=[jax.ShapeDtypeStruct((total, window), BF)] * 3
-        + [jax.ShapeDtypeStruct((8, share), F32)],
-        scratch_shapes=[pltpu.VMEM((tokens, window), F32)],
-        compiler_params=pltpu.CompilerParams(vmem_limit_bytes=48 * 1024 * 1024),
-        cost_estimate=pl.CostEstimate(flops=1000, bytes_accessed=1000, transcendentals=0),
-        name="backward_rows",
-    )(off, adjoint, later, local, reach, rate, conv, forget, admit, x_win, edge, gates, chan, carry[:, None, :], tail[:, None, :], after)
-
-
 def partner(mask):
     s = lax.axis_index("seq")
     if mask == 1:
@@ -399,26 +251,45 @@
     return [far_near, far_side] + arriving
 
 
-def gather_phase(send, first_slot, out):
+def both_ways(send, slot, source, out):
+    half = source.shape[0] // 2
+    low, high = pl.ds(0, half), pl.ds(half, half)
+    return [
+        send(slot, source.at[low], out.at[1, low], 1),
+        send(slot + 1, source.at[high], out.at[2, high], 2),
+        send(slot + 2, source.at[high], out.at[1, high], 1),
+        send(slot + 3, source.at[low], out.at[2, low], 2),
+    ]
+
+
+def pass_on(send, slot, out, copies):
     half = out.shape[1] // 2
     low, high = pl.ds(0, half), pl.ds(half, half)
-    near_low = send(first_slot, out.at[0, low], out.at[1, low], 1)
-    side_high = send(first_slot + 1, out.at[0, high], out.at[2, high], 2)
-    near_high = send(first_slot + 2, out.at[0, high], out.at[1, high], 1)
-    side_low = send(first_slot + 3, out.at[0, low], out.at[2, low], 2)
-    near_low.wait_recv()
-    far_low = send(first_slot + 4, out.at[1, low], out.at[3, low], 2)
-    side_high.wait_recv()
-    far_high = send(first_slot + 5, out.at[2, high], out.at[3, high], 1)
-    for copy in (near_high, side_low, far_low, far_high):
+    copies[0].wait_recv()
+    far_low = send(slot + 4, out.at[1, low], out.at[3, low], 2)
+    copies[1].wait_recv()
+    far_high = send(slot + 5, out.at[2, high], out.at[3, high], 1)
+    return copies + [far_low, far_high]
+
+
+def settle(copies):
+    for copy in copies[2:]:
         copy.wait_recv()
-    return [near_low, side_high, near_high, side_low, far_low, far_high]
-
-
-def product_of(left, right, contract, rows, tile):
+    for copy in copies:
+        copy.wait_send()
+
+
+def at_seq(k):
+    s = lax.axis_index("seq")
+    return s if k == 0 else 3 - s if k == 3 else partner(k)["seq"]
+
+
+def product_of(left, right, contract, rows, tile, ready=None):
     def product(k, store):
         def step(c, carry):
             cols = pl.ds(pl.multiple_of(c * tile, tile), tile)
+            if ready is not None and k == 3:
+                ready(c)
             total = None
             for a, b in zip(left, right):
                 part = b[cols, :] if contract else b[:, cols]
@@ -462,7 +333,8 @@
         normed_out[0, r] = (stream * rms_parts(stream) * gain_ref[...]).astype(BF)
 
     over_chunks(rows, finish)
-    copies += gather_phase(send, 6, normed_out)
+    gathered = pass_on(send, 6, normed_out, both_ways(send, 6, normed_out.at[0], normed_out))
+    settle(gathered)
     for copy in copies:
         copy.wait_send()
 
@@ -477,10 +349,11 @@
     ]
 
 
-def remote_call(kernel, name, ident, outs, operands, scratch):
+def remote_call(kernel, name, ident, outs, operands, scratch, far=0):
     return pl.pallas_call(
         kernel,
-        in_specs=[pl.BlockSpec(memory_space=pltpu.VMEM)] * len(operands),
+        in_specs=[pl.BlockSpec(memory_space=pltpu.VMEM)] * (len(operands) - far)
+        + [pl.BlockSpec(memory_space=pl.ANY)] * far,
         out_specs=[pl.BlockSpec(memory_space=pltpu.VMEM)] * len(outs),
         out_shape=[jax.ShapeDtypeStruct(shape, kind) for shape, kind in outs],
         scratch_shapes=scratch,
@@ -506,16 +379,33 @@
 
 
 def stream_back_kernel(
-    rows_ref, weight_ref, stream_ref, gain_ref, upstream_ref,
-    grad_out, low_out, gain_out,
+    rows_ref, stream_ref, gain_ref, upstream_ref, weight_far, hidden_far, down_far,
+    grad_out, low_out, gain_out, feed_out,
+    weight_ref, hidden_ref, down_ref, fetches,
     acc, sent, got, sends, recvs,
 ):
     rows, width = stream_ref.shape
+    tile = 512
+
+    def fetch(c):
+        part = pl.ds(pl.multiple_of(c * tile, tile), tile)
+        return pltpu.make_async_copy(weight_far.at[part], weight_ref.at[part], fetches.at[c])
+
+    count = width // tile
+    for c in range(count):
+        fetch(c).start()
+    late = [
+        pltpu.make_async_copy(hidden_far, hidden_ref, fetches.at[count]),
+        pltpu.make_async_copy(down_far, down_ref, fetches.at[count + 1]),
+    ]
+    for copy in late:
+        copy.start()
     greet()
     send = sender(sends, recvs)
-    copies = reduce_phase(
-        product_of([rows_ref], [weight_ref], True, rows, 512), send, 0, acc, sent, got
-    )
+    product = product_of(
+        [rows_ref], [weight_ref], True, rows, tile, ready=lambda c: fetch(c).wait()
+    )
+    copies = reduce_phase(product, send, 0, acc, sent, got)
     gain_out[...] = jnp.zeros_like(gain_out)
 
     def finish(r):
@@ -531,26 +421,50 @@
         gain_out[...] += gained[:8] + gained[8:]
 
     over_chunks(rows, finish)
-    copies += gather_phase(send, 6, low_out)
+    gathered = both_ways(send, 6, low_out.at[0], low_out)
+    for copy in late:
+        copy.wait()
+    feed = product_of([hidden_ref], [down_ref], False, rows, tile)
+
+    def feed_block(k):
+        feed(k, lambda cols, value: feed_out.__setitem__((k, slice(None), cols), value.astype(BF)))
+
+    feed_block(3)
+    gathered = pass_on(send, 6, low_out, gathered)
+    for k in range(3):
+        feed_block(k)
+    settle(gathered)
     for copy in copies:
         copy.wait_send()
 
 
-def stream_back(rows_all, weight, stream, gain, upstream):
+def stream_back(rows_all, weight, stream, gain, upstream, hidden, down):
     rows, width = stream.shape
     groups = rows_all.shape[0] // rows
     return remote_call(
         stream_back_kernel,
         "stream_back",
         2,
-        [((rows, width), F32), ((groups, rows, width), BF), ((8, width), F32)],
-        (rows_all, weight, stream, gain, upstream),
-        exchange_scratch(rows, width, 12),
+        [
+            ((rows, width), F32),
+            ((groups, rows, width), BF),
+            ((8, width), F32),
+            ((groups, rows, width), BF),
+        ],
+        (rows_all, stream, gain, upstream, weight, hidden, down),
+        [
+            pltpu.VMEM(weight.shape, BF),
+            pltpu.VMEM(hidden.shape, BF),
+            pltpu.VMEM(down.shape, BF),
+            pltpu.SemaphoreType.DMA((width // 512 + 2,)),
+        ]
+        + exchange_scratch(rows, width, 12),
+        far=3,
     )
 
 
 def inputs_back_kernel(
-    branch_ref, y_ref, weight_ref, flat_ref, gain_ref, stream_grad_ref,
+    branch_ref, y_ref, weight_ref, flat_ref, gain_ref,
     grad_out, gain_out,
     acc, sent, got, sends, recvs,
 ):
@@ -570,7 +484,7 @@
         inv = rms_parts(values)
         scaled = grad * gain_ref[...]
         inner = jnp.mean(values * scaled, axis=-1, keepdims=True)
-        grad_out[r] = stream_grad_ref[r] + inv * scaled - values * (inv * inv * inv * inner)
+        grad_out[r] = inv * scaled - values * (inv * inv * inv * inner)
         gained = grad * values * inv
         gain_out[...] += gained[:8] + gained[8:]
 
@@ -579,54 +493,490 @@
         copy.wait_send()
 
 
-def inputs_back(branch_rows, y_rows, weight, flat, gain, stream_grad):
+def inputs_back(branch_rows, y_rows, weight, flat, gain):
     rows, width = flat.shape
     return remote_call(
         inputs_back_kernel,
         "inputs_back",
         3,
         [((rows, width), F32), ((8, width), F32)],
-        (branch_rows, y_rows, weight, flat, gain, stream_grad),
+        (branch_rows, y_rows, weight, flat, gain),
         exchange_scratch(rows, width, 6),
     )
 
 
-def result_kernel(
-    hidden_ref, weight_ref, stream_ref, temporal_ref, valid_ref,
-    result_out, sums_out,
-    acc, sent, got, sends, recvs,
+def start_kernel(inputs_ref, inputs_out, edge_out, sends, recvs):
+    seqs = edge_out.shape[1] // ROWS16
+    tokens = inputs_ref.shape[0] // seqs
+    w = lax.axis_index("wide")
+    wide = lax.axis_size("wide")
+    after, before = lax.rem(w + 1, wide), lax.rem(w + wide - 1, wide)
+    barrier = pltpu.get_barrier_semaphore()
+    for mask in (1, 2):
+        pl.semaphore_signal(barrier, inc=1, device_id=partner(mask), device_id_type=MESH)
+    pl.semaphore_signal(barrier, inc=1, device_id={"wide": before}, device_id_type=MESH)
+    pl.semaphore_wait(barrier, 3)
+    send = sender(sends, recvs)
+    edges = []
+    for q in range(seqs):
+        copy = pltpu.make_async_remote_copy(
+            src_ref=inputs_ref.at[pl.ds((q + 1) * tokens - ROWS16, ROWS16)],
+            dst_ref=edge_out.at[0, pl.ds(q * ROWS16, ROWS16)],
+            send_sem=sends.at[12 + q],
+            recv_sem=recvs.at[12 + q],
+            device_id={"wide": after},
+            device_id_type=MESH,
+        )
+        copy.start()
+        edges.append(copy)
+    blocks = both_ways(send, 0, inputs_ref, inputs_out)
+    inputs_out[0] = inputs_ref[...]
+    for copy in edges:
+        copy.wait_recv()
+        copy.wait_send()
+    edges = both_ways(send, 6, edge_out.at[0], edge_out)
+    blocks = pass_on(send, 0, inputs_out, blocks)
+    edges = pass_on(send, 6, edge_out, edges)
+    settle(blocks)
+    settle(edges)
+
+
+def start(inputs, groups, seqs):
+    rows, width = inputs.shape
+    copies = 12 + seqs
+    return remote_call(
+        start_kernel,
+        "start",
+        6,
+        [((groups, rows, width), BF), ((groups, seqs * ROWS16, width), BF)],
+        (inputs,),
+        [pltpu.SemaphoreType.DMA((copies,)), pltpu.SemaphoreType.DMA((copies,))],
+    )
+
+
+def middle_kernel(
+    grad_ref, y_ref, local_ref, reach_ref, carry_ref, rate_ref, chan_ref, ends_ref,
+    edge_ref, gates_ref, valid_ref, feed_ref,
+    conv_far, forget_far, admit_far, x_far, stream_far, temporal_far,
+    y_rows_out, branch_out, forget_out, admit_out, sums_out, result_out, squares_out,
+    adjoint, later, heads, packet, packet_in, tails, after, conv_rows,
+    conv_ref, forget_ref, admit_ref, x_ref, stream_ref, temporal_ref,
+    sent, got, fetches, sends, recvs, head_sends, head_recvs,
 ):
-    rows = stream_ref.shape[0]
-    greet()
+    wide, seqs, share = ends_ref.shape
+    tokens = grad_ref.shape[0] // seqs
+    window = x_ref.shape[1]
+    rows, width = stream_ref.shape
+    half = rows // 2
+    low, high = pl.ds(0, half), pl.ds(half, half)
+    w = lax.axis_index("wide")
+    first_channel = lax.axis_index("seq") * share
+    base = jnp.minimum(first_channel // BW * BW, lax.axis_size("seq") * share - window)
+    off = pl.multiple_of(first_channel - base, LANES)
+    fetched = []
+    for i, (far, near) in enumerate(
+        (
+            (conv_far, conv_ref),
+            (forget_far, forget_ref),
+            (admit_far, admit_ref),
+            (x_far, x_ref),
+            (stream_far, stream_ref),
+            (temporal_far, temporal_ref),
+        )
+    ):
+        copy = pltpu.make_async_copy(far, near, fetches.at[i])
+        copy.start()
+        fetched.append(copy)
+
+    barrier = pltpu.get_barrier_semaphore()
+    for mask in (1, 2):
+        pl.semaphore_signal(barrier, inc=1, device_id=partner(mask), device_id_type=MESH)
+
+    def tell(i, carry):
+        other = lax.rem(w + i, wide)
+        pl.semaphore_signal(barrier, inc=1, device_id={"wide": other}, device_id_type=MESH)
+        return carry
+
+    lax.fori_loop(1, wide, tell, 0)
+    pl.semaphore_wait(barrier, wide + 1)
     send = sender(sends, recvs)
-    copies = reduce_phase(
-        product_of([hidden_ref], [weight_ref], False, rows, 512), send, 0, acc, sent, got
-    )
+    far_near = send(0, feed_ref.at[3, low], got.at[0, low], 1)
+    far_side = send(1, feed_ref.at[3, high], got.at[0, high], 2)
+    near_low = send(2, feed_ref.at[1, low], got.at[1, low], 1)
+    side_high = send(3, feed_ref.at[2, high], got.at[2, high], 2)
+
+    row = lax.broadcasted_iota(jnp.int32, (tokens, LANES), 0)
+    fetched[1].wait()
+    fetched[2].wait()
+
+    def scan_step(q, carry):
+        r = pl.ds(pl.multiple_of(q * tokens, tokens), tokens)
+        head_rows = pl.ds(pl.multiple_of(q * tokens, tokens), ROWS16)
+        for j in range(share // LANES):
+            lanes = slice(j * LANES, (j + 1) * LANES)
+            grad = grad_ref[r, lanes]
+            value, slope = gelu_parts(y_ref[r, lanes])
+            state = (local_ref[r, lanes] + reach_ref[r, lanes] * carry_ref[q, :, lanes]).astype(BF)
+            y_rows_out[r, lanes] = (grad * state.astype(F32) * slope).astype(BF)
+            state_grad = (grad * value).astype(BF).astype(F32)
+            rate = rate_ref[r, lanes]
+            ahead = jnp.where(row == tokens - 1, 1.0, pltpu.roll(rate, tokens - 1, 0))
+            adjoints, laters = scan_rows(ahead, state_grad, True)
+            adjoint[r, lanes] = adjoints
+            later[r, lanes] = laters
+            tails[q, :, lanes] = rate[:1] * adjoints[:1]
+            forget_sig = sigmoid(forget_ref[head_rows, lanes].astype(F32)[:HALO])
+            admit_sig = sigmoid(admit_ref[head_rows, lanes].astype(F32)[:HALO])
+            rate_log = -8.0 * chan_ref[2:3, lanes] * (0.1 + 0.9 * forget_sig)
+            gain = jnp.sqrt(drop_of(rate_log)) * admit_sig
+            for i, values in enumerate((adjoints[:HALO] * gain, laters[:HALO] * gain)):
+                for t in range(CONV - 1):
+                    packet[i, t, q, :, lanes] = values[t : t + 1]
+        return carry
+
+    lax.fori_loop(0, seqs, scan_step, 0)
+    for q in range(seqs):
+        heads[0, q : q + 1, :] = tails[q]
+
+    def head_copy(i):
+        return pltpu.make_async_remote_copy(
+            src_ref=heads.at[0],
+            dst_ref=heads.at[i],
+            send_sem=head_sends.at[i],
+            recv_sem=head_recvs.at[i],
+            device_id={"wide": lax.rem(w + i, wide)},
+            device_id_type=MESH,
+        )
+
+    def head_start(i, carry):
+        head_copy(i).start()
+        return carry
+
+    def head_wait(i, carry):
+        copy = head_copy(i)
+        copy.wait_recv()
+        copy.wait_send()
+        return carry
+
+    lax.fori_loop(1, wide, head_start, 0)
+    packets = pltpu.make_async_remote_copy(
+        src_ref=packet,
+        dst_ref=packet_in,
+        send_sem=sends.at[6],
+        recv_sem=recvs.at[6],
+        device_id={"wide": lax.rem(w + wide - 1, wide)},
+        device_id_type=MESH,
+    )
+    packets.start()
+
+    far_side.wait_recv()
+    sent[0] = (feed_ref[1, high].astype(F32) + got[0, high].astype(F32)).astype(BF)
+    near_high = send(4, sent.at[0], got.at[1, high], 1)
+    far_near.wait_recv()
+    sent[1] = (feed_ref[2, low].astype(F32) + got[0, low].astype(F32)).astype(BF)
+    side_low = send(5, sent.at[1], got.at[2, low], 2)
+
+    lax.fori_loop(1, wide, head_wait, 0)
+    packets.wait_recv()
+    packets.wait_send()
+
+    def tail_step(i, carry):
+        tail, next_tail = carry
+        j = wide - i
+        stepped = ends_ref[j] * tail + heads[lax.rem(w + i, wide)]
+        return jnp.where(j > w, stepped, tail), jnp.where(j > w + 1, stepped, next_tail)
+
+    zero = jnp.zeros((seqs, share), F32)
+    tail, next_tail = lax.fori_loop(1, wide, tail_step, (zero, zero))
+    next_tail = jnp.where(w == wide - 1, 0.0, next_tail)
+    inside = jnp.where(w == wide - 1, 0.0, 1.0)
+    after[...] = jnp.zeros_like(after)
+    for q in range(seqs):
+        tails[q] = tail[q : q + 1]
+        for t in range(CONV - 1):
+            after[q * HALO + t : q * HALO + t + 1, :] = (
+                inside * packet_in[0, t, q] + packet_in[1, t, q] * next_tail[q : q + 1]
+            )
+
+    forget_out[...] = jnp.zeros_like(forget_out)
+    admit_out[...] = jnp.zeros_like(admit_out)
+    conv_rows[...] = jnp.zeros_like(conv_rows)
     sums_out[...] = jnp.zeros_like(sums_out)
+    fetched[0].wait()
+    fetched[3].wait()
+
+    def rows_step(q, carry):
+        r = pl.ds(pl.multiple_of(q * tokens, tokens), tokens)
+        pack = pl.ds(pl.multiple_of(q * HALO, HALO), HALO)
+        for j in range(share // LANES):
+            lanes = slice(j * LANES, (j + 1) * LANES)
+            here = pl.ds(pl.multiple_of(off + j * LANES, LANES), LANES)
+            chan = [chan_ref[i : i + 1, lanes] for i in range(8)]
+            start = carry_ref[q, :, lanes]
+            carried = local_ref[r, lanes] + reach_ref[r, lanes] * start
+            before = jnp.where(row == 0, start, pltpu.roll(carried, 1, 0))
+            full = adjoint[r, lanes] + later[r, lanes] * tails[q, :, lanes]
+            forget_sig = sigmoid(forget_ref[r, lanes].astype(F32))
+            admit_sig = sigmoid(admit_ref[r, lanes].astype(F32))
+            span = 0.1 + 0.9 * forget_sig
+            rate = rate_ref[r, lanes]
+            scale = jnp.sqrt(drop_of(-8.0 * chan[2] * span))
+            gated = admit_sig * conv_ref[r, lanes]
+            log_grad = full * (rate * before - rate * rate / scale * gated)
+            conv_grad = full * scale * admit_sig
+            forget_rows = (
+                log_grad * (-7.2) * chan[2] * forget_sig * (1.0 - forget_sig)
+            ).astype(BF)
+            admit_rows = (full * scale * gated * (1.0 - admit_sig)).astype(BF)
+            forget_out[r, here] = forget_rows
+            admit_out[r, here] = admit_rows
+            ahead = jnp.concatenate([conv_grad, after[pack, lanes]], axis=0)
+            back = chan[4] * conv_grad
+            for k in range(1, CONV):
+                back = back + chan[4 + k] * pltpu.roll(ahead, tokens + HALO - k, 0)[:tokens]
+            conv_rows[:, here] = back.astype(BF).astype(F32)
+            padded = jnp.concatenate(
+                [edge_ref[pack, here], x_ref[r, here].astype(F32)], axis=0
+            )
+            sums = [
+                forget_rows.astype(F32),
+                admit_rows.astype(F32),
+                log_grad * (-8.0) * span,
+                conv_grad,
+                conv_grad * padded[HALO:],
+            ] + [conv_grad * pltpu.roll(padded, k, 0)[HALO:] for k in range(1, CONV)]
+            sums_out[:, lanes] += jnp.concatenate(
+                [jnp.sum(v, axis=0, keepdims=True) for v in sums], axis=0
+            )
+        for b in range(window // BW):
+            cols = slice(b * BW, (b + 1) * BW)
+            back = conv_rows[:, cols]
+            for source, at in ((forget_out, 0), (admit_out, BW)):
+                back = back + lax.dot_general(
+                    source[r, cols],
+                    gates_ref[cols, at : at + BW],
+                    (((1,), (1,)), ((), ())),
+                    preferred_element_type=F32,
+                )
+            branch_out[r, cols] = back.astype(BF)
+        return carry
+
+    lax.fori_loop(0, seqs, rows_step, 0)
+    fetched[4].wait()
+    fetched[5].wait()
+    for copy in (near_low, side_high, near_high, side_low):
+        copy.wait_recv()
+    squares_out[...] = jnp.zeros_like(squares_out)
 
     def finish(r):
-        feed = acc[0, r] + got[1, r].astype(F32) + got[2, r].astype(F32)
+        feed = feed_ref[0, r].astype(F32) + got[1, r].astype(F32) + got[2, r].astype(F32)
         result = stream_ref[r] + feed
-        result_out[r] = result.astype(BF)
+        result_out[r] = result
         valid = valid_ref[r]
         for i, values in enumerate((result, temporal_ref[r], feed)):
             square = valid * values * values
-            sums_out[i] += square[:8] + square[8:]
+            squares_out[i] += square[:8] + square[8:]
 
     over_chunks(rows, finish)
-    for copy in copies:
+    for copy in (far_near, far_side, near_low, side_high, near_high, side_low):
         copy.wait_send()
 
 
-def result_of(hidden, weight, stream, temporal, valid):
+def middle(
+    grad, y, local, reach, carry, rate, chan, ends, edge, gates, valid, feed,
+    conv, forget, admit, x_win, stream, temporal,
+):
+    total, share = grad.shape
+    window = x_win.shape[1]
     rows, width = stream.shape
+    wide, seqs = ends.shape[:2]
+    tokens = total // seqs
+    vmem = pl.BlockSpec(memory_space=pltpu.VMEM)
+    anywhere = pl.BlockSpec(memory_space=pl.ANY)
+    outs = [
+        ((total, share), BF),
+        ((total, window), BF),
+        ((total, window), BF),
+        ((total, window), BF),
+        ((8, share), F32),
+        ((rows, width), F32),
+        ((3, 8, width), F32),
+    ]
+    return pl.pallas_call(
+        middle_kernel,
+        in_specs=[vmem] * 12 + [anywhere] * 6,
+        out_specs=[vmem] * len(outs),
+        out_shape=[jax.ShapeDtypeStruct(shape, kind) for shape, kind in outs],
+        scratch_shapes=[
+            pltpu.VMEM((total, share), F32),
+            pltpu.VMEM((total, share), F32),
+            pltpu.VMEM((wide, seqs, share), F32),
+            pltpu.VMEM((2, CONV - 1, seqs, 1, share), F32),
+            pltpu.VMEM((2, CONV - 1, seqs, 1, share), F32),
+            pltpu.VMEM((seqs, 1, share), F32),
+            pltpu.VMEM((seqs * HALO, share), F32),
+            pltpu.VMEM((tokens, window), F32),
+            pltpu.VMEM((total, share), F32),
+            pltpu.VMEM((total, share), BF),
+            pltpu.VMEM((total, share), BF),
+            pltpu.VMEM((total, window), BF),
+            pltpu.VMEM((rows, width), F32),
+            pltpu.VMEM((rows, width), F32),
+            pltpu.VMEM((2, rows // 2, width), BF),
+            pltpu.VMEM((3, rows, width), BF),
+            pltpu.SemaphoreType.DMA((6,)),
+            pltpu.SemaphoreType.DMA((7,)),
+            pltpu.SemaphoreType.DMA((7,)),
+            pltpu.SemaphoreType.DMA((wide,)),
+            pltpu.SemaphoreType.DMA((wide,)),
+        ],
+        compiler_params=pltpu.CompilerParams(
+            collective_id=7, has_side_effects=True, vmem_limit_bytes=60 * 1024 * 1024
+        ),
+        cost_estimate=pl.CostEstimate(flops=1000, bytes_accessed=1000, transcendentals=0),
+        name="middle",
+    )(
+        grad, y, local, reach, carry[:, None, :], rate, chan, ends, edge, gates, valid, feed,
+        conv, forget, admit, x_win, stream, temporal,
+    )
+
+
+def place(k, block, buffer, plan, outs):
+    buffer[...] = block[...].astype(F32)
+    other = at_seq(k)
+    for (first, count, tiles, starts), out in zip(plan, outs):
+        base = other * 0
+        for j, start_col in enumerate(starts):
+            base = jnp.where(other == j, start_col, base)
+        for i in range(tiles):
+            cols = pl.ds(pl.multiple_of(base + i * LANES, LANES), LANES)
+            out[:, cols] += buffer[first + i * count : first + (i + 1) * count, :]
+
+
+def spread_kernel(first_ref, second_ref, first_out, second_out, first_blocks, second_blocks, sends, recvs):
+    greet()
+    send = sender(sends, recvs)
+    first = both_ways(send, 0, first_ref, first_blocks)
+    second = both_ways(send, 6, second_ref, second_blocks)
+
+    def put(k, block, out):
+        columns = block.shape[1]
+        other = at_seq(k)
+        for i in range(columns // LANES):
+            start_col = pl.multiple_of(other * columns + i * LANES, LANES)
+            out[:, pl.ds(start_col, LANES)] = block[:, i * LANES : (i + 1) * LANES]
+
+    put(0, first_ref, first_out)
+    put(0, second_ref, second_out)
+    first = pass_on(send, 0, first_blocks, first)
+    second = pass_on(send, 6, second_blocks, second)
+    settle(first)
+    for k in (1, 2, 3):
+        put(k, first_blocks.at[k], first_out)
+    settle(second)
+    for k in (1, 2, 3):
+        put(k, second_blocks.at[k], second_out)
+
+
+def spread(first, second, groups):
+    counts = [first.shape[0], second.shape[0]]
+    first, second = (jnp.pad(v, ((0, -v.shape[0] % 32), (0, 0))) for v in (first, second))
+    wholes = remote_call(
+        spread_kernel,
+        "spread",
+        8,
+        [((v.shape[0], groups * v.shape[1]), BF) for v in (first, second)],
+        (first, second),
+        [
+            pltpu.VMEM((groups,) + first.shape, BF),
+            pltpu.VMEM((groups,) + second.shape, BF),
+            pltpu.SemaphoreType.DMA((12,)),
+            pltpu.SemaphoreType.DMA((12,)),
+        ],
+    )
+    return [v[:count] for v, count in zip(wholes, counts)]
+
+
+def last_kernel(
+    plan, parts_ref, sums_ref,
+    first_out, second_out, sums_out,
+    blocks, buffer, total, got_sums, sends, recvs, sum_sends, sum_recvs,
+):
+    wide = sums_ref.shape[0]
+    w = lax.axis_index("wide")
+    barrier = pltpu.get_barrier_semaphore()
+    for mask in (1, 2):
+        pl.semaphore_signal(barrier, inc=1, device_id=partner(mask), device_id_type=MESH)
+
+    def tell(i, carry):
+        other = lax.rem(w + i, wide)
+        pl.semaphore_signal(barrier, inc=1, device_id={"wide": other}, device_id_type=MESH)
+        return carry
+
+    lax.fori_loop(1, wide, tell, 0)
+    pl.semaphore_wait(barrier, wide + 1)
+    send = sender(sends, recvs)
+    copies = both_ways(send, 0, parts_ref, blocks)
+
+    def chunk(i):
+        other = lax.rem(w + i, wide)
+        return pltpu.make_async_remote_copy(
+            src_ref=sums_ref.at[other],
+            dst_ref=got_sums.at[i],
+            send_sem=sum_sends.at[i],
+            recv_sem=sum_recvs.at[i],
+            device_id={"wide": other},
+            device_id_type=MESH,
+        )
+
+    def begin(i, carry):
+        chunk(i).start()
+        return carry
+
+    def finish(i, carry):
+        copy = chunk(i)
+        copy.wait_recv()
+        copy.wait_send()
+        return carry + got_sums[i]
+
+    lax.fori_loop(1, wide, begin, 0)
+    outs = (first_out, second_out)
+    for out in outs:
+        out[...] = jnp.zeros_like(out)
+    place(0, parts_ref, buffer, plan, outs)
+    total[0] = lax.fori_loop(1, wide, finish, sums_ref[w])
+    to_near = send(6, total.at[0], total.at[1], 1)
+    copies = pass_on(send, 0, blocks, copies)
+    to_near.wait_recv()
+    total[2] = total[0] + total[1]
+    to_side = send(7, total.at[2], total.at[3], 2)
+    settle(copies)
+    for k in (1, 2, 3):
+        place(k, blocks.at[k], buffer, plan, outs)
+    to_side.wait_recv()
+    sums_out[...] = total[2] + total[3]
+    to_near.wait_send()
+    to_side.wait_send()
+
+
+def spread_last(parts, sums, plan, shapes):
+    wide, count, _unused = sums.shape
     return remote_call(
-        result_kernel,
-        "result_of",
-        4,
-        [((rows, width), BF), ((3, 8, width), F32)],
-        (hidden, weight, stream, temporal, valid),
-        exchange_scratch(rows, width, 6),
+        functools.partial(last_kernel, plan),
+        "spread_last",
+        5,
+        [(shape, F32) for shape in shapes] + [((count, LANES), F32)],
+        (parts, sums),
+        [
+            pltpu.VMEM((4,) + parts.shape, BF),
+            pltpu.VMEM(parts.shape, F32),
+            pltpu.VMEM((4, count, LANES), F32),
+            pltpu.VMEM((wide, count, LANES), F32),
+            pltpu.SemaphoreType.DMA((8,)),
+            pltpu.SemaphoreType.DMA((8,)),
+            pltpu.SemaphoreType.DMA((wide,)),
+            pltpu.SemaphoreType.DMA((wide,)),
+        ],
     )
 
 
@@ -673,13 +1023,9 @@
 
     flat_low = inputs.reshape(rows, width)
     upstream = cotangent.reshape(rows, width)
-    edge = lax.ppermute(
-        inputs[:, tokens - HALO :, :].reshape(seqs * HALO, width),
-        "wide",
-        [(i, i + 1) for i in range(wide - 1)],
-    )
-    token_blocks = gather_seq(flat_low)
-    edge_blocks = [swap(edge, k) if k else edge for k in range(groups)]
+    all_low, edge_low = start(flat_low, groups, seqs)
+    all_low = all_low.reshape(total, width)
+    edge_low = jnp.where(w == 0, 0.0, edge_low.reshape(all_seqs * ROWS16, width).astype(F32))
 
     x_y_cols = lax.all_gather(
         jnp.concatenate(
@@ -701,7 +1047,9 @@
     small = jnp.concatenate(
         [lax.dynamic_slice_in_dim(gates_quarter, s * gate_cols, gate_cols, 1), small], axis=0
     )
-    small, token_blocks[1] = lax.optimization_barrier((small, token_blocks[1]))
+    small, edge_low, later_upstream = lax.optimization_barrier((small, edge_low, upstream))
+    upstream_near = swap(later_upstream, 1)
+    upstream_side = swap(later_upstream, 2)
     small = lax.all_gather(small, "wide")
     gates_quarter = small[:, :rw].reshape(channels, gate_cols)
     small = small[:, rw:].reshape(wide, -1).astype(F32)
@@ -723,30 +1071,41 @@
         near = [jnp.where(s % 2 == 1, parts[k ^ 1], parts[k]) for k in range(groups)]
         return [jnp.where(s // 2 == 1, near[k ^ 2], near[k]) for k in range(groups)]
 
-    gate_parts, out_parts = [], []
-    for k in range(groups):
-        other = s ^ k
-        part = lax.dynamic_slice_in_dim(gates_quarter, base_of(other), window, 0)
-        gate_parts.append(swap(part, k) if k else part)
-        part = lax.dynamic_slice_in_dim(out_quarter, other * share, share, 0)
-        out_parts.append(swap(part, k) if k else part)
-    gates = jnp.concatenate(in_order(gate_parts), axis=1)
-    out_rows = jnp.concatenate(in_order(out_parts), axis=1)
-
-    all_low = jnp.concatenate(token_blocks + edge_blocks, axis=0)
-    normed_ext = rms_norm(all_low.astype(F32), gain_one).astype(BF)
-    normed_all = normed_ext[:total]
+    def swapped(part_of):
+        return [swap(part_of(s ^ k), k) if k else part_of(s) for k in range(groups)]
+
+    gates = jnp.concatenate(
+        in_order(
+            swapped(lambda j: lax.dynamic_slice_in_dim(gates_quarter, base_of(j), window, 0))
+        ),
+        axis=1,
+    )
+    normed_all = rms_norm(all_low.astype(F32), gain_one).astype(BF)
+    normed_edge = rms_norm(edge_low, gain_one).astype(BF)
+    normed_all, upstream_near, upstream_side = lax.optimization_barrier(
+        (normed_all, upstream_near, upstream_side)
+    )
+    half = rows // 2
+    upstream_far = [swap(upstream_near[:half], 2), swap(upstream_side[half:], 1)]
 
     x_y = dot(normed_all, x_y_cols)
     x_win = x_y[:, :window].astype(BF)
     branch_y = x_y[:, window:]
-    edge_win = dot(normed_ext[total:], x_y_cols[:, :window]).astype(BF).astype(F32)
+    x_win, out_quarter, *upstream_far = lax.optimization_barrier(
+        (x_win, out_quarter, *upstream_far)
+    )
+    upstream_all = jnp.concatenate([upstream, upstream_near, upstream_side, *upstream_far], axis=0)
+    out_rows = jnp.concatenate(
+        in_order(swapped(lambda j: lax.dynamic_slice_in_dim(out_quarter, j * share, share, 0))),
+        axis=1,
+    )
+    edge_win = dot(normed_edge, x_y_cols[:, :window]).astype(BF).astype(F32)
+    edge_win = edge_win.reshape(all_seqs, ROWS16, window)[:, ROWS16 - HALO :]
+    edge_win = edge_win.reshape(all_seqs * HALO, window)
     offset = off.reshape(1)
     forget, admit, conv_out, rate, local, reach, ends = temporal_forward(
         offset, x_win, edge_win, gates, per_channel, tokens
     )
-    ends, later_upstream = lax.optimization_barrier((ends, upstream))
-    upstream_all = jnp.concatenate(gather_seq(later_upstream), axis=0)
     ends = lax.all_gather(ends, "wide")[:, :, :, 0]
     carry = jnp.zeros((all_seqs, share), F32)
     for j in range(wide - 1):
@@ -777,41 +1136,26 @@
     mlp_part = contract_rows(normed_two_all, mlp_rows).astype(BF)
     mlp_rows, mlp_part = lax.optimization_barrier((mlp_rows, mlp_part))
     mlp_grad = lax.psum_scatter(mlp_part, "wide", scatter_dimension=0, tiled=True)
-    stream_grad, stream_low_all, gain_two_grad = stream_back(
-        mlp_rows, mlp_full, stream, gain_two, upstream
+    stream_grad, stream_low_all, gain_two_grad, feed_parts = stream_back(
+        mlp_rows, mlp_full, stream, gain_two, upstream, hidden_low, down_full
     )
     gain_two_grad = jnp.sum(gain_two_grad, axis=0)
     stream_low_all = stream_low_all.reshape(total, width)
     stream_low_all, down_grad = lax.optimization_barrier((stream_low_all, down_grad))
+    mixed_grad = contract_last(stream_low_all, out_rows)
+    out_grad = contract_rows(mixed_low, stream_low_all).astype(BF)
+    mixed_grad, out_grad = lax.optimization_barrier((mixed_grad, out_grad))
+    out_parts = swapped(lambda j: lax.dynamic_slice_in_dim(out_grad, j * quarter, quarter, 1))
     position = w * tokens + jnp.arange(tokens, dtype=jnp.int32)
     valid = (position[None, :] < lengths[:, None]).astype(F32).reshape(rows, 1)
-    mixed_grad = contract_last(stream_low_all, out_rows)
-    y_rows, adjoint, later, heads = backward_scan(
-        mixed_grad, branch_y, local, reach, carry, rate, tokens
-    )
-    heads = lax.all_gather(heads, "wide")[:, :, 0]
-
-    def firsts(values):
-        return values.reshape(all_seqs, tokens, share)[:, :HALO].astype(F32)
-
-    first_rate = -8.0 * per_channel[2] * (0.1 + 0.9 * jax.nn.sigmoid(firsts(forget)))
-    gain = jnp.sqrt(-jnp.expm1(2.0 * first_rate)) * jax.nn.sigmoid(firsts(admit))
-    after = lax.ppermute(
-        jnp.stack([firsts(adjoint) * gain, firsts(later) * gain]),
-        "wide",
-        [(i + 1, i) for i in range(wide - 1)],
-    )
-    tail = jnp.zeros((all_seqs, share), F32)
-    next_tail = tail
-    for j in range(wide - 1, 0, -1):
-        stepped = ends[j, :, 0] * tail + heads[j]
-        next_tail = jnp.where(j > w + 1, stepped, next_tail)
-        tail = jnp.where(j > w, stepped, tail)
-    after = (after[0] + after[1] * next_tail[:, None, :]).reshape(all_seqs * HALO, share)
-    branch_rows, forget_win, admit_win, channel_grads = backward_rows(
-        offset, adjoint, later, local, reach, rate, conv_out, forget, admit,
-        x_win, edge_win, gates, per_channel, carry, tail, after, tokens,
-    )
+    y_rows, branch_rows, forget_win, admit_win, channel_grads, result, squares = middle(
+        mixed_grad, branch_y, local, reach, carry, rate, per_channel, ends[:, :, 0],
+        edge_win, gates, valid, feed_parts, conv_out, forget, admit, x_win, stream, temporal,
+    )
+    y_rows, branch_rows, *out_parts = lax.optimization_barrier((y_rows, branch_rows, *out_parts))
+    out_cols = jnp.concatenate(in_order(out_parts), axis=0)
+    partial_sums = jnp.concatenate([jnp.sum(squares, axis=(1, 2)), jnp.sum(valid).reshape(1)])
+
     bases = [min(j * share // BW * BW, channels - window) for j in range(groups)]
 
     def placed(parts, axis):
@@ -823,9 +1167,6 @@
         ]
         return sum(jnp.pad(p.astype(F32), r) for p, r in zip(parts, rest))
 
-    def swapped(part_of):
-        return [swap(part_of(s ^ k), k) if k else part_of(s) for k in range(groups)]
-
     def stack(values):
         values = values.reshape(wide, values.shape[0] // wide, values.shape[1])
         tiles = values.shape[2] // LANES
@@ -833,18 +1174,6 @@
             [values[:, :, i * LANES : (i + 1) * LANES] for i in range(tiles)], axis=1
         )
 
-    def unstack(values, count, columns):
-        return jnp.concatenate(
-            [values[i * count : (i + 1) * count] for i in range(columns // LANES)], axis=1
-        )
-
-    out_grad = contract_rows(mixed_low, stream_low_all).astype(BF)
-    out_cols = jnp.concatenate(
-        in_order(
-            swapped(lambda j: lax.dynamic_slice_in_dim(out_grad, j * quarter, quarter, 1))
-        ),
-        axis=0,
-    )
     gelu_part = contract_rows(normed_all, y_rows).astype(BF)
 
     gate_grads = jnp.concatenate(
@@ -859,46 +1188,52 @@
         ],
         axis=1,
     ).astype(BF)
+    branch_part = contract_rows(normed_all, branch_rows).astype(BF)
+    def sum_over_wide(values):
+        return lax.psum_scatter(values, "wide", scatter_dimension=0, tiled=True)
+
+    out_cols, gelu_part = lax.optimization_barrier((out_cols, gelu_part))
     gate_cols_grad = placed(
         in_order(
             swapped(lambda j: lax.dynamic_slice_in_dim(gate_grads, j * gate_cols, gate_cols, 1))
         ),
         0,
     ).astype(BF)
-    branch_part = contract_rows(normed_all, branch_rows).astype(BF)
-    first_pieces = [(gelu_part, share), (out_cols, quarter)]
-    second_pieces = [(branch_part, window), (gate_cols_grad, gate_cols)]
-    first = jnp.concatenate([stack(values) for values, _unused in first_pieces], axis=1)
-    second = jnp.concatenate([stack(values) for values, _unused in second_pieces], axis=1)
-    first, mlp_grad, branch_late = lax.optimization_barrier((first, mlp_grad, branch_rows))
-    first = lax.psum_scatter(first, "wide", scatter_dimension=0, tiled=True)
-    inputs_grad, gain_one_grad = inputs_back(
-        branch_late, y_rows, x_y_cols, flat_low, gain_one, stream_grad
-    )
-    second = lax.psum_scatter(second, "wide", scatter_dimension=0, tiled=True)
-    first, gain_one_grad, stream_late = lax.optimization_barrier((first, gain_one_grad, stream))
-    output, square_sums = result_of(hidden_low, down_full, stream_late, temporal, valid)
-    second, square_sums = lax.optimization_barrier((second, square_sums))
-
-    def spread(summed, pieces):
-        parts = in_order(swapped(lambda j: summed[0]))
-        start, spread_pieces = 0, []
-        for values, columns in pieces:
+    out_sum = sum_over_wide(out_cols)
+    gelu_sum = sum_over_wide(gelu_part)
+    pieces = [(branch_part, window), (gate_cols_grad, gate_cols)]
+    stacked = jnp.concatenate([stack(values) for values, _unused in pieces], axis=1)
+    stacked = jnp.pad(stacked, ((0, 0), (0, -stacked.shape[1] % 32), (0, 0)))
+    stacked, mlp_grad = lax.optimization_barrier((stacked, mlp_grad))
+    first_back, gain_one_grad = inputs_back(
+        branch_rows, y_rows, x_y_cols, flat_low, gain_one
+    )
+    gelu_sum, gain_one_grad = lax.optimization_barrier((gelu_sum, gain_one_grad))
+    last_sum = sum_over_wide(stacked)
+
+    def plan_of(pieces, starts):
+        plan, at = [], 0
+        for (values, columns), cols in zip(pieces, starts):
             count = values.shape[0] // wide
-            size = count * columns // LANES
-            spread_pieces.append([unstack(p[start : start + size], count, columns) for p in parts])
-            start += size
-        return spread_pieces
-
-    gelu_parts_all, out_parts_all = spread(first, first_pieces)
-    branch_parts_all, gate_parts_all = spread(second, second_pieces)
-    gelu_whole = jnp.concatenate(gelu_parts_all, axis=1).astype(F32)
-    out_whole = jnp.concatenate(out_parts_all, axis=1).astype(F32)
-    branch_whole = placed(branch_parts_all, 1)
-    gates_whole = jnp.concatenate(gate_parts_all, axis=1).astype(F32)
-    partial_sums = jnp.concatenate([jnp.sum(square_sums, axis=(1, 2)), jnp.sum(valid).reshape(1)])
-    inputs_grad = inputs_grad.reshape(seqs, tokens, width)
-    output = output.reshape(seqs, tokens, width)
+            plan.append((at, count, columns // LANES, tuple(cols)))
+            at += count * columns // LANES
+        return tuple(plan)
+
+    out_whole, gelu_whole = spread(out_sum, gelu_sum, groups)
+    earlier = lax.optimization_barrier(
+        (
+            last_sum,
+            result.astype(BF).reshape(seqs, tokens, width),
+            (stream_grad + first_back).reshape(seqs, tokens, width),
+            gelu_whole.astype(F32),
+            out_whole.astype(F32),
+            mlp_grad[:, :hidden_units].astype(F32),
+            mlp_grad[:, hidden_units:].astype(F32),
+            down_grad.astype(F32),
+        )
+    )
+    last_sum, output, inputs_grad, gelu_whole, out_whole, gate_grad, up_grad, down_grad = earlier
+
     channel_all = lax.dynamic_update_slice_in_dim(
         jnp.zeros((8, channels), F32), channel_grads, s * share, 1
     )
@@ -911,12 +1246,18 @@
         ],
         axis=1,
     )
-    sums = jnp.sum(lax.all_to_all(sums, "wide", 0, 0), axis=0)
-    sums = sums + swap(sums, 1)
-    sums = sums + swap(sums, 2)
+    sums = jnp.pad(sums, ((0, 0), (0, -sums.shape[1] % (8 * LANES)))).reshape(wide, -1, LANES)
+    branch_whole, gates_whole, sums = spread_last(
+        last_sum[0],
+        sums,
+        plan_of(pieces, (bases, [j * gate_cols for j in range(groups)])),
+        ((dw, channels), (rw, 2 * BW)),
+    )
+    sums = sums.reshape(-1)
     channel_sums = sums[: 8 * rw].reshape(8, rw)
     gain_sums = sums[8 * rw : 8 * rw + 2 * dw].reshape(2, dw)
-    totals = sums[8 * rw + 2 * dw :]
+    totals = sums[8 * rw + 2 * dw : 8 * rw + 2 * dw + 4]
+
     statistics = jnp.sqrt(totals[0:3] / (totals[3] * width))
     return (
         output,
@@ -933,9 +1274,9 @@
         channel_sums[3],
         out_whole,
         gain_sums[1],
-        mlp_grad[:, :hidden_units].astype(F32),
-        mlp_grad[:, hidden_units:].astype(F32),
-        down_grad.astype(F32),
+        gate_grad,
+        up_grad,
+        down_grad,
         statistics,
     )
 

time: 727 us -> 690 us (0.949)
  Pallas kernels: 296 us -> 386 us
  waiting for transfers between devices: 81.6 us -> 12.5 us
  blocking collectives: 61.8 us -> 35.4 us
  starting transfers between devices: 43.7 us -> 19.6 us
  local copies, waits for them, and re-layouts: 71.6 us -> 57.1 us
    ppermute x31 -> x16, waiting for transfers between devices: 77.7 us -> 9.14 us  [swap(): lax.ppermute(values, 'seq', [(i, i ^ mask) for i in range(lax.axis_size('...]
    pallas_call x4 -> x6, Pallas kernels: 256 us -> 309 us  [remote_call(): pl.pallas_call(kernel, in_specs=[pl.BlockSpec(memory_space=pltpu.VMEM)] *...]
    pallas_call x2 -> x1, Pallas kernels: 26.6 us -> 64.5 us  [middle(): pl.pallas_call(middle_kernel, in_specs=[vmem] * 12 + [anywhere] * 6, out_...]
    ppermute x31 -> x16, starting transfers between devices: 39.3 us -> 18.7 us  [swap(): lax.ppermute(values, 'seq', [(i, i ^ mask) for i in range(lax.axis_size('...]
    unnamed x195 -> x109, local copies, waits for them, and re-layouts: 44.7 us -> 27.5 us
    all_gather x1 -> x0, blocking collectives: 15.3 us -> none  [body(): heads = lax.all_gather(heads, 'wide')[:, :, 0]]
    all_to_all x1 -> x0, blocking collectives: 13.9 us -> none  [body(): sums = jnp.sum(lax.all_to_all(sums, 'wide', 0, 0), axis=0)]
  transfers between devices with their start and end apart: 41 -> 25, of which waited for: 10 -> 5; matrix products, arithmetic and copies ran while one was open for 28% -> 28% of each run, Pallas kernels for 41% -> 53%
where the time goes in v3:
time: 690 us; the launch traced here: 681 us
  Pallas kernels  386 us (56%)
  matrix products  103 us (15%)
  local copies, waits for them, and re-layouts  57.1 us (8%)
  other arithmetic  51.6 us (7%)
  blocking collectives  35.4 us (5%)
  starting transfers between devices  19.6 us (3%)
  between operations  15.9 us (2%)
  waiting for transfers between devices  12.5 us (2%)
    pallas_call x6, Pallas kernels, remote_call(): pl.pallas_call(kernel, in_specs=[pl.BlockSpec(memory_space=pltpu.VMEM)] *...  309 us
    pallas_call x1, Pallas kernels, middle(): pl.pallas_call(middle_kernel, in_specs=[vmem] * 12 + [anywhere] * 6, out_...  64.5 us
    dot_general x5, matrix products, contract_rows(): lax.dot_general(left, right, (((0,), (0,)), ((), ())), preferred_element_...  46 us
    dot_general x3, matrix products, dot(): return jnp.dot(left, right, preferred_element_type=F32)  30.5 us
    unnamed x109, local copies, waits for them, and re-layouts  27.5 us
    dot_general x2, matrix products, contract_last(): lax.dot_general(left, right, (((1,), (1,)), ((), ())), preferred_element_...  22.2 us
    ppermute x16, starting transfers between devices, swap(): lax.ppermute(values, 'seq', [(i, i ^ mask) for i in range(lax.axis_size('...  18.7 us
    all_gather x1, blocking collectives, body(): ends = lax.all_gather(ends, 'wide')[:, :, :, 0]  17.9 us
  transfers between devices with their start and end apart: 25, of which 5 were waited for; matrix products, arithmetic and copies ran while one was open for 28% of the time, Pallas kernels for 53%

profile of v3, /device:TPU:0, one launch (start us, length us, event | category | flops | bytes accessed | tf_op | source)
XLA Modules:
  0.0 680.7 jit_solution(4604350643668165018)
XLA Ops:
  14.4 47.1 %start.1 = (bf16[4,256,2048]{2,1,0:T(8,128)(2,1)}, bf16[4,32,2048]{2,1,0:T(8,128)(2,1)}) custom-call(bf16[256,2048]{1,0:T(8,128)(2,1)} %bitcast.373), custom_call_target="tpu_custom_call" | custom-call | flops 1000 | bytes 1000 | tf_op jit(solution)/shard_map/start/pallas_call | solution.py:353
  65.1 17.4 %all-gather = bf16[2752,128]{1,0:T(8,128)(2,1)S(1)} all-gather(bf16[344,128]{1,0:T(8,128)(2,1)S(1)} %pad_maximum_fusion.6), channel_id=2, replica_groups=mesh['seq'=4,'wide'=8] {'wide'}, dimensions={0}, use_global_device_ids=true | all-gather | bytes 792576 | tf_op jit(solution)/shard_map/all_gather | solution.py:1053
  92.7 5.3 fusion.1
  112.2 10.4 %fusion.65 = f32[1024,1408]{1,0:T(8,128)S(1)} fusion(bf16[1024,2048]{1,0:T(8,128)(2,1)} %fusion.1, bf16[2048,1408]{1,0:T(8,128)(2,1)} %all-gather.7.cloned.1.call-done.weight_ref), kind=kOutput, calls=%fused_computation.209 | convolution fusion | flops 5905580032 | bytes 15728640 | tf_op jit(solution)/shard_map/dot_general | solution.py:21
  134.0 12.8 %temporal_forward.1 = (bf16[1024,640]{1,0:T(8,128)(2,1)S(1)}, bf16[1024,640]{1,0:T(8,128)(2,1)S(1)}, f32[1024,640]{1,0:T(8,128)}, f32[1024,640]{1,0:T(8,128)}, f...) custom-call(s32[1]{0:T(128)} %bitcast.6.off_ref, bf16[1024,768]{1,0:T(8,128)(2,1)S(1)} %slice.328.x_ref.x_far, ...), custom_call_target="tpu_custom_call" | custom-call | flops 1000 | bytes 1000 | tf_op jit(solution)/shard_map/temporal_forward/pallas_call | solution.py:139
  146.8 17.9 %all-gather.1 = f32[64,2,1,640]{3,1,2,0:T(2,128)S(1)} all-gather(f32[8,2,1,640]{3,1,2,0:T(2,128)S(1)} %copy.102), channel_id=3, replica_groups=mesh['seq'=4,'wide'=8] {'wide'}, dimensions={0}, use_global_device_ids=true | all-gather | bytes 368640 | tf_op jit(solution)/shard_map/all_gather | solution.py:1109
  164.8 6.4 fusion.63
  177.6 82.5 %stream_and_norm.1 = (f32[256,2048]{1,0:T(8,128)}, f32[256,2048]{1,0:T(8,128)}, bf16[4,256,2048]{2,1,0:T(8,128)(2,1)}) custom-call(bf16[1024,640]{1,0:T(8,128)(2,1)} %get-tuple-element.165.mixed_ref, bf16[640,2048]{1,0:T(8,128)(2,1)} %pad_maximum_fusion.1.weight_ref, bf16[256,2048]{1,0:T(8,128)(2,1)} %bitcast.374, f32[1,2048]{1,0:T(1,128)} %bitcast.412), custom_call_target="tpu_custom_call" | custom-call | flops 1000 | bytes 1000 | tf_op jit(solution)/shard_map/stream_and_norm/pallas_call | solution.py:353
  260.2 17.2 %fusion.66 = f32[1024,3072]{1,0:T(8,128)S(1)} fusion(bf16[1024,2048]{1,0:T(8,128)(2,1)} %bitcast.423, bf16[2048,3072]{1,0:T(8,128)(2,1)} %all-gather.11.cloned.1.call-done.weight_far), kind=kOutput, calls=%fused_computation.210 | convolution fusion | flops 12884901888 | bytes 29360128 | tf_op jit(solution)/shard_map/dot_general | solution.py:21
  283.6 10.9 %convolution_convert_fusion.1 = bf16[1536,2048]{1,0:T(8,128)(2,1)} fusion(bf16[1024,1536]{1,0:T(8,128)(2,1)S(1)} %multiply_convert_fusion.1.hidden_far, bf16[1024,2048]{1,0:T(8,128)(2,1)} %constant_dynamic-update-slice_fusion), kind=kOutput, calls=%fused_computation.8 | convolution fusion | flops 6445596672 | bytes 13631488 | tf_op jit(solution)/shard_map/dot_general | solution.py:29
  296.3 17.3 %fusion.17 = (bf16[1024,1536]{1,0:T(8,128)(2,1)S(1)}, bf16[1024,1536]{1,0:T(8,128)(2,1)S(1)}) fusion(f32[1024,3072]{1,0:T(8,128)} %copy-done.9, bf16[1024,2048]{1,0:T(8,128)(2,1)} %constant_dynamic-update-slice_fusion, bf16[1536,2048]{1,0:T(8,128)(2,1)} %all-gather.13.cloned.1.call-done.down_far), kind=kOutput, calls=%fused_computation.24 | convolution fusion | flops 6486491136 | bytes 29360128 | tf_op jit(solution)/shard_map/dot_general | solution.py:25
  317.0 18.9 %convolution_convert_fusion = bf16[2048,3072]{1,0:T(8,128)(2,1)} fusion(bf16[1024,2048]{1,0:T(8,128)(2,1)} %bitcast.424, bf16[1024,1536]{1,0:T(8,128)(2,1)S(1)} %get-tuple-element.163, bf16[1024,1536]{1,0:T(8,128)(2,1)S(1)} %get-tuple-element.162), kind=kOutput, calls=%fused_computation | convolution fusion | flops 12903776256 | bytes 23068672 | tf_op jit(solution)/shard_map/dot_general | solution.py:29
  336.2 88.6 %stream_back.1 = (f32[256,2048]{1,0:T(8,128)}, bf16[4,256,2048]{2,1,0:T(8,128)(2,1)}, f32[8,2048]{1,0:T(8,128)}, bf16[4,256,2048]{2,1,0:T(8,128)(2,1)}) custom-call(bf16[1024,3072]{1,0:T(8,128)(2,1)} %pad_maximum_fusion.rows_ref, f32[256,2048]{1,0:T(8,128)} %get-tuple-element.105.stream_ref.stream_far, f32[1,2048]{1,0:T(1,128)} %bitcast.413, ...), custom_call_target="tpu_custom_call" | custom-call | flops 1000 | bytes 1000 | tf_op jit(solution)/shard_map/stream_back/pallas_call | solution.py:353
  424.8 5.3 convolution_convert_fusion.4
  430.1 4.9 fusion.61.grad_ref
  441.2 64.5 %middle.1 = (bf16[1024,640]{1,0:T(8,128)(2,1)}, bf16[1024,768]{1,0:T(8,128)(2,1)}, bf16[1024,768]{1,0:T(8,128)(2,1)}, bf16[1024,768]{1,0:T(8,128)(2,1)}, f32[8,6...) custom-call(f32[1024,640]{1,0:T(8,128)} %fusion.61.grad_ref, f32[1024,640]{1,0:T(8,128)} %get-tuple-element.164.y_ref, ...), custom_call_target="tpu_custom_call" | custom-call | flops 1000 | bytes 1000 | tf_op jit(solution)/shard_map/middle/pallas_call | solution.py:805
  509.3 7.2 %convolution_convert_fusion.3 = bf16[2048,640]{1,0:T(8,128)(2,1)} fusion(bf16[1024,2048]{1,0:T(8,128)(2,1)} %fusion.1, bf16[1024,640]{1,0:T(8,128)(2,1)S(1)} %copy-done.27), kind=kOutput, calls=%fused_computation.30 | convolution fusion | flops 2685665280 | bytes 8126464 | tf_op jit(solution)/shard_map/dot_general | solution.py:29
  532.8 4.3 collective-permute-done.15
  537.0 3.5 collective-permute-done.13
  542.2 3.8 convolution_convert_fusion.2
  558.4 44.4 %inputs_back.1 = (f32[256,2048]{1,0:T(8,128)}, f32[8,2048]{1,0:T(8,128)}) custom-call(bf16[1024,768]{1,0:T(8,128)(2,1)} %get-tuple-element.120.branch_ref, bf16[1024,640]{1,0:T(8,128)(2,1)} %get-tuple-element.127.y_ref, bf16[2048,1408]{1,0:T(8,128)(2,1)} %all-gather.7.cloned.1.call-done.weight_ref, bf16[256,2048]{1,0:T(8,128)(2,1)} %bitcast.375, ...), custom_call_target="tpu_custom_call" | custom-call | flops 1000 | bytes 1000 | tf_op jit(solution)/shard_map/inputs_back/pallas_call | solution.py:353
  606.0 23.6 %spread.1 = (bf16[320,2048]{1,0:T(8,128)(2,1)}, bf16[256,2560]{1,0:T(8,128)(2,1)}) custom-call(bf16[320,512]{1,0:T(8,128)(2,1)} %reduce-scatter.12.cloned.1.call-done.first_ref, bf16[256,640]{1,0:T(8,128)(2,1)} %reduce-scatter.14.cloned.1.call-done.second_ref), custom_call_target="tpu_custom_call" | custom-call | flops 1000 | bytes 1000 | tf_op jit(solution)/shard_map/spread/pallas_call | solution.py:353
  638.8 22.4 %spread_last.1 = (f32[256,2560]{1,0:T(8,128)}, f32[320,512]{1,0:T(8,128)}, f32[32,128]{1,0:T(8,128)}) custom-call(bf16[1856,128]{1,0:T(8,128)(2,1)} %bitcast.407, f32[8,32,128]{2,1,0:T(8,128)} %bitcast.406), custom_call_target="tpu_custom_call" | custom-call | flops 1000 | bytes 1000 | tf_op jit(solution)/shard_map/spread_last/pallas_call | solution.py:353
  670.4 3.4 copy.166
  (250 shorter events, 124.9 us)
Async XLA Ops:
  7.2 105.0 %all-gather.7.cloned.1.call-start = ((), (), s32[]{:S(2)}) async-start(), calls=%async_computation.5 | async-start | bytes 6488064 | tf_op jit(solution)/shard_map/all_gather | solution.py:1030
  9.8 115.5 %all-gather.9.cloned.1.call-start = ((), (), s32[]{:S(2)}) async-start(), calls=%async_computation.6 | async-start | bytes 2949120 | tf_op jit(solution)/shard_map/all_gather | solution.py:1061
  11.8 248.5 %all-gather.11.cloned.1.call-start = ((), (), s32[]{:S(2)}) async-start(), calls=%async_computation.7 | async-start | bytes 14155776 | tf_op jit(solution)/shard_map/all_gather | solution.py:1064
  14.4 281.9 %all-gather.13.cloned.1.call-start = ((), (), s32[]{:S(2)}) async-start(), calls=%async_computation.8 | async-start | bytes 7077888 | tf_op jit(solution)/shard_map/all_gather | solution.py:1067
  63.0 38.0 %collective-permute-start.1 = (bf16[256,2048]{1,0:T(8,128)(2,1)S(1)}, bf16[256,2048]{1,0:T(8,128)(2,1)}, u32[]{:S(2)}, u32[]{:S(2)}) collective-permute-start(bf16[256,2048]{1,0:T(8,128)(2,1)S(1)} %bitcast.377), channel_id=1, source_target_pairs={{0,16},{8,24},{16,0},{24,8},{1,17},{9,25},{17,1},{25,9},{2,18},{10... | collective-permute-start | bytes 3145736 | tf_op jit(solution)/shard_map/ppermute | solution.py:33
  63.7 37.4 %collective-permute-start = (bf16[256,2048]{1,0:T(8,128)(2,1)S(1)}, bf16[256,2048]{1,0:T(8,128)(2,1)}, u32[]{:S(2)}, u32[]{:S(2)}) collective-permute-start(bf16[256,2048]{1,0:T(8,128)(2,1)S(1)} %bitcast.378), channel_id=1, source_target_pairs={{0,8},{8,0},{16,24},{24,16},{1,9},{9,1},{17,25},{25,17},{2,10},{10... | collective-permute-start | bytes 3145736 | tf_op jit(solution)/shard_map/ppermute | solution.py:33
  84.4 15.4 %collective-permute-start.6 = (bf16[768,128]{1,0:T(8,128)(2,1)}, bf16[768,128]{1,0:T(8,128)(2,1)S(1)}, u32[]{:S(2)}, u32[]{:S(2)}) collective-permute-start(bf16[768,128]{1,0:T(8,128)(2,1)} %get-tuple-element.195), channel_id=1, source_target_pairs={{0,8},{8,0},{16,24},{24,16},{1,9},{9,1},{17,25},{25,17},{2,10},{10... | collective-permute-start | bytes 589832 | tf_op jit(solution)/shard_map/ppermute | solution.py:33
  85.2 14.5 %collective-permute-start.5 = (bf16[768,128]{1,0:T(8,128)(2,1)}, bf16[768,128]{1,0:T(8,128)(2,1)S(1)}, u32[]{:S(2)}, u32[]{:S(2)}) collective-permute-start(bf16[768,128]{1,0:T(8,128)(2,1)} %get-tuple-element.196), channel_id=1, source_target_pairs={{0,16},{8,24},{16,0},{24,8},{1,17},{9,25},{17,1},{25,9},{2,18},{10... | collective-permute-start | bytes 589832 | tf_op jit(solution)/shard_map/ppermute | solution.py:33
  86.8 13.0 %collective-permute-start.4 = (bf16[768,128]{1,0:T(8,128)(2,1)}, bf16[768,128]{1,0:T(8,128)(2,1)}, u32[]{:S(2)}, u32[]{:S(2)}) collective-permute-start(bf16[768,128]{1,0:T(8,128)(2,1)} %get-tuple-element.197), channel_id=1, source_target_pairs={{0,24},{8,16},{16,8},{24,0},{1,25},{9,17},{17,9},{25,1},{2,26},{10... | collective-permute-start | bytes 589832 | tf_op jit(solution)/shard_map/ppermute | solution.py:33
  87.9 336.9 %reduce-scatter.6.cloned.1.call-start = ((), (), s32[]{:S(2)}) async-start(), calls=%async_computation.9 | async-start | bytes 7077888 | tf_op jit(solution)/shard_map/reduce_scatter | solution.py:1131
  107.5 17.8 %collective-permute-start.3 = (bf16[128,2048]{1,0:T(8,128)(2,1)}, bf16[128,2048]{1,0:T(8,128)(2,1)S(1)}, u32[]{:S(2)}, u32[]{:S(2)}) collective-permute-start(bf16[128,2048]{1,0:T(8,128)(2,1)} %slice.164), channel_id=1, source_target_pairs={{0,8},{8,0},{16,24},{24,16},{1,9},{9,1},{17,25},{25,17},{2,10},{10... | collective-permute-start | bytes 1572872 | tf_op jit(solution)/shard_map/ppermute | solution.py:33
  108.4 16.9 %collective-permute-start.2 = (bf16[128,2048]{1,0:T(8,128)(2,1)}, bf16[128,2048]{1,0:T(8,128)(2,1)}, u32[]{:S(2)}, u32[]{:S(2)}) collective-permute-start(bf16[128,2048]{1,0:T(8,128)(2,1)} %slice.163), channel_id=1, source_target_pairs={{0,16},{8,24},{16,0},{24,8},{1,17},{9,25},{17,1},{25,9},{2,18},{10... | collective-permute-start | bytes 1572872 | tf_op jit(solution)/shard_map/ppermute | solution.py:33
  127.5 46.5 %collective-permute-start.9 = (bf16[640,512]{1,0:T(8,128)(2,1)S(1)}, bf16[640,512]{1,0:T(8,128)(2,1)S(1)}, u32[]{:S(2)}, u32[]{:S(2)}) collective-permute-start(bf16[640,512]{1,0:T(8,128)(2,1)S(1)} %get-tuple-element.178), channel_id=1, source_target_pairs={{0,8},{8,0},{16,24},{24,16},{1,9},{9,1},{17,25},{25,17},{2,10},{10... | collective-permute-start | bytes 1966088 | tf_op jit(solution)/shard_map/ppermute | solution.py:33
  128.5 45.5 %collective-permute-start.8 = (bf16[640,512]{1,0:T(8,128)(2,1)S(1)}, bf16[640,512]{1,0:T(8,128)(2,1)S(1)}, u32[]{:S(2)}, u32[]{:S(2)}) collective-permute-start(bf16[640,512]{1,0:T(8,128)(2,1)S(1)} %get-tuple-element.179), channel_id=1, source_target_pairs={{0,16},{8,24},{16,0},{24,8},{1,17},{9,25},{17,1},{25,9},{2,18},{10... | collective-permute-start | bytes 1966088 | tf_op jit(solution)/shard_map/ppermute | solution.py:33
  129.7 44.3 %collective-permute-start.7 = (bf16[640,512]{1,0:T(8,128)(2,1)S(1)}, bf16[640,512]{1,0:T(8,128)(2,1)S(1)}, u32[]{:S(2)}, u32[]{:S(2)}) collective-permute-start(bf16[640,512]{1,0:T(8,128)(2,1)S(1)} %get-tuple-element.180), channel_id=1, source_target_pairs={{0,24},{8,16},{16,8},{24,0},{1,25},{9,17},{17,9},{25,1},{2,26},{10... | collective-permute-start | bytes 1966088 | tf_op jit(solution)/shard_map/ppermute | solution.py:33
  294.6 257.8 %reduce-scatter.8.cloned.1.call-start = ((), (), s32[]{:S(2)}) async-start(), calls=%async_computation.10 | async-start | bytes 14155776 | tf_op jit(solution)/shard_map/reduce_scatter | solution.py:1138
  335.9 270.1 %reduce-scatter.14.cloned.1.call-start = ((), (), s32[]{:S(2)}) async-start(), calls=%async_computation.13 | async-start | bytes 2949120 | tf_op jit(solution)/shard_map/reduce_scatter | solution.py:1193
  435.4 70.3 %collective-permute-start.12 = (bf16[640,512]{1,0:T(8,128)(2,1)S(1)}, bf16[640,512]{1,0:T(8,128)(2,1)}, u32[]{:S(2)}, u32[]{:S(2)}) collective-permute-start(bf16[640,512]{1,0:T(8,128)(2,1)S(1)} %get-tuple-element.174), channel_id=1, source_target_pairs={{0,24},{8,16},{16,8},{24,0},{1,25},{9,17},{17,9},{25,1},{2,26},{10... | collective-permute-start | bytes 1966088 | tf_op jit(solution)/shard_map/ppermute | solution.py:33
  437.1 68.6 %collective-permute-start.11 = (bf16[640,512]{1,0:T(8,128)(2,1)S(1)}, bf16[640,512]{1,0:T(8,128)(2,1)}, u32[]{:S(2)}, u32[]{:S(2)}) collective-permute-start(bf16[640,512]{1,0:T(8,128)(2,1)S(1)} %get-tuple-element.175), channel_id=1, source_target_pairs={{0,16},{8,24},{16,0},{24,8},{1,17},{9,25},{17,1},{25,9},{2,18},{10... | collective-permute-start | bytes 1966088 | tf_op jit(solution)/shard_map/ppermute | solution.py:33
  437.6 68.1 %collective-permute-start.10 = (bf16[640,512]{1,0:T(8,128)(2,1)S(1)}, bf16[640,512]{1,0:T(8,128)(2,1)}, u32[]{:S(2)}, u32[]{:S(2)}) collective-permute-start(bf16[640,512]{1,0:T(8,128)(2,1)S(1)} %get-tuple-element.176), channel_id=1, source_target_pairs={{0,8},{8,0},{16,24},{24,16},{1,9},{9,1},{17,25},{25,17},{2,10},{10... | collective-permute-start | bytes 1966088 | tf_op jit(solution)/shard_map/ppermute | solution.py:33
  516.5 89.5 %reduce-scatter.12.cloned.1.call-start = ((), (), s32[]{:S(2)}) async-start(), calls=%async_computation.12 | async-start | bytes 2949120 | tf_op jit(solution)/shard_map/reduce_scatter | solution.py:1193
  517.3 121.5 %reduce-scatter.10.cloned.1.call-start = ((), (), s32[]{:S(2)}) async-start(), calls=%async_computation.11 | async-start | bytes 4276224 | tf_op jit(solution)/shard_map/reduce_scatter | solution.py:1193
  530.0 10.5 %collective-permute-start.13 = (bf16[768,128]{1,0:T(8,128)(2,1)S(1)}, bf16[768,128]{1,0:T(8,128)(2,1)S(1)}, u32[]{:S(2)}, u32[]{:S(2)}) collective-permute-start(bf16[768,128]{1,0:T(8,128)(2,1)S(1)} %get-tuple-element.191), channel_id=1, source_target_pairs={{0,24},{8,16},{16,8},{24,0},{1,25},{9,17},{17,9},{25,1},{2,26},{10... | collective-permute-start | bytes 589832 | tf_op jit(solution)/shard_map/ppermute | solution.py:33
  531.4 10.5 %collective-permute-start.14 = (bf16[768,128]{1,0:T(8,128)(2,1)S(1)}, bf16[768,128]{1,0:T(8,128)(2,1)S(1)}, u32[]{:S(2)}, u32[]{:S(2)}) collective-permute-start(bf16[768,128]{1,0:T(8,128)(2,1)S(1)} %get-tuple-element.192), channel_id=1, source_target_pairs={{0,16},{8,24},{16,0},{24,8},{1,17},{9,25},{17,1},{25,9},{2,18},{10... | collective-permute-start | bytes 589832 | tf_op jit(solution)/shard_map/ppermute | solution.py:33
  (46 other events, 1191.8 us)
Sparse Core Ops, SparseCore 0:
  10.3 65.2 all-gather.6
  77.8 33.0 all-gather.8
  113.1 118.3 all-gather.10
  232.8 63.3 all-gather.12
  298.4 67.9 reduce-scatter.5
  368.6 131.4 reduce-scatter.7
  516.7 34.9 reduce-scatter.13
  554.5 36.3 reduce-scatter.11
  593.2 45.5 reduce-scatter.9

commit v4 on v3

--- a/solution.py
+++ b/solution.py
@@ -464,18 +464,46 @@
 
 
 def inputs_back_kernel(
-    branch_ref, y_ref, weight_ref, flat_ref, gain_ref,
-    grad_out, gain_out,
+    branch_ref, y_ref, weight_ref, flat_ref, gain_ref, columns_ref,
+    grad_out, gain_out, columns_out,
     acc, sent, got, sends, recvs,
 ):
-    rows, width = flat_ref.shape
-    greet()
+    rows = flat_ref.shape[0]
+    s = lax.axis_index("seq")
+    count, columns = columns_ref.shape[0], columns_out.shape[1]
+    barrier = pltpu.get_barrier_semaphore()
+    for k in (1, 2, 3):
+        pl.semaphore_signal(barrier, inc=1, device_id={"seq": at_seq(k)}, device_id_type=MESH)
+    pl.semaphore_wait(barrier, 3)
     send = sender(sends, recvs)
+    here = pl.ds(pl.multiple_of(s * count, ROWS16), count)
+
+    def columns_of(k):
+        return columns_ref.at[:, pl.ds(pl.multiple_of(at_seq(k) * columns, LANES), columns)]
+
+    moved = []
+    for k in (3, 1, 2):
+        copy = pltpu.make_async_remote_copy(
+            src_ref=columns_of(k),
+            dst_ref=columns_out.at[here],
+            send_sem=sends.at[5 + k],
+            recv_sem=recvs.at[5 + k],
+            device_id={"seq": at_seq(k)},
+            device_id_type=MESH,
+        )
+        moved.append(copy)
     window = branch_ref.shape[1]
     weights = [weight_ref.at[:, :window], weight_ref.at[:, window:]]
-    copies = reduce_phase(
-        product_of([branch_ref, y_ref], weights, True, rows, 512), send, 0, acc, sent, got
-    )
+    product = product_of([branch_ref, y_ref], weights, True, rows, 512)
+
+    def product_and_move(k, store):
+        if k == 0:
+            for copy in moved:
+                copy.start()
+        product(k, store)
+
+    copies = reduce_phase(product_and_move, send, 0, acc, sent, got)
+    columns_out[here] = columns_of(0)[...]
     gain_out[...] = jnp.zeros_like(gain_out)
 
     def finish(r):
@@ -489,19 +517,22 @@
         gain_out[...] += gained[:8] + gained[8:]
 
     over_chunks(rows, finish)
-    for copy in copies:
+    for copy in moved:
+        copy.wait_recv()
+    for copy in copies + moved:
         copy.wait_send()
 
 
-def inputs_back(branch_rows, y_rows, weight, flat, gain):
+def inputs_back(branch_rows, y_rows, weight, flat, gain, columns):
     rows, width = flat.shape
+    count, whole = columns.shape
     return remote_call(
         inputs_back_kernel,
         "inputs_back",
         3,
-        [((rows, width), F32), ((8, width), F32)],
-        (branch_rows, y_rows, weight, flat, gain),
-        exchange_scratch(rows, width, 6),
+        [((rows, width), F32), ((8, width), F32), ((4 * count, whole // 4), BF)],
+        (branch_rows, y_rows, weight, flat, gain, columns),
+        exchange_scratch(rows, width, 9),
     )
 
 
@@ -841,6 +872,110 @@
     )
 
 
+def grads_kernel(
+    bases, normed_ref, y_ref, branch_ref, x_ref, forget_ref, admit_ref,
+    stacked_out,
+    gates, blocks, gate_total, sends, recvs,
+):
+    step = pl.program_id(0)
+    wide, stacked_rows, quarter = stacked_out.shape
+    window = x_ref.shape[1]
+    tiles = (window + y_ref.shape[1]) // LANES
+    group = wide // pl.num_programs(0)
+    part = normed_ref.shape[1] // group
+    room = stacked_rows - tiles * part
+    share = gate_total.shape[0] // wide
+
+    def quarter_of(k):
+        return pl.ds(pl.multiple_of(at_seq(k) * quarter, LANES), quarter)
+
+    def exchange(k):
+        return pltpu.make_async_remote_copy(
+            src_ref=gates.at[:, quarter_of(k)],
+            dst_ref=blocks.at[k],
+            send_sem=sends.at[k],
+            recv_sem=recvs.at[k],
+            device_id={"seq": at_seq(k)},
+            device_id_type=MESH,
+        )
+
+    @pl.when(step == 0)
+    def _():
+        barrier = pltpu.get_barrier_semaphore()
+        for k in (1, 2, 3):
+            pl.semaphore_signal(barrier, inc=1, device_id={"seq": at_seq(k)}, device_id_type=MESH)
+        for b in range(window // BW):
+            cols = slice(b * BW, (b + 1) * BW)
+            block = x_ref[:, cols].T
+            for source, at in ((forget_ref, 0), (admit_ref, BW)):
+                gates[cols, at : at + BW] = jnp.dot(
+                    block, source[:, cols], preferred_element_type=F32
+                ).astype(BF)
+        pl.semaphore_wait(barrier, 3)
+        for k in (3, 1, 2):
+            exchange(k).start()
+
+    left = normed_ref[...].T
+    first = 0
+    for right in (branch_ref, y_ref):
+        sums = jnp.dot(left, right[...], preferred_element_type=F32).astype(BF)
+        count = right.shape[1] // LANES
+        for g in range(group):
+            for i in range(count):
+                at = (first + i) * part
+                stacked_out[step * group + g, at : at + part, :] = sums[
+                    g * part : (g + 1) * part, i * LANES : (i + 1) * LANES
+                ]
+        first += count
+
+    @pl.when(step == pl.num_programs(0) - 1)
+    def _():
+        gate_total[...] = jnp.zeros_like(gate_total)
+        for k in range(4):
+            if k:
+                exchange(k).wait_recv()
+            other = at_seq(k)
+            base = other * 0
+            for j, start_row in enumerate(bases):
+                base = jnp.where(other == j, start_row, base)
+            at = pl.ds(pl.multiple_of(base, 8), window)
+            value = blocks[k] if k else gates[:, quarter_of(0)]
+            gate_total[at, :] += value.astype(F32)
+        for g in range(wide):
+            value = gate_total[g * share : (g + 1) * share, :]
+            if room > share:
+                value = jnp.concatenate([value, jnp.zeros((room - share, quarter), F32)], axis=0)
+            stacked_out[g, tiles * part :, :] = value.astype(BF)
+        for k in (1, 2, 3):
+            exchange(k).wait_send()
+
+
+def temporal_grads(normed, y_rows, branch_rows, x_win, forget_win, admit_win, wide, bases, stacked_rows):
+    total, width = normed.shape
+    share, window = y_rows.shape[1], x_win.shape[1]
+    quarter = 2 * BW // 4
+    return pl.pallas_call(
+        functools.partial(grads_kernel, bases),
+        grid=(width // BW,),
+        in_specs=[pl.BlockSpec((total, BW), lambda i: (0, i))]
+        + [whole(v.shape) for v in (y_rows, branch_rows, x_win, forget_win, admit_win)],
+        out_specs=whole((wide, stacked_rows, quarter)),
+        out_shape=jax.ShapeDtypeStruct((wide, stacked_rows, quarter), BF),
+        scratch_shapes=[
+            pltpu.VMEM((window, 2 * BW), BF),
+            pltpu.VMEM((4, window, quarter), BF),
+            pltpu.VMEM((4 * share, quarter), F32),
+            pltpu.SemaphoreType.DMA((4,)),
+            pltpu.SemaphoreType.DMA((4,)),
+        ],
+        compiler_params=pltpu.CompilerParams(
+            collective_id=9, has_side_effects=True, vmem_limit_bytes=48 * 1024 * 1024
+        ),
+        cost_estimate=pl.CostEstimate(flops=1000, bytes_accessed=1000, transcendentals=0),
+        name="temporal_grads",
+    )(normed, y_rows, branch_rows, x_win, forget_win, admit_win)
+
+
 def place(k, block, buffer, plan, outs):
     buffer[...] = block[...].astype(F32)
     other = at_seq(k)
@@ -853,56 +988,23 @@
             out[:, cols] += buffer[first + i * count : first + (i + 1) * count, :]
 
 
-def spread_kernel(first_ref, second_ref, first_out, second_out, first_blocks, second_blocks, sends, recvs):
-    greet()
-    send = sender(sends, recvs)
-    first = both_ways(send, 0, first_ref, first_blocks)
-    second = both_ways(send, 6, second_ref, second_blocks)
-
-    def put(k, block, out):
-        columns = block.shape[1]
-        other = at_seq(k)
-        for i in range(columns // LANES):
-            start_col = pl.multiple_of(other * columns + i * LANES, LANES)
-            out[:, pl.ds(start_col, LANES)] = block[:, i * LANES : (i + 1) * LANES]
-
-    put(0, first_ref, first_out)
-    put(0, second_ref, second_out)
-    first = pass_on(send, 0, first_blocks, first)
-    second = pass_on(send, 6, second_blocks, second)
-    settle(first)
-    for k in (1, 2, 3):
-        put(k, first_blocks.at[k], first_out)
-    settle(second)
-    for k in (1, 2, 3):
-        put(k, second_blocks.at[k], second_out)
-
-
-def spread(first, second, groups):
-    counts = [first.shape[0], second.shape[0]]
-    first, second = (jnp.pad(v, ((0, -v.shape[0] % 32), (0, 0))) for v in (first, second))
-    wholes = remote_call(
-        spread_kernel,
-        "spread",
-        8,
-        [((v.shape[0], groups * v.shape[1]), BF) for v in (first, second)],
-        (first, second),
-        [
-            pltpu.VMEM((groups,) + first.shape, BF),
-            pltpu.VMEM((groups,) + second.shape, BF),
-            pltpu.SemaphoreType.DMA((12,)),
-            pltpu.SemaphoreType.DMA((12,)),
-        ],
-    )
-    return [v[:count] for v, count in zip(wholes, counts)]
-
-
-def last_kernel(
-    plan, parts_ref, sums_ref,
-    first_out, second_out, sums_out,
-    blocks, buffer, total, got_sums, sends, recvs, sum_sends, sum_recvs,
-):
+def put(k, block, out):
+    columns = block.shape[1]
+    other = at_seq(k)
+    for i in range(columns // LANES):
+        start_col = pl.multiple_of(other * columns + i * LANES, LANES)
+        out[:, pl.ds(start_col, LANES)] = block[:, i * LANES : (i + 1) * LANES]
+
+
+def spread_kernel(plan, parts_ref, early_ref, late_ref, *refs):
+    outs, refs = refs[: len(plan)], refs[len(plan) :]
+    sums_out, blocks, buffer, *refs = refs
+    wholes, refs = refs[: len(plan)], refs[len(plan) :]
+    total, sums_ref, got_sums, sends, recvs, sum_sends, sum_recvs = refs
     wide = sums_ref.shape[0]
+    early = early_ref.shape[1]
+    sums_ref[:, :early] = early_ref[...]
+    sums_ref[:, early:] = late_ref[...]
     w = lax.axis_index("wide")
     barrier = pltpu.get_barrier_semaphore()
     for mask in (1, 2):
@@ -916,7 +1018,6 @@
     lax.fori_loop(1, wide, tell, 0)
     pl.semaphore_wait(barrier, wide + 1)
     send = sender(sends, recvs)
-    copies = both_ways(send, 0, parts_ref, blocks)
 
     def chunk(i):
         other = lax.rem(w + i, wide)
@@ -940,37 +1041,41 @@
         return carry + got_sums[i]
 
     lax.fori_loop(1, wide, begin, 0)
-    outs = (first_out, second_out)
-    for out in outs:
+    copies = both_ways(send, 0, parts_ref, blocks)
+    for out in wholes:
         out[...] = jnp.zeros_like(out)
-    place(0, parts_ref, buffer, plan, outs)
+    place(0, parts_ref, buffer, plan, wholes)
     total[0] = lax.fori_loop(1, wide, finish, sums_ref[w])
     to_near = send(6, total.at[0], total.at[1], 1)
     copies = pass_on(send, 0, blocks, copies)
     to_near.wait_recv()
     total[2] = total[0] + total[1]
     to_side = send(7, total.at[2], total.at[3], 2)
+    to_side.wait_recv()
+    sums_out[...] = total[2] + total[3]
     settle(copies)
     for k in (1, 2, 3):
-        place(k, blocks.at[k], buffer, plan, outs)
-    to_side.wait_recv()
-    sums_out[...] = total[2] + total[3]
+        place(k, blocks.at[k], buffer, plan, wholes)
+    for out, values in zip(outs, wholes):
+        out[...] = values[...].astype(BF)
     to_near.wait_send()
     to_side.wait_send()
 
 
-def spread_last(parts, sums, plan, shapes):
-    wide, count, _unused = sums.shape
+def spread(parts, early, late, plan, shapes):
+    wide = early.shape[0]
+    count = early.shape[1] + late.shape[1]
     return remote_call(
-        functools.partial(last_kernel, plan),
-        "spread_last",
-        5,
-        [(shape, F32) for shape in shapes] + [((count, LANES), F32)],
-        (parts, sums),
-        [
-            pltpu.VMEM((4,) + parts.shape, BF),
-            pltpu.VMEM(parts.shape, F32),
+        functools.partial(spread_kernel, plan),
+        "spread",
+        8,
+        [(shape, BF) for shape in shapes] + [((count, LANES), F32)],
+        (parts, early, late),
+        [pltpu.VMEM((4,) + parts.shape, BF), pltpu.VMEM(parts.shape, F32)]
+        + [pltpu.VMEM(shape, F32) for shape in shapes]
+        + [
             pltpu.VMEM((4, count, LANES), F32),
+            pltpu.VMEM((wide, count, LANES), F32),
             pltpu.VMEM((wide, count, LANES), F32),
             pltpu.SemaphoreType.DMA((8,)),
             pltpu.SemaphoreType.DMA((8,)),
@@ -978,6 +1083,35 @@
             pltpu.SemaphoreType.DMA((wide,)),
         ],
     )
+
+
+def last_kernel(columns_ref, columns_out, column_blocks, sends, recvs):
+    greet()
+    send = sender(sends, recvs)
+    copies = both_ways(send, 0, columns_ref, column_blocks)
+    put(0, columns_ref, columns_out)
+    copies = pass_on(send, 0, column_blocks, copies)
+    settle(copies)
+    for k in (1, 2, 3):
+        put(k, column_blocks.at[k], columns_out)
+
+
+def spread_last(columns):
+    count = columns.shape[0]
+    columns = jnp.pad(columns, ((0, -count % 32), (0, 0)))
+    (wholes,) = remote_call(
+        last_kernel,
+        "spread_last",
+        5,
+        [((columns.shape[0], 4 * columns.shape[1]), BF)],
+        (columns,),
+        [
+            pltpu.VMEM((4,) + columns.shape, BF),
+            pltpu.SemaphoreType.DMA((6,)),
+            pltpu.SemaphoreType.DMA((6,)),
+        ],
+    )
+    return wholes[:count]
 
 
 def body(
@@ -1145,140 +1279,93 @@
     mixed_grad = contract_last(stream_low_all, out_rows)
     out_grad = contract_rows(mixed_low, stream_low_all).astype(BF)
     mixed_grad, out_grad = lax.optimization_barrier((mixed_grad, out_grad))
-    out_parts = swapped(lambda j: lax.dynamic_slice_in_dim(out_grad, j * quarter, quarter, 1))
     position = w * tokens + jnp.arange(tokens, dtype=jnp.int32)
     valid = (position[None, :] < lengths[:, None]).astype(F32).reshape(rows, 1)
     y_rows, branch_rows, forget_win, admit_win, channel_grads, result, squares = middle(
         mixed_grad, branch_y, local, reach, carry, rate, per_channel, ends[:, :, 0],
         edge_win, gates, valid, feed_parts, conv_out, forget, admit, x_win, stream, temporal,
     )
-    y_rows, branch_rows, *out_parts = lax.optimization_barrier((y_rows, branch_rows, *out_parts))
-    out_cols = jnp.concatenate(in_order(out_parts), axis=0)
     partial_sums = jnp.concatenate([jnp.sum(squares, axis=(1, 2)), jnp.sum(valid).reshape(1)])
 
-    bases = [min(j * share // BW * BW, channels - window) for j in range(groups)]
-
-    def placed(parts, axis):
-        rest = [
-            tuple(
-                (bases[j], channels - window - bases[j]) if d == axis else (0, 0) for d in range(2)
-            )
-            for j in range(groups)
-        ]
-        return sum(jnp.pad(p.astype(F32), r) for p, r in zip(parts, rest))
-
-    def stack(values):
-        values = values.reshape(wide, values.shape[0] // wide, values.shape[1])
-        tiles = values.shape[2] // LANES
-        return jnp.concatenate(
-            [values[:, :, i * LANES : (i + 1) * LANES] for i in range(tiles)], axis=1
-        )
-
-    gelu_part = contract_rows(normed_all, y_rows).astype(BF)
-
-    gate_grads = jnp.concatenate(
-        [
-            jnp.einsum(
-                "tki,tkj->kij",
-                x_win.reshape(total, blocks, BW),
-                rows_win.reshape(total, blocks, BW),
-                preferred_element_type=F32,
-            ).reshape(window, BW)
-            for rows_win in (forget_win, admit_win)
-        ],
-        axis=1,
-    ).astype(BF)
-    branch_part = contract_rows(normed_all, branch_rows).astype(BF)
+    bases = tuple(min(j * share // BW * BW, channels - window) for j in range(groups))
+    branch_size = dw * window // LANES
+    gates_at = branch_size + dw * share // LANES
+    stacked_rows = (gates_at + rw + 31) // 32 * 32
+    stacked = temporal_grads(
+        normed_all, y_rows, branch_rows, x_win, forget_win, admit_win, wide, bases, stacked_rows
+    )
+
     def sum_over_wide(values):
         return lax.psum_scatter(values, "wide", scatter_dimension=0, tiled=True)
 
-    out_cols, gelu_part = lax.optimization_barrier((out_cols, gelu_part))
-    gate_cols_grad = placed(
-        in_order(
-            swapped(lambda j: lax.dynamic_slice_in_dim(gate_grads, j * gate_cols, gate_cols, 1))
-        ),
-        0,
-    ).astype(BF)
-    out_sum = sum_over_wide(out_cols)
-    gelu_sum = sum_over_wide(gelu_part)
-    pieces = [(branch_part, window), (gate_cols_grad, gate_cols)]
-    stacked = jnp.concatenate([stack(values) for values, _unused in pieces], axis=1)
-    stacked = jnp.pad(stacked, ((0, 0), (0, -stacked.shape[1] % 32), (0, 0)))
     stacked, mlp_grad = lax.optimization_barrier((stacked, mlp_grad))
-    first_back, gain_one_grad = inputs_back(
-        branch_rows, y_rows, x_y_cols, flat_low, gain_one
-    )
-    gelu_sum, gain_one_grad = lax.optimization_barrier((gelu_sum, gain_one_grad))
-    last_sum = sum_over_wide(stacked)
-
-    def plan_of(pieces, starts):
-        plan, at = [], 0
-        for (values, columns), cols in zip(pieces, starts):
-            count = values.shape[0] // wide
-            plan.append((at, count, columns // LANES, tuple(cols)))
-            at += count * columns // LANES
-        return tuple(plan)
-
-    out_whole, gelu_whole = spread(out_sum, gelu_sum, groups)
-    earlier = lax.optimization_barrier(
-        (
-            last_sum,
-            result.astype(BF).reshape(seqs, tokens, width),
-            (stream_grad + first_back).reshape(seqs, tokens, width),
-            gelu_whole.astype(F32),
-            out_whole.astype(F32),
-            mlp_grad[:, :hidden_units].astype(F32),
-            mlp_grad[:, hidden_units:].astype(F32),
-            down_grad.astype(F32),
-        )
-    )
-    last_sum, output, inputs_grad, gelu_whole, out_whole, gate_grad, up_grad, down_grad = earlier
-
+    temporal_sum = sum_over_wide(stacked)
     channel_all = lax.dynamic_update_slice_in_dim(
         jnp.zeros((8, channels), F32), channel_grads, s * share, 1
     )
-    sums = jnp.concatenate(
+    early_sums = jnp.concatenate(
         [
             channel_all.reshape(8, wide, rw).transpose(1, 0, 2).reshape(wide, 8 * rw),
-            jnp.sum(gain_one_grad, axis=0).reshape(wide, dw),
             gain_two_grad.reshape(wide, dw),
             jnp.tile(partial_sums[None, :], (wide, 1)),
         ],
         axis=1,
     )
-    sums = jnp.pad(sums, ((0, 0), (0, -sums.shape[1] % (8 * LANES)))).reshape(wide, -1, LANES)
-    branch_whole, gates_whole, sums = spread_last(
-        last_sum[0],
-        sums,
-        plan_of(pieces, (bases, [j * gate_cols for j in range(groups)])),
-        ((dw, channels), (rw, 2 * BW)),
-    )
-    sums = sums.reshape(-1)
+    early_sums = jnp.pad(early_sums, ((0, 0), (0, -early_sums.shape[1] % (8 * LANES))))
+    early_sums = early_sums.reshape(wide, -1, LANES)
+    branch_late, early_sums = lax.optimization_barrier((branch_rows, early_sums))
+    first_back, gain_one_grad, out_cols = inputs_back(
+        branch_late, y_rows, x_y_cols, flat_low, gain_one, out_grad
+    )
+    out_sum = sum_over_wide(out_cols)
+    late_sums = jnp.sum(gain_one_grad, axis=0).reshape(wide, dw)
+    late_sums = jnp.pad(late_sums, ((0, 0), (0, -dw % (8 * LANES)))).reshape(wide, -1, LANES)
+    temporal_sum, late_sums = lax.optimization_barrier((temporal_sum, late_sums))
+
+    plan = (
+        (0, dw, window // LANES, bases),
+        (branch_size, dw, share // LANES, tuple(j * share for j in range(groups))),
+        (gates_at, rw, gate_cols // LANES, tuple(j * gate_cols for j in range(groups))),
+    )
+    branch_whole, gelu_whole, gates_whole, sums = spread(
+        temporal_sum[0],
+        early_sums,
+        late_sums,
+        plan,
+        ((dw, channels), (dw, channels), (rw, 2 * BW)),
+    )
+    late_at = early_sums.shape[1]
+    gain_one_sum = sums[late_at:].reshape(-1)[:dw]
+    sums = sums[:late_at].reshape(-1)
     channel_sums = sums[: 8 * rw].reshape(8, rw)
-    gain_sums = sums[8 * rw : 8 * rw + 2 * dw].reshape(2, dw)
-    totals = sums[8 * rw + 2 * dw : 8 * rw + 2 * dw + 4]
-
+    gain_two_sum = sums[8 * rw : 8 * rw + dw]
+    totals = sums[8 * rw + dw : 8 * rw + dw + 4]
     statistics = jnp.sqrt(totals[0:3] / (totals[3] * width))
-    return (
-        output,
-        inputs_grad,
-        gain_sums[0],
-        gelu_whole,
-        branch_whole,
-        gates_whole[:, :BW],
-        gates_whole[:, BW:],
-        channel_sums[0],
-        channel_sums[1],
-        channel_sums[2],
-        channel_sums[4:8],
-        channel_sums[3],
-        out_whole,
-        gain_sums[1],
-        gate_grad,
-        up_grad,
-        down_grad,
-        statistics,
-    )
+    earlier = lax.optimization_barrier(
+        (
+            out_sum,
+            result.astype(BF).reshape(seqs, tokens, width),
+            (stream_grad + first_back).reshape(seqs, tokens, width),
+            gain_one_sum,
+            gelu_whole.astype(F32),
+            branch_whole.astype(F32),
+            gates_whole[:, :BW].astype(F32),
+            gates_whole[:, BW:].astype(F32),
+            channel_sums[0],
+            channel_sums[1],
+            channel_sums[2],
+            channel_sums[4:8],
+            channel_sums[3],
+            gain_two_sum,
+            mlp_grad[:, :hidden_units].astype(F32),
+            mlp_grad[:, hidden_units:].astype(F32),
+            down_grad.astype(F32),
+            statistics,
+        )
+    )
+    out_sum, *outputs = earlier
+    outputs.insert(12, spread_last(out_sum).astype(F32))
+    return tuple(outputs)
 
 
 def solution(mesh):

time: 690 us -> 679 us (0.984)
  Pallas kernels: 386 us -> 421 us
  local copies, waits for them, and re-layouts: 57.1 us -> 42.7 us
  matrix products: 103 us -> 89.4 us
  waiting for transfers between devices: 12.5 us -> 1.95 us
  starting transfers between devices: 19.6 us -> 12.3 us
    pallas_call x6, Pallas kernels: 309 us -> 344 us  [remote_call(): pl.pallas_call(kernel, in_specs=[pl.BlockSpec(memory_space=pltpu.VMEM)] *...]
    pallas_call x1, Pallas kernels: 64.5 us -> 47.9 us  [middle(): pl.pallas_call(middle_kernel, in_specs=[vmem] * 12 + [anywhere] * 6, out_...]
    pallas_call x0 -> x1, Pallas kernels: none -> 16.4 us  [temporal_grads(): pl.pallas_call(functools.partial(grads_kernel, bases), grid=(width // BW,...]
    dot_general x5 -> x3, matrix products: 46 us -> 36.7 us  [contract_rows(): lax.dot_general(left, right, (((0,), (0,)), ((), ())), preferred_element_...]
    ppermute x16 -> x10, waiting for transfers between devices: 9.14 us -> 0.03 us  [swap(): lax.ppermute(values, 'seq', [(i, i ^ mask) for i in range(lax.axis_size('...]
    ppermute x16 -> x10, starting transfers between devices: 18.7 us -> 11.6 us  [swap(): lax.ppermute(values, 'seq', [(i, i ^ mask) for i in range(lax.axis_size('...]
    unnamed x109 -> x100, local copies, waits for them, and re-layouts: 27.5 us -> 23.4 us
  transfers between devices with their start and end apart: 25 -> 18, of which waited for: 5 -> 1; matrix products, arithmetic and copies ran while one was open for 28% -> 25% of each run, Pallas kernels for 53% -> 61%
where the time goes in v4:
time: 679 us; the launch traced here: 670 us
  Pallas kernels  421 us (62%)
  matrix products  89.4 us (13%)
  other arithmetic  50.8 us (7%)
  local copies, waits for them, and re-layouts  42.7 us (6%)
  blocking collectives  35.7 us (5%)
  between operations  16.1 us (2%)
  starting transfers between devices  12.3 us (2%)
    pallas_call x6, Pallas kernels, remote_call(): pl.pallas_call(kernel, in_specs=[pl.BlockSpec(memory_space=pltpu.VMEM)] *...  344 us
    pallas_call x1, Pallas kernels, middle(): pl.pallas_call(middle_kernel, in_specs=[vmem] * 12 + [anywhere] * 6, out_...  47.9 us
    dot_general x3, matrix products, contract_rows(): lax.dot_general(left, right, (((0,), (0,)), ((), ())), preferred_element_...  36.7 us
    dot_general x3, matrix products, dot(): return jnp.dot(left, right, preferred_element_type=F32)  30.5 us
    unnamed x100, local copies, waits for them, and re-layouts  23.4 us
    dot_general x2, matrix products, contract_last(): lax.dot_general(left, right, (((1,), (1,)), ((), ())), preferred_element_...  22.2 us
    all_gather x1, blocking collectives, body(): ends = lax.all_gather(ends, 'wide')[:, :, :, 0]  18.2 us
    all_gather x1, blocking collectives, body(): small = lax.all_gather(small, 'wide')  17.5 us
  transfers between devices with their start and end apart: 18, of which 1 were waited for; matrix products, arithmetic and copies ran while one was open for 25% of the time, Pallas kernels for 61%

profile of v4, /device:TPU:0, one launch (start us, length us, event | category | flops | bytes accessed | tf_op | source)
XLA Modules:
  0.0 670.0 jit_solution(15496923425111011812)
XLA Ops:
  14.4 47.0 %start.1 = (bf16[4,256,2048]{2,1,0:T(8,128)(2,1)}, bf16[4,32,2048]{2,1,0:T(8,128)(2,1)}) custom-call(bf16[256,2048]{1,0:T(8,128)(2,1)} %bitcast.364), custom_call_target="tpu_custom_call" | custom-call | flops 1000 | bytes 1000 | tf_op jit(solution)/shard_map/start/pallas_call | solution.py:353
  65.0 17.5 %all-gather = bf16[2752,128]{1,0:T(8,128)(2,1)S(1)} all-gather(bf16[344,128]{1,0:T(8,128)(2,1)S(1)} %pad_maximum_fusion.5), channel_id=2, replica_groups=mesh['seq'=4,'wide'=8] {'wide'}, dimensions={0}, use_global_device_ids=true | all-gather | bytes 792576 | tf_op jit(solution)/shard_map/all_gather | solution.py:1187
  89.3 3.1 multiply_reduce_fusion
  92.6 5.3 fusion.1.normed_ref
  112.2 10.4 %fusion.59 = f32[1024,1408]{1,0:T(8,128)S(1)} fusion(bf16[1024,2048]{1,0:T(8,128)(2,1)} %fusion.1.normed_ref, bf16[2048,1408]{1,0:T(8,128)(2,1)} %all-gather.7.cloned.1.call-done.weight_ref), kind=kOutput, calls=%fused_computation.168 | convolution fusion | flops 5905580032 | bytes 15728640 | tf_op jit(solution)/shard_map/dot_general | solution.py:21
  133.9 12.8 %temporal_forward.1 = (bf16[1024,640]{1,0:T(8,128)(2,1)S(1)}, bf16[1024,640]{1,0:T(8,128)(2,1)S(1)}, f32[1024,640]{1,0:T(8,128)}, f32[1024,640]{1,0:T(8,128)}, f...) custom-call(s32[1]{0:T(128)} %bitcast.off_ref, bf16[1024,768]{1,0:T(8,128)(2,1)S(1)} %slice.305.x_ref.x_far, ...), custom_call_target="tpu_custom_call" | custom-call | flops 1000 | bytes 1000 | tf_op jit(solution)/shard_map/temporal_forward/pallas_call | solution.py:139
  146.7 18.2 %all-gather.1 = f32[64,2,1,640]{3,1,2,0:T(2,128)S(1)} all-gather(f32[8,2,1,640]{3,1,2,0:T(2,128)S(1)} %copy.88), channel_id=3, replica_groups=mesh['seq'=4,'wide'=8] {'wide'}, dimensions={0}, use_global_device_ids=true | all-gather | bytes 368640 | tf_op jit(solution)/shard_map/all_gather | solution.py:1243
  165.0 6.4 fusion.58
  177.7 82.3 %stream_and_norm.1 = (f32[256,2048]{1,0:T(8,128)}, f32[256,2048]{1,0:T(8,128)}, bf16[4,256,2048]{2,1,0:T(8,128)(2,1)}) custom-call(bf16[1024,640]{1,0:T(8,128)(2,1)} %get-tuple-element.171.mixed_ref, bf16[640,2048]{1,0:T(8,128)(2,1)} %pad_maximum_fusion.1.weight_ref, bf16[256,2048]{1,0:T(8,128)(2,1)} %bitcast.365, f32[1,2048]{1,0:T(1,128)} %bitcast.389), custom_call_target="tpu_custom_call" | custom-call | flops 1000 | bytes 1000 | tf_op jit(solution)/shard_map/stream_and_norm/pallas_call | solution.py:353
  260.1 17.2 %fusion.60 = f32[1024,3072]{1,0:T(8,128)S(1)} fusion(bf16[1024,2048]{1,0:T(8,128)(2,1)} %bitcast.398, bf16[2048,3072]{1,0:T(8,128)(2,1)} %all-gather.11.cloned.1.call-done.weight_far), kind=kOutput, calls=%fused_computation.169 | convolution fusion | flops 12884901888 | bytes 29360128 | tf_op jit(solution)/shard_map/dot_general | solution.py:21
  283.5 10.9 %convolution_convert_fusion.1 = bf16[1536,2048]{1,0:T(8,128)(2,1)} fusion(bf16[1024,1536]{1,0:T(8,128)(2,1)S(1)} %multiply_convert_fusion.1.hidden_far, bf16[1024,2048]{1,0:T(8,128)(2,1)} %constant_dynamic-update-slice_fusion), kind=kOutput, calls=%fused_computation.8 | convolution fusion | flops 6445596672 | bytes 13631488 | tf_op jit(solution)/shard_map/dot_general | solution.py:29
  296.4 17.3 %fusion.17 = (bf16[1024,1536]{1,0:T(8,128)(2,1)S(1)}, bf16[1024,1536]{1,0:T(8,128)(2,1)S(1)}) fusion(f32[1024,3072]{1,0:T(8,128)} %copy-done.12, bf16[1024,2048]{1,0:T(8,128)(2,1)} %constant_dynamic-update-slice_fusion, bf16[1536,2048]{1,0:T(8,128)(2,1)} %all-gather.13.cloned.1.call-done.down_far), kind=kOutput, calls=%fused_computation.24 | convolution fusion | flops 6486491136 | bytes 29360128 | tf_op jit(solution)/shard_map/dot_general | solution.py:25
  313.7 3.4 pad_maximum_fusion.rows_ref
  317.1 18.8 %convolution_convert_fusion = bf16[2048,3072]{1,0:T(8,128)(2,1)} fusion(bf16[1024,2048]{1,0:T(8,128)(2,1)} %bitcast.399, bf16[1024,1536]{1,0:T(8,128)(2,1)S(1)} %get-tuple-element.169, bf16[1024,1536]{1,0:T(8,128)(2,1)S(1)} %get-tuple-element.168), kind=kOutput, calls=%fused_computation | convolution fusion | flops 12903776256 | bytes 23068672 | tf_op jit(solution)/shard_map/dot_general | solution.py:29
  338.8 88.6 %stream_back.1 = (f32[256,2048]{1,0:T(8,128)}, bf16[4,256,2048]{2,1,0:T(8,128)(2,1)}, f32[8,2048]{1,0:T(8,128)}, bf16[4,256,2048]{2,1,0:T(8,128)(2,1)}) custom-call(bf16[1024,3072]{1,0:T(8,128)(2,1)} %pad_maximum_fusion.rows_ref, f32[256,2048]{1,0:T(8,128)} %get-tuple-element.109.stream_ref.stream_far, f32[1,2048]{1,0:T(1,128)} %bitcast.390, ...), custom_call_target="tpu_custom_call" | custom-call | flops 1000 | bytes 1000 | tf_op jit(solution)/shard_map/stream_back/pallas_call | solution.py:353
  427.4 6.9 %convolution_convert_fusion.2.columns_ref = bf16[640,2048]{1,0:T(8,128)(2,1)} fusion(bf16[1024,640]{1,0:T(8,128)(2,1)S(1)} %copy-done.14, bf16[1024,2048]{1,0:T(8,128)(2,1)} %bitcast.400), kind=kOutput, calls=%fused_computation.29 | convolution fusion | flops 2685665280 | bytes 8126464 | tf_op jit(solution)/shard_map/dot_general | solution.py:29
  434.3 4.9 fusion.57.grad_ref
  439.3 47.9 %middle.1 = (bf16[1024,640]{1,0:T(8,128)(2,1)}, bf16[1024,768]{1,0:T(8,128)(2,1)}, bf16[1024,768]{1,0:T(8,128)(2,1)}, bf16[1024,768]{1,0:T(8,128)(2,1)}, f32[8,6...) custom-call(f32[1024,640]{1,0:T(8,128)} %fusion.57.grad_ref, f32[1024,640]{1,0:T(8,128)} %get-tuple-element.170.y_ref, ...), custom_call_target="tpu_custom_call" | custom-call | flops 1000 | bytes 1000 | tf_op jit(solution)/shard_map/middle/pallas_call | solution.py:836
  491.3 16.4 %temporal_grads.1 = bf16[8,3136,128]{2,1,0:T(8,128)(2,1)} custom-call(bf16[1024,2048]{1,0:T(8,128)(2,1)} %fusion.1.normed_ref, bf16[1024,640]{1,0:T(8,128)(2,1)S(1)} %copy-done.6, bf16[1024,768]{1,0:T(8,128)(2,1)S(1)} %copy-done.5, bf16[1024,768]{1,0:T(8,128)(2,1)S(1)} %copy-done.3, bf16[1024,768]{1,0:T(8,128)(2,1)S(1)} %copy-done.8, ...), custom_call_target="tpu_custom_call" | custom-call | flops 1000 | bytes 1000 | tf_op jit(solution)/shard_map/temporal_grads/pallas_call | solution.py:957
  511.5 74.3 %inputs_back.1 = (f32[256,2048]{1,0:T(8,128)}, f32[8,2048]{1,0:T(8,128)}, bf16[2560,512]{1,0:T(8,128)(2,1)}) custom-call(bf16[1024,768]{1,0:T(8,128)(2,1)} %get-tuple-element.125.branch_ref, bf16[1024,640]{1,0:T(8,128)(2,1)} %get-tuple-element.126.y_ref, bf16[2048,1408]{1,0:T(8,128)(2,1)} %all-gather.7.cloned.1.call-done.weight_ref, ...), custom_call_target="tpu_custom_call" | custom-call | flops 1000 | bytes 1000 | tf_op jit(solution)/shard_map/inputs_back/pallas_call | solution.py:353
  595.3 36.5 %spread.1 = (bf16[256,2560]{1,0:T(8,128)(2,1)}, bf16[256,2560]{1,0:T(8,128)(2,1)}, bf16[320,512]{1,0:T(8,128)(2,1)}, f32[32,128]{1,0:T(8,128)}) custom-call(bf16[3136,128]{1,0:T(8,128)(2,1)} %bitcast.382, f32[8,24,128]{2,1,0:T(8,128)} %bitcast.383, f32[8,8,128]{2,1,0:T(8,128)} %bitcast.388), custom_call_target="tpu_custom_call" | custom-call | flops 1000 | bytes 1000 | tf_op jit(solution)/shard_map/spread/pallas_call | solution.py:353
  635.5 3.1 convert_element_type.128
  644.3 15.2 %spread_last.1 = bf16[320,2048]{1,0:T(8,128)(2,1)} custom-call(bf16[320,512]{1,0:T(8,128)(2,1)} %reduce-scatter.7.cloned.1.call-done.columns_ref), custom_call_target="tpu_custom_call" | custom-call | flops 1000 | bytes 1000 | tf_op jit(solution)/shard_map/spread_last/pallas_call | solution.py:353
  659.6 3.1 convert_element_type.135
  (214 shorter events, 86.2 us)
Async XLA Ops:
  7.2 105.0 %all-gather.7.cloned.1.call-start = ((), (), s32[]{:S(2)}) async-start(), calls=%async_computation.4 | async-start | bytes 6488064 | tf_op jit(solution)/shard_map/all_gather | solution.py:1164
  8.8 52.7 %copy-start.35 = (bf16[320]{0:T(512)(128)(2,1)S(1)}, bf16[320]{0:T(512)(128)(2,1)}, u32[]{:S(2)}) copy-start(bf16[320]{0:T(512)(128)(2,1)} %param.25) | copy-start | bytes 1924
  8.9 52.7 %copy-start.29 = (bf16[320,256]{1,0:T(8,128)(2,1)S(1)}, bf16[320,256]{1,0:T(8,128)(2,1)}, u32[]{:S(2)}) copy-start(bf16[320,256]{1,0:T(8,128)(2,1)} %param.23) | copy-start | bytes 491524
  8.9 52.7 %copy-start.30 = (bf16[320,256]{1,0:T(8,128)(2,1)S(1)}, bf16[320,256]{1,0:T(8,128)(2,1)}, u32[]{:S(2)}) copy-start(bf16[320,256]{1,0:T(8,128)(2,1)} %param.24) | copy-start | bytes 491524
  9.9 115.4 %all-gather.9.cloned.1.call-start = ((), (), s32[]{:S(2)}) async-start(), calls=%async_computation.5 | async-start | bytes 2949120 | tf_op jit(solution)/shard_map/all_gather | solution.py:1195
  11.7 248.4 %all-gather.11.cloned.1.call-start = ((), (), s32[]{:S(2)}) async-start(), calls=%async_computation.6 | async-start | bytes 14155776 | tf_op jit(solution)/shard_map/all_gather | solution.py:1198
  14.3 282.0 %all-gather.13.cloned.1.call-start = ((), (), s32[]{:S(2)}) async-start(), calls=%async_computation.7 | async-start | bytes 7077888 | tf_op jit(solution)/shard_map/all_gather | solution.py:1201
  62.9 38.1 %collective-permute-start.1 = (bf16[256,2048]{1,0:T(8,128)(2,1)S(1)}, bf16[256,2048]{1,0:T(8,128)(2,1)}, u32[]{:S(2)}, u32[]{:S(2)}) collective-permute-start(bf16[256,2048]{1,0:T(8,128)(2,1)S(1)} %bitcast.368), channel_id=1, source_target_pairs={{0,16},{8,24},{16,0},{24,8},{1,17},{9,25},{17,1},{25,9},{2,18},{10... | collective-permute-start | bytes 3145736 | tf_op jit(solution)/shard_map/ppermute | solution.py:33
  63.6 37.5 %collective-permute-start = (bf16[256,2048]{1,0:T(8,128)(2,1)S(1)}, bf16[256,2048]{1,0:T(8,128)(2,1)}, u32[]{:S(2)}, u32[]{:S(2)}) collective-permute-start(bf16[256,2048]{1,0:T(8,128)(2,1)S(1)} %bitcast.369), channel_id=1, source_target_pairs={{0,8},{8,0},{16,24},{24,16},{1,9},{9,1},{17,25},{25,17},{2,10},{10... | collective-permute-start | bytes 3145736 | tf_op jit(solution)/shard_map/ppermute | solution.py:33
  84.3 15.4 %collective-permute-start.6 = (bf16[768,128]{1,0:T(8,128)(2,1)}, bf16[768,128]{1,0:T(8,128)(2,1)S(1)}, u32[]{:S(2)}, u32[]{:S(2)}) collective-permute-start(bf16[768,128]{1,0:T(8,128)(2,1)} %get-tuple-element.185), channel_id=1, source_target_pairs={{0,8},{8,0},{16,24},{24,16},{1,9},{9,1},{17,25},{25,17},{2,10},{10... | collective-permute-start | bytes 589832 | tf_op jit(solution)/shard_map/ppermute | solution.py:33
  85.2 14.6 %collective-permute-start.5 = (bf16[768,128]{1,0:T(8,128)(2,1)}, bf16[768,128]{1,0:T(8,128)(2,1)S(1)}, u32[]{:S(2)}, u32[]{:S(2)}) collective-permute-start(bf16[768,128]{1,0:T(8,128)(2,1)} %get-tuple-element.186), channel_id=1, source_target_pairs={{0,16},{8,24},{16,0},{24,8},{1,17},{9,25},{17,1},{25,9},{2,18},{10... | collective-permute-start | bytes 589832 | tf_op jit(solution)/shard_map/ppermute | solution.py:33
  86.7 13.0 %collective-permute-start.4 = (bf16[768,128]{1,0:T(8,128)(2,1)}, bf16[768,128]{1,0:T(8,128)(2,1)}, u32[]{:S(2)}, u32[]{:S(2)}) collective-permute-start(bf16[768,128]{1,0:T(8,128)(2,1)} %get-tuple-element.187), channel_id=1, source_target_pairs={{0,24},{8,16},{16,8},{24,0},{1,25},{9,17},{17,9},{25,1},{2,26},{10... | collective-permute-start | bytes 589832 | tf_op jit(solution)/shard_map/ppermute | solution.py:33
  87.8 339.6 %reduce-scatter.5.cloned.1.call-start = ((), (), s32[]{:S(2)}) async-start(), calls=%async_computation.8 | async-start | bytes 7077888 | tf_op jit(solution)/shard_map/reduce_scatter | solution.py:1265
  107.5 17.8 %collective-permute-start.3 = (bf16[128,2048]{1,0:T(8,128)(2,1)}, bf16[128,2048]{1,0:T(8,128)(2,1)S(1)}, u32[]{:S(2)}, u32[]{:S(2)}) collective-permute-start(bf16[128,2048]{1,0:T(8,128)(2,1)} %slice.153), channel_id=1, source_target_pairs={{0,8},{8,0},{16,24},{24,16},{1,9},{9,1},{17,25},{25,17},{2,10},{10... | collective-permute-start | bytes 1572872 | tf_op jit(solution)/shard_map/ppermute | solution.py:33
  108.4 16.9 %collective-permute-start.2 = (bf16[128,2048]{1,0:T(8,128)(2,1)}, bf16[128,2048]{1,0:T(8,128)(2,1)}, u32[]{:S(2)}, u32[]{:S(2)}) collective-permute-start(bf16[128,2048]{1,0:T(8,128)(2,1)} %slice.152), channel_id=1, source_target_pairs={{0,16},{8,24},{16,0},{24,8},{1,17},{9,25},{17,1},{25,9},{2,18},{10... | collective-permute-start | bytes 1572872 | tf_op jit(solution)/shard_map/ppermute | solution.py:33
  127.4 46.7 %collective-permute-start.9 = (bf16[640,512]{1,0:T(8,128)(2,1)S(1)}, bf16[640,512]{1,0:T(8,128)(2,1)S(1)}, u32[]{:S(2)}, u32[]{:S(2)}) collective-permute-start(bf16[640,512]{1,0:T(8,128)(2,1)S(1)} %get-tuple-element.176), channel_id=1, source_target_pairs={{0,8},{8,0},{16,24},{24,16},{1,9},{9,1},{17,25},{25,17},{2,10},{10... | collective-permute-start | bytes 1966088 | tf_op jit(solution)/shard_map/ppermute | solution.py:33
  128.5 45.7 %collective-permute-start.8 = (bf16[640,512]{1,0:T(8,128)(2,1)S(1)}, bf16[640,512]{1,0:T(8,128)(2,1)S(1)}, u32[]{:S(2)}, u32[]{:S(2)}) collective-permute-start(bf16[640,512]{1,0:T(8,128)(2,1)S(1)} %get-tuple-element.177), channel_id=1, source_target_pairs={{0,16},{8,24},{16,0},{24,8},{1,17},{9,25},{17,1},{25,9},{2,18},{10... | collective-permute-start | bytes 1966088 | tf_op jit(solution)/shard_map/ppermute | solution.py:33
  129.7 44.4 %collective-permute-start.7 = (bf16[640,512]{1,0:T(8,128)(2,1)S(1)}, bf16[640,512]{1,0:T(8,128)(2,1)S(1)}, u32[]{:S(2)}, u32[]{:S(2)}) collective-permute-start(bf16[640,512]{1,0:T(8,128)(2,1)S(1)} %get-tuple-element.178), channel_id=1, source_target_pairs={{0,24},{8,16},{16,8},{24,0},{1,25},{9,17},{17,9},{25,1},{2,26},{10... | collective-permute-start | bytes 1966088 | tf_op jit(solution)/shard_map/ppermute | solution.py:33
  176.0 84.1 %copy-start.19 = (bf16[640,512]{1,0:T(8,128)(2,1)}, bf16[640,512]{1,0:T(8,128)(2,1)S(1)}, u32[]{:S(2)}) copy-start(bf16[640,512]{1,0:T(8,128)(2,1)S(1)} %get-tuple-element.175) | copy-start | bytes 1966084
  294.4 213.3 %reduce-scatter.9.cloned.1.call-start = ((), (), s32[]{:S(2)}) async-start(), calls=%async_computation.10 | async-start | bytes 14155776 | tf_op jit(solution)/shard_map/reduce_scatter | solution.py:1272
  335.9 259.4 %reduce-scatter.11.cloned.1.call-start = ((), (), s32[]{:S(2)}) async-start(), calls=%async_computation.11 | async-start | bytes 7225344 | tf_op jit(solution)/shard_map/reduce_scatter | solution.py:1299
  338.8 88.6 %copy-start.14 = (bf16[1024,640]{1,0:T(8,128)(2,1)S(1)}, bf16[1024,640]{1,0:T(8,128)(2,1)}, u32[]{:S(2)}) copy-start(bf16[1024,640]{1,0:T(8,128)(2,1)} %get-tuple-element.171.mixed_ref) | copy-start | bytes 3932164
  507.8 136.5 %reduce-scatter.7.cloned.1.call-start = ((), (), s32[]{:S(2)}) async-start(), calls=%async_computation.9 | async-start | bytes 2949120 | tf_op jit(solution)/shard_map/reduce_scatter | solution.py:1299
  511.5 76.0 %copy-start.26 = (bf16[1536,256]{1,0:T(8,128)(2,1)S(1)}, bf16[1536,256]{1,0:T(8,128)(2,1)}, u32[]{:S(2)}) copy-start(bf16[1536,256]{1,0:T(8,128)(2,1)} %reduce-scatter.5.cloned.1.call-done) | copy-start | bytes 2359300
  (37 other events, 713.3 us)
Sparse Core Ops, SparseCore 0:
  10.3 65.2 all-gather.6
  77.8 33.0 all-gather.8
  113.1 118.3 all-gather.10
  232.9 63.3 all-gather.12
  298.5 67.9 reduce-scatter.4
  368.7 131.4 reduce-scatter.8
  507.9 70.9 reduce-scatter.10
  586.0 38.8 reduce-scatter.6

commit v5 on v4

--- a/solution.py
+++ b/solution.py
@@ -378,10 +378,44 @@
     )
 
 
+def rows_kernel(upstream_ref, down_ref, gate_ref, up_ref, rows_out):
+    tile = gate_ref.shape[1]
+    hidden = rows_out.shape[1] // 2
+    grad = lax.dot_general(
+        upstream_ref[...], down_ref[...], (((1,), (1,)), ((), ())), preferred_element_type=F32
+    )
+    value, slope = gelu_parts(gate_ref[...])
+    at = pl.multiple_of(pl.program_id(0) * tile, tile)
+    rows_out[:, pl.ds(at, tile)] = (grad * up_ref[...] * slope).astype(BF)
+    rows_out[:, pl.ds(hidden + at, tile)] = (grad * value).astype(BF)
+
+
+def mlp_rows(upstream, down, gate_up):
+    total, width = upstream.shape
+    hidden = down.shape[0]
+    tile = BW
+    half = hidden // tile
+    return pl.pallas_call(
+        rows_kernel,
+        grid=(half,),
+        in_specs=[
+            whole(upstream.shape),
+            pl.BlockSpec((tile, width), lambda j: (j, 0)),
+            pl.BlockSpec((total, tile), lambda j: (0, j)),
+            pl.BlockSpec((total, tile), lambda j: (0, half + j)),
+        ],
+        out_specs=whole((total, 2 * hidden)),
+        out_shape=jax.ShapeDtypeStruct((total, 2 * hidden), BF),
+        compiler_params=pltpu.CompilerParams(vmem_limit_bytes=48 * 1024 * 1024),
+        cost_estimate=pl.CostEstimate(flops=1000, bytes_accessed=1000, transcendentals=0),
+        name="mlp_rows",
+    )(upstream, down, gate_up, gate_up)
+
+
 def stream_back_kernel(
-    rows_ref, stream_ref, gain_ref, upstream_ref, weight_far, hidden_far, down_far,
-    grad_out, low_out, gain_out, feed_out,
-    weight_ref, hidden_ref, down_ref, fetches,
+    rows_ref, stream_ref, gain_ref, upstream_ref, weight_far, hidden_far, down_far, out_far,
+    grad_out, low_out, gain_out, feed_out, mixed_out,
+    weight_ref, hidden_ref, down_ref, out_ref, fetches,
     acc, sent, got, sends, recvs,
 ):
     rows, width = stream_ref.shape
@@ -397,6 +431,7 @@
     late = [
         pltpu.make_async_copy(hidden_far, hidden_ref, fetches.at[count]),
         pltpu.make_async_copy(down_far, down_ref, fetches.at[count + 1]),
+        pltpu.make_async_copy(out_far, out_ref, fetches.at[count + 2]),
     ]
     for copy in late:
         copy.start()
@@ -429,16 +464,32 @@
     def feed_block(k):
         feed(k, lambda cols, value: feed_out.__setitem__((k, slice(None), cols), value.astype(BF)))
 
+    def mixed_block(k):
+        mixed_out[k] = lax.dot_general(
+            low_out[k], out_ref[...], (((1,), (1,)), ((), ())), preferred_element_type=F32
+        )
+
     feed_block(3)
     gathered = pass_on(send, 6, low_out, gathered)
-    for k in range(3):
-        feed_block(k)
-    settle(gathered)
+    feed_block(0)
+    mixed_block(0)
+    feed_block(1)
+    feed_block(2)
+    near_low, side_high, near_high, side_low, far_low, far_high = gathered
+    near_high.wait_recv()
+    mixed_block(1)
+    side_low.wait_recv()
+    mixed_block(2)
+    far_low.wait_recv()
+    far_high.wait_recv()
+    mixed_block(3)
+    for copy in gathered:
+        copy.wait_send()
     for copy in copies:
         copy.wait_send()
 
 
-def stream_back(rows_all, weight, stream, gain, upstream, hidden, down):
+def stream_back(rows_all, weight, stream, gain, upstream, hidden, down, out_rows):
     rows, width = stream.shape
     groups = rows_all.shape[0] // rows
     return remote_call(
@@ -450,23 +501,25 @@
             ((groups, rows, width), BF),
             ((8, width), F32),
             ((groups, rows, width), BF),
+            ((groups, rows, out_rows.shape[0]), F32),
         ],
-        (rows_all, stream, gain, upstream, weight, hidden, down),
+        (rows_all, stream, gain, upstream, weight, hidden, down, out_rows),
         [
             pltpu.VMEM(weight.shape, BF),
             pltpu.VMEM(hidden.shape, BF),
             pltpu.VMEM(down.shape, BF),
-            pltpu.SemaphoreType.DMA((width // 512 + 2,)),
+            pltpu.VMEM(out_rows.shape, BF),
+            pltpu.SemaphoreType.DMA((width // 512 + 3,)),
         ]
         + exchange_scratch(rows, width, 12),
-        far=3,
+        far=4,
     )
 
 
 def inputs_back_kernel(
-    branch_ref, y_ref, weight_ref, flat_ref, gain_ref, columns_ref,
+    branch_ref, y_ref, weight_ref, flat_ref, gain_ref, mixed_ref, low_ref,
     grad_out, gain_out, columns_out,
-    acc, sent, got, sends, recvs,
+    columns_ref, acc, sent, got, sends, recvs,
 ):
     rows = flat_ref.shape[0]
     s = lax.axis_index("seq")
@@ -498,6 +551,13 @@
 
     def product_and_move(k, store):
         if k == 0:
+            left = mixed_ref[...].T
+            tile = 512
+            for c in range(columns_ref.shape[1] // tile):
+                cols = slice(c * tile, (c + 1) * tile)
+                columns_ref[:, cols] = jnp.dot(
+                    left, low_ref[:, cols], preferred_element_type=F32
+                ).astype(BF)
             for copy in moved:
                 copy.start()
         product(k, store)
@@ -523,16 +583,16 @@
         copy.wait_send()
 
 
-def inputs_back(branch_rows, y_rows, weight, flat, gain, columns):
+def inputs_back(branch_rows, y_rows, weight, flat, gain, mixed, low):
     rows, width = flat.shape
-    count, whole = columns.shape
+    count, columns = mixed.shape[1], low.shape[1]
     return remote_call(
         inputs_back_kernel,
         "inputs_back",
         3,
-        [((rows, width), F32), ((8, width), F32), ((4 * count, whole // 4), BF)],
-        (branch_rows, y_rows, weight, flat, gain, columns),
-        exchange_scratch(rows, width, 9),
+        [((rows, width), F32), ((8, width), F32), ((4 * count, columns // 4), BF)],
+        (branch_rows, y_rows, weight, flat, gain, mixed, low),
+        [pltpu.VMEM((count, columns), BF)] + exchange_scratch(rows, width, 9),
     )
 
 
@@ -1114,6 +1174,44 @@
     return wholes[:count]
 
 
+def finish_kernel(
+    mlp_ref, down_ref, stream_ref, first_ref, result_ref, gelu_ref, branch_ref,
+    gate_out, up_out, down_out, inputs_out, result_out, gelu_out, branch_out,
+):
+    hidden = gate_out.shape[1]
+    gate_out[...] = mlp_ref[:, :hidden].astype(F32)
+    up_out[...] = mlp_ref[:, hidden:].astype(F32)
+    down_out[...] = down_ref[...].astype(F32)
+    inputs_out[...] = stream_ref[...] + first_ref[...]
+    result_out[...] = result_ref[...].astype(BF)
+    gelu_out[...] = gelu_ref[...].astype(F32)
+    branch_out[...] = branch_ref[...].astype(F32)
+
+
+def finish(mlp, down, stream_grad, first_back, result, gelu, branch):
+    steps = max(1, min(8, mlp.shape[0] // 16))
+    half = (mlp.shape[0], mlp.shape[1] // 2)
+    operands = (mlp, down, stream_grad, first_back, result, gelu, branch)
+    outs = [
+        (half, F32), (half, F32), (down.shape, F32), (stream_grad.shape, F32),
+        (result.shape, BF), (gelu.shape, F32), (branch.shape, F32),
+    ]
+
+    def part(shape):
+        return pl.BlockSpec((shape[0] // steps, shape[1]), lambda i: (i, 0))
+
+    return pl.pallas_call(
+        finish_kernel,
+        grid=(steps,),
+        in_specs=[part(v.shape) for v in operands],
+        out_specs=[part(shape) for shape, _unused in outs],
+        out_shape=[jax.ShapeDtypeStruct(shape, kind) for shape, kind in outs],
+        compiler_params=pltpu.CompilerParams(vmem_limit_bytes=48 * 1024 * 1024),
+        cost_estimate=pl.CostEstimate(flops=1000, bytes_accessed=1000, transcendentals=0),
+        name="finish",
+    )(*operands)
+
+
 def body(
     inputs,
     lengths,
@@ -1263,22 +1361,17 @@
         (hidden_low, down_part, upstream_all)
     )
     down_grad = lax.psum_scatter(down_part, "wide", scatter_dimension=1, tiled=True)
-    hidden_grad = contract_last(upstream_low, down_full)
-    gate_rows = (hidden_grad * up_values * gelu_parts(gate)[1]).astype(BF)
-    up_rows = (hidden_grad * gelu_gate).astype(BF)
-    mlp_rows = jnp.concatenate([gate_rows, up_rows], axis=1)
-    mlp_part = contract_rows(normed_two_all, mlp_rows).astype(BF)
-    mlp_rows, mlp_part = lax.optimization_barrier((mlp_rows, mlp_part))
+    rows_all = mlp_rows(upstream_low, down_full, gate_up)
+    mlp_part = contract_rows(normed_two_all, rows_all).astype(BF)
+    rows_all, mlp_part = lax.optimization_barrier((rows_all, mlp_part))
     mlp_grad = lax.psum_scatter(mlp_part, "wide", scatter_dimension=0, tiled=True)
-    stream_grad, stream_low_all, gain_two_grad, feed_parts = stream_back(
-        mlp_rows, mlp_full, stream, gain_two, upstream, hidden_low, down_full
-    )
+    stream_grad, stream_low_all, gain_two_grad, feed_parts, mixed_grad = stream_back(
+        rows_all, mlp_full, stream, gain_two, upstream, hidden_low, down_full, out_rows
+    )
+    mixed_grad = mixed_grad.reshape(total, share)
     gain_two_grad = jnp.sum(gain_two_grad, axis=0)
     stream_low_all = stream_low_all.reshape(total, width)
-    stream_low_all, down_grad = lax.optimization_barrier((stream_low_all, down_grad))
-    mixed_grad = contract_last(stream_low_all, out_rows)
-    out_grad = contract_rows(mixed_low, stream_low_all).astype(BF)
-    mixed_grad, out_grad = lax.optimization_barrier((mixed_grad, out_grad))
+    mixed_grad, down_grad = lax.optimization_barrier((mixed_grad, down_grad))
     position = w * tokens + jnp.arange(tokens, dtype=jnp.int32)
     valid = (position[None, :] < lengths[:, None]).astype(F32).reshape(rows, 1)
     y_rows, branch_rows, forget_win, admit_win, channel_grads, result, squares = middle(
@@ -1315,7 +1408,7 @@
     early_sums = early_sums.reshape(wide, -1, LANES)
     branch_late, early_sums = lax.optimization_barrier((branch_rows, early_sums))
     first_back, gain_one_grad, out_cols = inputs_back(
-        branch_late, y_rows, x_y_cols, flat_low, gain_one, out_grad
+        branch_late, y_rows, x_y_cols, flat_low, gain_one, mixed_low, stream_low_all
     )
     out_sum = sum_over_wide(out_cols)
     late_sums = jnp.sum(gain_one_grad, axis=0).reshape(wide, dw)
@@ -1341,14 +1434,17 @@
     gain_two_sum = sums[8 * rw : 8 * rw + dw]
     totals = sums[8 * rw + dw : 8 * rw + dw + 4]
     statistics = jnp.sqrt(totals[0:3] / (totals[3] * width))
+    gate_grad, up_grad, down_grad, inputs_grad, output, gelu_whole, branch_whole = finish(
+        mlp_grad, down_grad, stream_grad, first_back, result, gelu_whole, branch_whole
+    )
     earlier = lax.optimization_barrier(
         (
             out_sum,
-            result.astype(BF).reshape(seqs, tokens, width),
-            (stream_grad + first_back).reshape(seqs, tokens, width),
+            output.reshape(seqs, tokens, width),
+            inputs_grad.reshape(seqs, tokens, width),
             gain_one_sum,
-            gelu_whole.astype(F32),
-            branch_whole.astype(F32),
+            gelu_whole,
+            branch_whole,
             gates_whole[:, :BW].astype(F32),
             gates_whole[:, BW:].astype(F32),
             channel_sums[0],
@@ -1357,9 +1453,9 @@
             channel_sums[4:8],
             channel_sums[3],
             gain_two_sum,
-            mlp_grad[:, :hidden_units].astype(F32),
-            mlp_grad[:, hidden_units:].astype(F32),
-            down_grad.astype(F32),
+            gate_grad,
+            up_grad,
+            down_grad,
             statistics,
         )
     )

time: 679 us -> 670 us (0.987)
  matrix products: 89.4 us -> 59.9 us
  Pallas kernels: 421 us -> 447 us
  other arithmetic: 50.8 us -> 34.6 us
  starting transfers between devices: 12.3 us -> 23.1 us
    pallas_call x0 -> x2, Pallas kernels: none -> 26.2 us  [the longest x1 17.4 us: mlp_rows(): pl.pallas_call(rows_kernel, grid=(half,), in_specs=[whole(upstream.shape)...]
    dot_general x2 -> x0, matrix products: 22.2 us -> none  [contract_last(): lax.dot_general(left, right, (((1,), (1,)), ((), ())), preferred_element_...]
    convert_element_type x5 -> x0, other arithmetic: 11.1 us -> none  [the longest x1 3.11 us: body(): gelu_whole.astype(F32)]
    reduce_scatter x1, starting transfers between devices: 0.21 us -> 11.2 us  [body(): lax.psum_scatter(mlp_part, 'wide', scatter_dimension=0, tiled=True)]
    dot_general x3 -> x2, matrix products: 36.7 us -> 29.5 us  [contract_rows(): lax.dot_general(left, right, (((0,), (0,)), ((), ())), preferred_element_...]
    unnamed x100 -> x92, local copies, waits for them, and re-layouts: 23.4 us -> 26.3 us
  transfers between devices with their start and end apart: 18 -> 18, of which waited for: 1 -> 0; matrix products, arithmetic and copies ran while one was open for 25% -> 18% of each run, Pallas kernels for 61% -> 65%
where the time goes in v5:
time: 670 us; the launch traced here: 660 us
  Pallas kernels  447 us (67%)
  matrix products  59.9 us (9%)
  local copies, waits for them, and re-layouts  42.7 us (6%)
  blocking collectives  36.1 us (5%)
  other arithmetic  34.6 us (5%)
  starting transfers between devices  23.1 us (3%)
  between operations  16 us (2%)
    pallas_call x6, Pallas kernels, remote_call(): pl.pallas_call(kernel, in_specs=[pl.BlockSpec(memory_space=pltpu.VMEM)] *...  343 us
    pallas_call x1, Pallas kernels, middle(): pl.pallas_call(middle_kernel, in_specs=[vmem] * 12 + [anywhere] * 6, out_...  50.1 us
    dot_general x3, matrix products, dot(): return jnp.dot(left, right, preferred_element_type=F32)  30.4 us
    dot_general x2, matrix products, contract_rows(): lax.dot_general(left, right, (((0,), (0,)), ((), ())), preferred_element_...  29.5 us
    unnamed x92, local copies, waits for them, and re-layouts  26.3 us
    all_gather x1, blocking collectives, body(): ends = lax.all_gather(ends, 'wide')[:, :, :, 0]  18.7 us
    all_gather x1, blocking collectives, body(): small = lax.all_gather(small, 'wide')  17.5 us
    pallas_call x1, Pallas kernels, mlp_rows(): pl.pallas_call(rows_kernel, grid=(half,), in_specs=[whole(upstream.shape)...  17.4 us
  transfers between devices with their start and end apart: 18, of which 0 were waited for; matrix products, arithmetic and copies ran while one was open for 18% of the time, Pallas kernels for 65%

profile of v5, /device:TPU:0, one launch (start us, length us, event | category | flops | bytes accessed | tf_op | source)
XLA Modules:
  0.0 660.1 jit_solution(8778715203672507507)
XLA Ops:
  11.7 2.6 pad_maximum_fusion.1
  14.4 47.1 %start.1 = (bf16[4,256,2048]{2,1,0:T(8,128)(2,1)}, bf16[4,32,2048]{2,1,0:T(8,128)(2,1)}) custom-call(bf16[256,2048]{1,0:T(8,128)(2,1)} %bitcast.361), custom_call_target="tpu_custom_call" | custom-call | flops 1000 | bytes 1000 | tf_op jit(solution)/shard_map/start/pallas_call | solution.py:353
  65.0 17.5 %all-gather = bf16[2752,128]{1,0:T(8,128)(2,1)S(1)} all-gather(bf16[344,128]{1,0:T(8,128)(2,1)S(1)} %pad_maximum_fusion.4), channel_id=2, replica_groups=mesh['seq'=4,'wide'=8] {'wide'}, dimensions={0}, use_global_device_ids=true | all-gather | bytes 792576 | tf_op jit(solution)/shard_map/all_gather | solution.py:1285
  88.7 3.1 multiply_reduce_fusion
  92.1 5.3 fusion.1.normed_ref
  111.7 10.4 %fusion.51 = f32[1024,1408]{1,0:T(8,128)S(1)} fusion(bf16[1024,2048]{1,0:T(8,128)(2,1)} %fusion.1.normed_ref, bf16[2048,1408]{1,0:T(8,128)(2,1)} %all-gather.7.cloned.1.call-done.weight_ref), kind=kOutput, calls=%fused_computation.152 | convolution fusion | flops 5905580032 | bytes 15728640 | tf_op jit(solution)/shard_map/dot_general | solution.py:21
  130.5 2.9 fusion.24
  133.5 12.8 %temporal_forward.1 = (bf16[1024,640]{1,0:T(8,128)(2,1)S(1)}, bf16[1024,640]{1,0:T(8,128)(2,1)S(1)}, f32[1024,640]{1,0:T(8,128)}, f32[1024,640]{1,0:T(8,128)}, f...) custom-call(s32[1]{0:T(128)} %bitcast.off_ref, bf16[1024,768]{1,0:T(8,128)(2,1)S(1)} %slice.289.x_ref.x_far, ...), custom_call_target="tpu_custom_call" | custom-call | flops 1000 | bytes 1000 | tf_op jit(solution)/shard_map/temporal_forward/pallas_call | solution.py:139
  146.3 18.7 %all-gather.1 = f32[64,2,1,640]{3,1,2,0:T(2,128)S(1)} all-gather(f32[8,2,1,640]{3,1,2,0:T(2,128)S(1)} %copy.88), channel_id=3, replica_groups=mesh['seq'=4,'wide'=8] {'wide'}, dimensions={0}, use_global_device_ids=true | all-gather | bytes 368640 | tf_op jit(solution)/shard_map/all_gather | solution.py:1341
  165.0 6.4 fusion.50
  177.7 82.2 %stream_and_norm.1 = (f32[256,2048]{1,0:T(8,128)}, f32[256,2048]{1,0:T(8,128)}, bf16[4,256,2048]{2,1,0:T(8,128)(2,1)}) custom-call(bf16[1024,640]{1,0:T(8,128)(2,1)} %get-tuple-element.181.mixed_ref, bf16[640,2048]{1,0:T(8,128)(2,1)} %pad_maximum_fusion.weight_ref.out_far, bf16[256,2048]{1,0:T(8,128)(2,1)} %bitcast.362, f32[1,2048]{1,0:T(1,128)} %bitcast.386), custom_call_target="tpu_custom_call" | custom-call | flops 1000 | bytes 1000 | tf_op jit(solution)/shard_map/stream_and_norm/pallas_call | solution.py:353
  259.9 17.2 %fusion.52.gate_ref.up_ref = f32[1024,3072]{1,0:T(8,128)S(1)} fusion(bf16[1024,2048]{1,0:T(8,128)(2,1)} %bitcast.395, bf16[2048,3072]{1,0:T(8,128)(2,1)} %all-gather.11.cloned.1.call-done.weight_far), kind=kOutput, calls=%fused_computation.153 | convolution fusion | flops 12884901888 | bytes 29360128 | tf_op jit(solution)/shard_map/dot_general | solution.py:21
  283.2 10.9 %convolution_convert_fusion.1 = bf16[1536,2048]{1,0:T(8,128)(2,1)} fusion(bf16[1024,1536]{1,0:T(8,128)(2,1)S(1)} %fusion.10.hidden_far, bf16[1024,2048]{1,0:T(8,128)(2,1)} %constant_dynamic-update-slice_fusion.upstream_ref), kind=kOutput, calls=%fused_computation.6 | convolution fusion | flops 6445596672 | bytes 13631488 | tf_op jit(solution)/shard_map/dot_general | solution.py:29
  294.2 11.2 %reduce-scatter.9.cloned.1.call-start = ((), (), s32[]{:S(2)}) async-start(), calls=%async_computation.10 | async-start | bytes 14155776 | tf_op jit(solution)/shard_map/reduce_scatter | solution.py:1367
  305.5 17.4 %mlp_rows.1.rows_ref = bf16[1024,3072]{1,0:T(8,128)(2,1)} custom-call(bf16[1024,2048]{1,0:T(8,128)(2,1)} %constant_dynamic-update-slice_fusion.upstream_ref, bf16[1536,2048]{1,0:T(8,128)(2,1)} %all-gather.13.cloned.1.call-done.down_ref.down_far, f32[1024,3072]{1,0:T(8,128)} %copy-done.16, f32[1024,3072]{1,0:T(8,128)} %copy-done.16), custom_call_target="tpu_custom_call" | custom-call | flops 1000 | bytes 1000 | tf_op jit(solution)/shard_map/mlp_rows/pallas_call | solution.py:398
  322.8 18.5 %convolution_convert_fusion = bf16[2048,3072]{1,0:T(8,128)(2,1)} fusion(bf16[1024,2048]{1,0:T(8,128)(2,1)S(1)} %bitcast.396, bf16[1024,3072]{1,0:T(8,128)(2,1)} %mlp_rows.1.rows_ref), kind=kOutput, calls=%fused_computation | convolution fusion | flops 12891193344 | bytes 23068672 | tf_op jit(solution)/shard_map/dot_general | solution.py:29
  344.3 87.2 %stream_back.1 = (f32[256,2048]{1,0:T(8,128)}, bf16[4,256,2048]{2,1,0:T(8,128)(2,1)}, f32[8,2048]{1,0:T(8,128)}, bf16[4,256,2048]{2,1,0:T(8,128)(2,1)}, f32[4,256,640]{2,1,0:T(8,128)}) custom-call(bf16[1024,3072]{1,0:T(8,128)(2,1)} %mlp_rows.1.rows_ref, f32[256,2048]{1,0:T(8,128)} %get-tuple-element.115.stream_ref.stream_far, f32[1,2048]{1,0:T(1,128)} %bitcast.387, ...), custom_call_target="tpu_custom_call" | custom-call | flops 1000 | bytes 1000 | tf_op jit(solution)/shard_map/stream_back/pallas_call | solution.py:353
  431.5 50.1 %middle.1 = (bf16[1024,640]{1,0:T(8,128)(2,1)}, bf16[1024,768]{1,0:T(8,128)(2,1)}, bf16[1024,768]{1,0:T(8,128)(2,1)}, bf16[1024,768]{1,0:T(8,128)(2,1)}, f32[8,6...) custom-call(f32[1024,640]{1,0:T(8,128)} %bitcast.378, f32[1024,640]{1,0:T(8,128)} %get-tuple-element.180.y_ref, ...), custom_call_target="tpu_custom_call" | custom-call | flops 1000 | bytes 1000 | tf_op jit(solution)/shard_map/middle/pallas_call | solution.py:896
  485.8 15.7 %temporal_grads.1 = bf16[8,3136,128]{2,1,0:T(8,128)(2,1)} custom-call(bf16[1024,2048]{1,0:T(8,128)(2,1)} %fusion.1.normed_ref, bf16[1024,640]{1,0:T(8,128)(2,1)S(1)} %copy-done.6, bf16[1024,768]{1,0:T(8,128)(2,1)S(1)} %copy-done.5, bf16[1024,768]{1,0:T(8,128)(2,1)S(1)} %copy-done.3, bf16[1024,768]{1,0:T(8,128)(2,1)S(1)} %copy-done.8, ...), custom_call_target="tpu_custom_call" | custom-call | flops 1000 | bytes 1000 | tf_op jit(solution)/shard_map/temporal_grads/pallas_call | solution.py:1017
  504.8 76.0 %inputs_back.1 = (f32[256,2048]{1,0:T(8,128)}, f32[8,2048]{1,0:T(8,128)}, bf16[2560,512]{1,0:T(8,128)(2,1)}) custom-call(bf16[1024,768]{1,0:T(8,128)(2,1)} %get-tuple-element.130.branch_ref, bf16[1024,640]{1,0:T(8,128)(2,1)} %get-tuple-element.131.y_ref, bf16[2048,1408]{1,0:T(8,128)(2,1)} %all-gather.7.cloned.1.call-done.weight_ref, ...), custom_call_target="tpu_custom_call" | custom-call | flops 1000 | bytes 1000 | tf_op jit(solution)/shard_map/inputs_back/pallas_call | solution.py:353
  582.4 34.8 %spread.1 = (bf16[256,2560]{1,0:T(8,128)(2,1)}, bf16[256,2560]{1,0:T(8,128)(2,1)}, bf16[320,512]{1,0:T(8,128)(2,1)}, f32[32,128]{1,0:T(8,128)}) custom-call(bf16[3136,128]{1,0:T(8,128)(2,1)} %bitcast.379, f32[8,24,128]{2,1,0:T(8,128)} %bitcast.380, f32[8,8,128]{2,1,0:T(8,128)} %bitcast.385), custom_call_target="tpu_custom_call" | custom-call | flops 1000 | bytes 1000 | tf_op jit(solution)/shard_map/spread/pallas_call | solution.py:353
  621.0 8.8 %finish.1 = (f32[256,1536]{1,0:T(8,128)}, f32[256,1536]{1,0:T(8,128)}, f32[1536,256]{1,0:T(8,128)}, f32[256,2048]{1,0:T(8,128)}, bf16[256,2048]{1,0:T(8,128)(2,1...) custom-call(bf16[256,3072]{1,0:T(8,128)(2,1)S(1)} %copy-done.9, bf16[1536,256]{1,0:T(8,128)(2,1)S(1)} %copy-done.14, ...), custom_call_target="tpu_custom_call" | custom-call | flops 1000 | bytes 1000 | tf_op jit(solution)/shard_map/finish/pallas_call | solution.py:1203
  634.4 15.3 %spread_last.1 = bf16[320,2048]{1,0:T(8,128)(2,1)} custom-call(bf16[320,512]{1,0:T(8,128)(2,1)} %reduce-scatter.7.cloned.1.call-done.columns_ref), custom_call_target="tpu_custom_call" | custom-call | flops 1000 | bytes 1000 | tf_op jit(solution)/shard_map/spread_last/pallas_call | solution.py:353
  649.7 3.1 convert_element_type.99
  (198 shorter events, 68.9 us)
Async XLA Ops:
  7.2 104.4 %all-gather.7.cloned.1.call-start = ((), (), s32[]{:S(2)}) async-start(), calls=%async_computation.4 | async-start | bytes 6488064 | tf_op jit(solution)/shard_map/all_gather | solution.py:1262
  8.8 52.7 %copy-start.31 = (bf16[320]{0:T(512)(128)(2,1)S(1)}, bf16[320]{0:T(512)(128)(2,1)}, u32[]{:S(2)}) copy-start(bf16[320]{0:T(512)(128)(2,1)} %param.25) | copy-start | bytes 1924
  8.8 52.7 %copy-start.32 = (bf16[320]{0:T(512)(128)(2,1)S(1)}, bf16[320]{0:T(512)(128)(2,1)}, u32[]{:S(2)}) copy-start(bf16[320]{0:T(512)(128)(2,1)} %param.26) | copy-start | bytes 1924
  8.9 52.7 %copy-start.33 = (bf16[320]{0:T(512)(128)(2,1)S(1)}, bf16[320]{0:T(512)(128)(2,1)}, u32[]{:S(2)}) copy-start(bf16[320]{0:T(512)(128)(2,1)} %param.27) | copy-start | bytes 1924
  8.9 52.7 %copy-start.34 = (bf16[320]{0:T(512)(128)(2,1)S(1)}, bf16[320]{0:T(512)(128)(2,1)}, u32[]{:S(2)}) copy-start(bf16[320]{0:T(512)(128)(2,1)} %param.29) | copy-start | bytes 1924
  8.9 52.8 %copy-start.25 = (bf16[320,256]{1,0:T(8,128)(2,1)S(1)}, bf16[320,256]{1,0:T(8,128)(2,1)}, u32[]{:S(2)}) copy-start(bf16[320,256]{1,0:T(8,128)(2,1)} %param.23) | copy-start | bytes 491524
  8.9 52.8 %copy-start.26 = (bf16[320,256]{1,0:T(8,128)(2,1)S(1)}, bf16[320,256]{1,0:T(8,128)(2,1)}, u32[]{:S(2)}) copy-start(bf16[320,256]{1,0:T(8,128)(2,1)} %param.24) | copy-start | bytes 491524
  9.9 115.0 %all-gather.9.cloned.1.call-start = ((), (), s32[]{:S(2)}) async-start(), calls=%async_computation.5 | async-start | bytes 2949120 | tf_op jit(solution)/shard_map/all_gather | solution.py:1293
  11.7 248.2 %all-gather.11.cloned.1.call-start = ((), (), s32[]{:S(2)}) async-start(), calls=%async_computation.6 | async-start | bytes 14155776 | tf_op jit(solution)/shard_map/all_gather | solution.py:1296
  14.3 291.1 %all-gather.13.cloned.1.call-start = ((), (), s32[]{:S(2)}) async-start(), calls=%async_computation.7 | async-start | bytes 7077888 | tf_op jit(solution)/shard_map/all_gather | solution.py:1299
  62.9 37.6 %collective-permute-start.1 = (bf16[256,2048]{1,0:T(8,128)(2,1)S(1)}, bf16[256,2048]{1,0:T(8,128)(2,1)}, u32[]{:S(2)}, u32[]{:S(2)}) collective-permute-start(bf16[256,2048]{1,0:T(8,128)(2,1)S(1)} %bitcast.366), channel_id=1, source_target_pairs={{0,16},{8,24},{16,0},{24,8},{1,17},{9,25},{17,1},{25,9},{2,18},{10... | collective-permute-start | bytes 3145736 | tf_op jit(solution)/shard_map/ppermute | solution.py:33
  63.6 36.9 %collective-permute-start = (bf16[256,2048]{1,0:T(8,128)(2,1)S(1)}, bf16[256,2048]{1,0:T(8,128)(2,1)}, u32[]{:S(2)}, u32[]{:S(2)}) collective-permute-start(bf16[256,2048]{1,0:T(8,128)(2,1)S(1)} %bitcast.367), channel_id=1, source_target_pairs={{0,8},{8,0},{16,24},{24,16},{1,9},{9,1},{17,25},{25,17},{2,10},{10... | collective-permute-start | bytes 3145736 | tf_op jit(solution)/shard_map/ppermute | solution.py:33
  84.3 14.9 %collective-permute-start.6 = (bf16[768,128]{1,0:T(8,128)(2,1)}, bf16[768,128]{1,0:T(8,128)(2,1)S(1)}, u32[]{:S(2)}, u32[]{:S(2)}) collective-permute-start(bf16[768,128]{1,0:T(8,128)(2,1)} %get-tuple-element.193), channel_id=1, source_target_pairs={{0,8},{8,0},{16,24},{24,16},{1,9},{9,1},{17,25},{25,17},{2,10},{10... | collective-permute-start | bytes 589832 | tf_op jit(solution)/shard_map/ppermute | solution.py:33
  85.2 14.0 %collective-permute-start.5 = (bf16[768,128]{1,0:T(8,128)(2,1)}, bf16[768,128]{1,0:T(8,128)(2,1)S(1)}, u32[]{:S(2)}, u32[]{:S(2)}) collective-permute-start(bf16[768,128]{1,0:T(8,128)(2,1)} %get-tuple-element.194), channel_id=1, source_target_pairs={{0,16},{8,24},{16,0},{24,8},{1,17},{9,25},{17,1},{25,9},{2,18},{10... | collective-permute-start | bytes 589832 | tf_op jit(solution)/shard_map/ppermute | solution.py:33
  86.7 12.5 %collective-permute-start.4 = (bf16[768,128]{1,0:T(8,128)(2,1)}, bf16[768,128]{1,0:T(8,128)(2,1)}, u32[]{:S(2)}, u32[]{:S(2)}) collective-permute-start(bf16[768,128]{1,0:T(8,128)(2,1)} %get-tuple-element.195), channel_id=1, source_target_pairs={{0,24},{8,16},{16,8},{24,0},{1,25},{9,17},{17,9},{25,1},{2,26},{10... | collective-permute-start | bytes 589832 | tf_op jit(solution)/shard_map/ppermute | solution.py:33
  87.8 343.7 %reduce-scatter.5.cloned.1.call-start = ((), (), s32[]{:S(2)}) async-start(), calls=%async_computation.8 | async-start | bytes 7077888 | tf_op jit(solution)/shard_map/reduce_scatter | solution.py:1363
  106.9 17.9 %collective-permute-start.3 = (bf16[128,2048]{1,0:T(8,128)(2,1)}, bf16[128,2048]{1,0:T(8,128)(2,1)S(1)}, u32[]{:S(2)}, u32[]{:S(2)}) collective-permute-start(bf16[128,2048]{1,0:T(8,128)(2,1)} %slice.147), channel_id=1, source_target_pairs={{0,8},{8,0},{16,24},{24,16},{1,9},{9,1},{17,25},{25,17},{2,10},{10... | collective-permute-start | bytes 1572872 | tf_op jit(solution)/shard_map/ppermute | solution.py:33
  107.8 17.0 %collective-permute-start.2 = (bf16[128,2048]{1,0:T(8,128)(2,1)}, bf16[128,2048]{1,0:T(8,128)(2,1)}, u32[]{:S(2)}, u32[]{:S(2)}) collective-permute-start(bf16[128,2048]{1,0:T(8,128)(2,1)} %slice.146), channel_id=1, source_target_pairs={{0,16},{8,24},{16,0},{24,8},{1,17},{9,25},{17,1},{25,9},{2,18},{10... | collective-permute-start | bytes 1572872 | tf_op jit(solution)/shard_map/ppermute | solution.py:33
  127.0 47.2 %collective-permute-start.9 = (bf16[640,512]{1,0:T(8,128)(2,1)S(1)}, bf16[640,512]{1,0:T(8,128)(2,1)S(1)}, u32[]{:S(2)}, u32[]{:S(2)}) collective-permute-start(bf16[640,512]{1,0:T(8,128)(2,1)S(1)} %get-tuple-element.186), channel_id=1, source_target_pairs={{0,8},{8,0},{16,24},{24,16},{1,9},{9,1},{17,25},{25,17},{2,10},{10... | collective-permute-start | bytes 1966088 | tf_op jit(solution)/shard_map/ppermute | solution.py:33
  128.1 46.1 %collective-permute-start.8 = (bf16[640,512]{1,0:T(8,128)(2,1)S(1)}, bf16[640,512]{1,0:T(8,128)(2,1)S(1)}, u32[]{:S(2)}, u32[]{:S(2)}) collective-permute-start(bf16[640,512]{1,0:T(8,128)(2,1)S(1)} %get-tuple-element.187), channel_id=1, source_target_pairs={{0,16},{8,24},{16,0},{24,8},{1,17},{9,25},{17,1},{25,9},{2,18},{10... | collective-permute-start | bytes 1966088 | tf_op jit(solution)/shard_map/ppermute | solution.py:33
  129.2 44.9 %collective-permute-start.7 = (bf16[640,512]{1,0:T(8,128)(2,1)S(1)}, bf16[640,512]{1,0:T(8,128)(2,1)S(1)}, u32[]{:S(2)}, u32[]{:S(2)}) collective-permute-start(bf16[640,512]{1,0:T(8,128)(2,1)S(1)} %get-tuple-element.188), channel_id=1, source_target_pairs={{0,24},{8,16},{16,8},{24,0},{1,25},{9,17},{17,9},{25,1},{2,26},{10... | collective-permute-start | bytes 1966088 | tf_op jit(solution)/shard_map/ppermute | solution.py:33
  294.2 207.4 %reduce-scatter.9.cloned.1.call-start = ((), (), s32[]{:S(2)}) async-start(), calls=%async_computation.10 | async-start | bytes 14155776 | tf_op jit(solution)/shard_map/reduce_scatter | solution.py:1367
  341.4 241.0 %reduce-scatter.11.cloned.1.call-start = ((), (), s32[]{:S(2)}) async-start(), calls=%async_computation.11 | async-start | bytes 7225344 | tf_op jit(solution)/shard_map/reduce_scatter | solution.py:1392
  501.6 132.7 %reduce-scatter.7.cloned.1.call-start = ((), (), s32[]{:S(2)}) async-start(), calls=%async_computation.9 | async-start | bytes 2949120 | tf_op jit(solution)/shard_map/reduce_scatter | solution.py:1392
  (33 other events, 595.9 us)
Sparse Core Ops, SparseCore 0:
  10.3 65.2 all-gather.6
  77.8 33.0 all-gather.8
  113.1 118.3 all-gather.10
  232.9 63.3 all-gather.12
  298.5 67.9 reduce-scatter.4
  368.7 131.5 reduce-scatter.8
  502.6 69.3 reduce-scatter.10
  580.9 37.5 reduce-scatter.6

commit v6 on v5

--- a/solution.py
+++ b/solution.py
@@ -162,7 +162,7 @@
         scratch_shapes=[
             pltpu.VMEM((2, tokens, window), F32),
         ],
-        compiler_params=pltpu.CompilerParams(vmem_limit_bytes=48 * 1024 * 1024),
+        compiler_params=pltpu.CompilerParams(vmem_limit_bytes=60 * 1024 * 1024),
         cost_estimate=pl.CostEstimate(flops=1000, bytes_accessed=1000, transcendentals=0),
         name="temporal_forward",
     )(off, x_win, edge, gates, chan)
@@ -406,7 +406,7 @@
         ],
         out_specs=whole((total, 2 * hidden)),
         out_shape=jax.ShapeDtypeStruct((total, 2 * hidden), BF),
-        compiler_params=pltpu.CompilerParams(vmem_limit_bytes=48 * 1024 * 1024),
+        compiler_params=pltpu.CompilerParams(vmem_limit_bytes=60 * 1024 * 1024),
         cost_estimate=pl.CostEstimate(flops=1000, bytes_accessed=1000, transcendentals=0),
         name="mlp_rows",
     )(upstream, down, gate_up, gate_up)
@@ -517,11 +517,26 @@
 
 
 def inputs_back_kernel(
-    branch_ref, y_ref, weight_ref, flat_ref, gain_ref, mixed_ref, low_ref,
+    branch_ref, y_ref, flat_ref, gain_ref, weight_far, mixed_far, low_far,
     grad_out, gain_out, columns_out,
-    columns_ref, acc, sent, got, sends, recvs,
+    weight_ref, mixed_ref, low_ref, fetches, columns_ref, acc, sent, got, sends, recvs,
 ):
     rows = flat_ref.shape[0]
+    tile = 512
+    parts = weight_ref.shape[0] // tile
+
+    def fetch(c):
+        part = pl.ds(pl.multiple_of(c * tile, tile), tile)
+        return pltpu.make_async_copy(weight_far.at[part], weight_ref.at[part], fetches.at[c])
+
+    for c in range(parts):
+        fetch(c).start()
+    late = [
+        pltpu.make_async_copy(mixed_far, mixed_ref, fetches.at[parts]),
+        pltpu.make_async_copy(low_far, low_ref, fetches.at[parts + 1]),
+    ]
+    for copy in late:
+        copy.start()
     s = lax.axis_index("seq")
     count, columns = columns_ref.shape[0], columns_out.shape[1]
     barrier = pltpu.get_barrier_semaphore()
@@ -547,12 +562,15 @@
         moved.append(copy)
     window = branch_ref.shape[1]
     weights = [weight_ref.at[:, :window], weight_ref.at[:, window:]]
-    product = product_of([branch_ref, y_ref], weights, True, rows, 512)
+    product = product_of(
+        [branch_ref, y_ref], weights, True, rows, tile, ready=lambda c: fetch(c).wait()
+    )
 
     def product_and_move(k, store):
         if k == 0:
+            for copy in late:
+                copy.wait()
             left = mixed_ref[...].T
-            tile = 512
             for c in range(columns_ref.shape[1] // tile):
                 cols = slice(c * tile, (c + 1) * tile)
                 columns_ref[:, cols] = jnp.dot(
@@ -591,8 +609,16 @@
         "inputs_back",
         3,
         [((rows, width), F32), ((8, width), F32), ((4 * count, columns // 4), BF)],
-        (branch_rows, y_rows, weight, flat, gain, mixed, low),
-        [pltpu.VMEM((count, columns), BF)] + exchange_scratch(rows, width, 9),
+        (branch_rows, y_rows, flat, gain, weight, mixed, low),
+        [
+            pltpu.VMEM(weight.shape, BF),
+            pltpu.VMEM(mixed.shape, BF),
+            pltpu.VMEM(low.shape, BF),
+            pltpu.SemaphoreType.DMA((width // 512 + 2,)),
+            pltpu.VMEM((count, columns), BF),
+        ]
+        + exchange_scratch(rows, width, 9),
+        far=3,
     )
 
 
@@ -1029,7 +1055,7 @@
             pltpu.SemaphoreType.DMA((4,)),
         ],
         compiler_params=pltpu.CompilerParams(
-            collective_id=9, has_side_effects=True, vmem_limit_bytes=48 * 1024 * 1024
+            collective_id=9, has_side_effects=True, vmem_limit_bytes=60 * 1024 * 1024
         ),
         cost_estimate=pl.CostEstimate(flops=1000, bytes_accessed=1000, transcendentals=0),
         name="temporal_grads",
@@ -1046,14 +1072,6 @@
         for i in range(tiles):
             cols = pl.ds(pl.multiple_of(base + i * LANES, LANES), LANES)
             out[:, cols] += buffer[first + i * count : first + (i + 1) * count, :]
-
-
-def put(k, block, out):
-    columns = block.shape[1]
-    other = at_seq(k)
-    for i in range(columns // LANES):
-        start_col = pl.multiple_of(other * columns + i * LANES, LANES)
-        out[:, pl.ds(start_col, LANES)] = block[:, i * LANES : (i + 1) * LANES]
 
 
 def spread_kernel(plan, parts_ref, early_ref, late_ref, *refs):
@@ -1145,35 +1163,6 @@
     )
 
 
-def last_kernel(columns_ref, columns_out, column_blocks, sends, recvs):
-    greet()
-    send = sender(sends, recvs)
-    copies = both_ways(send, 0, columns_ref, column_blocks)
-    put(0, columns_ref, columns_out)
-    copies = pass_on(send, 0, column_blocks, copies)
-    settle(copies)
-    for k in (1, 2, 3):
-        put(k, column_blocks.at[k], columns_out)
-
-
-def spread_last(columns):
-    count = columns.shape[0]
-    columns = jnp.pad(columns, ((0, -count % 32), (0, 0)))
-    (wholes,) = remote_call(
-        last_kernel,
-        "spread_last",
-        5,
-        [((columns.shape[0], 4 * columns.shape[1]), BF)],
-        (columns,),
-        [
-            pltpu.VMEM((4,) + columns.shape, BF),
-            pltpu.SemaphoreType.DMA((6,)),
-            pltpu.SemaphoreType.DMA((6,)),
-        ],
-    )
-    return wholes[:count]
-
-
 def finish_kernel(
     mlp_ref, down_ref, stream_ref, first_ref, result_ref, gelu_ref, branch_ref,
     gate_out, up_out, down_out, inputs_out, result_out, gelu_out, branch_out,
@@ -1206,8 +1195,10 @@
         in_specs=[part(v.shape) for v in operands],
         out_specs=[part(shape) for shape, _unused in outs],
         out_shape=[jax.ShapeDtypeStruct(shape, kind) for shape, kind in outs],
-        compiler_params=pltpu.CompilerParams(vmem_limit_bytes=48 * 1024 * 1024),
-        cost_estimate=pl.CostEstimate(flops=1000, bytes_accessed=1000, transcendentals=0),
+        compiler_params=pltpu.CompilerParams(vmem_limit_bytes=60 * 1024 * 1024),
+        cost_estimate=pl.CostEstimate(
+            flops=8 * result.size, bytes_accessed=24 * 1024 * 1024, transcendentals=0
+        ),
         name="finish",
     )(*operands)
 
@@ -1392,7 +1383,6 @@
         return lax.psum_scatter(values, "wide", scatter_dimension=0, tiled=True)
 
     stacked, mlp_grad = lax.optimization_barrier((stacked, mlp_grad))
-    temporal_sum = sum_over_wide(stacked)
     channel_all = lax.dynamic_update_slice_in_dim(
         jnp.zeros((8, channels), F32), channel_grads, s * share, 1
     )
@@ -1406,7 +1396,8 @@
     )
     early_sums = jnp.pad(early_sums, ((0, 0), (0, -early_sums.shape[1] % (8 * LANES))))
     early_sums = early_sums.reshape(wide, -1, LANES)
-    branch_late, early_sums = lax.optimization_barrier((branch_rows, early_sums))
+    branch_late, early_sums, stacked = lax.optimization_barrier((branch_rows, early_sums, stacked))
+    temporal_sum = sum_over_wide(stacked)
     first_back, gain_one_grad, out_cols = inputs_back(
         branch_late, y_rows, x_y_cols, flat_low, gain_one, mixed_low, stream_low_all
     )
@@ -1434,17 +1425,11 @@
     gain_two_sum = sums[8 * rw : 8 * rw + dw]
     totals = sums[8 * rw + dw : 8 * rw + dw + 4]
     statistics = jnp.sqrt(totals[0:3] / (totals[3] * width))
-    gate_grad, up_grad, down_grad, inputs_grad, output, gelu_whole, branch_whole = finish(
-        mlp_grad, down_grad, stream_grad, first_back, result, gelu_whole, branch_whole
-    )
-    earlier = lax.optimization_barrier(
+    out_sum, gelu_whole = lax.optimization_barrier((out_sum, gelu_whole))
+    result, *vectors = lax.optimization_barrier(
         (
-            out_sum,
-            output.reshape(seqs, tokens, width),
-            inputs_grad.reshape(seqs, tokens, width),
+            result,
             gain_one_sum,
-            gelu_whole,
-            branch_whole,
             gates_whole[:, :BW].astype(F32),
             gates_whole[:, BW:].astype(F32),
             channel_sums[0],
@@ -1453,15 +1438,30 @@
             channel_sums[4:8],
             channel_sums[3],
             gain_two_sum,
-            gate_grad,
-            up_grad,
-            down_grad,
             statistics,
         )
     )
-    out_sum, *outputs = earlier
-    outputs.insert(12, spread_last(out_sum).astype(F32))
-    return tuple(outputs)
+    gain_one_sum, forget_whole, admit_whole, *channel_out, gain_two_sum, statistics = vectors
+    out_whole = jnp.concatenate(in_order(swapped(lambda j: out_sum)), axis=1).astype(F32)
+    gate_grad, up_grad, down_grad, inputs_grad, output, gelu_whole, branch_whole = finish(
+        mlp_grad, down_grad, stream_grad, first_back, result, gelu_whole, branch_whole
+    )
+    return (
+        output.reshape(seqs, tokens, width),
+        inputs_grad.reshape(seqs, tokens, width),
+        gain_one_sum,
+        gelu_whole,
+        branch_whole,
+        forget_whole,
+        admit_whole,
+        *channel_out,
+        out_whole,
+        gain_two_sum,
+        gate_grad,
+        up_grad,
+        down_grad,
+        statistics,
+    )
 
 
 def solution(mesh):

time: 670 us -> 653 us (0.975)
  Pallas kernels: 447 us -> 436 us
  starting transfers between devices: 23.1 us -> 15.4 us
    pallas_call x6 -> x5, Pallas kernels: 343 us -> 325 us  [remote_call(): pl.pallas_call(kernel, in_specs=[pl.BlockSpec(memory_space=pltpu.VMEM)] *...]
    reduce_scatter x1, starting transfers between devices: 11.2 us -> 0.21 us  [body(): lax.psum_scatter(mlp_part, 'wide', scatter_dimension=0, tiled=True)]
    unnamed x92 -> x66, local copies, waits for them, and re-layouts: 26.3 us -> 19.5 us
    ppermute x10 -> x13, starting transfers between devices: 11.6 us -> 14.7 us  [swap(): lax.ppermute(values, 'seq', [(i, i ^ mask) for i in range(lax.axis_size('...]
  transfers between devices with their start and end apart: 18 -> 21, of which waited for: 0 -> 2; matrix products, arithmetic and copies ran while one was open for 18% -> 19% of each run, Pallas kernels for 65% -> 68%
where the time goes in v6:
time: 653 us; the launch traced here: 643 us
  Pallas kernels  436 us (67%)
  matrix products  60.5 us (9%)
  local copies, waits for them, and re-layouts  40.3 us (6%)
  other arithmetic  35.9 us (5%)
  blocking collectives  34 us (5%)
  between operations  15.9 us (2%)
  starting transfers between devices  15.4 us (2%)
    pallas_call x5, Pallas kernels, remote_call(): pl.pallas_call(kernel, in_specs=[pl.BlockSpec(memory_space=pltpu.VMEM)] *...  325 us
    pallas_call x1, Pallas kernels, middle(): pl.pallas_call(middle_kernel, in_specs=[vmem] * 12 + [anywhere] * 6, out_...  48.1 us
    dot_general x2, matrix products, contract_rows(): lax.dot_general(left, right, (((0,), (0,)), ((), ())), preferred_element_...  30.4 us
    dot_general x3, matrix products, dot(): return jnp.dot(left, right, preferred_element_type=F32)  30.1 us
    unnamed x66, local copies, waits for them, and re-layouts  19.5 us
    pallas_call x1, Pallas kernels, temporal_grads(): pl.pallas_call(functools.partial(grads_kernel, bases), grid=(width // BW,...  19.2 us
    pallas_call x1, Pallas kernels, mlp_rows(): pl.pallas_call(rows_kernel, grid=(half,), in_specs=[whole(upstream.shape)...  17.7 us
    all_gather x1, blocking collectives, body(): small = lax.all_gather(small, 'wide')  17.7 us
  transfers between devices with their start and end apart: 21, of which 2 were waited for; matrix products, arithmetic and copies ran while one was open for 19% of the time, Pallas kernels for 68%

profile of v6, /device:TPU:0, one launch (start us, length us, event | category | flops | bytes accessed | tf_op | source)
XLA Modules:
  0.0 643.0 jit_solution(16622064208045262841)
XLA Ops:
  13.1 47.1 %start.1 = (bf16[4,256,2048]{2,1,0:T(8,128)(2,1)}, bf16[4,32,2048]{2,1,0:T(8,128)(2,1)}) custom-call(bf16[256,2048]{1,0:T(8,128)(2,1)} %bitcast.361), custom_call_target="tpu_custom_call" | custom-call | flops 1000 | bytes 1000 | tf_op jit(solution)/shard_map/start/pallas_call | solution.py:353
  63.9 17.7 %all-gather = bf16[2752,128]{1,0:T(8,128)(2,1)S(1)} all-gather(bf16[344,128]{1,0:T(8,128)(2,1)S(1)} %pad_maximum_fusion.4), channel_id=2, replica_groups=mesh['seq'=4,'wide'=8] {'wide'}, dimensions={0}, use_global_device_ids=true | all-gather | bytes 792576 | tf_op jit(solution)/shard_map/all_gather | solution.py:1276
  88.4 3.1 multiply_reduce_fusion
  91.7 5.3 fusion.1.normed_ref
  110.6 10.4 %fusion.51 = f32[1024,1408]{1,0:T(8,128)S(1)} fusion(bf16[1024,2048]{1,0:T(8,128)(2,1)} %fusion.1.normed_ref, bf16[2048,1408]{1,0:T(8,128)(2,1)} %all-gather.7.cloned.1.call-done.weight_far), kind=kOutput, calls=%fused_computation.161 | convolution fusion | flops 5905580032 | bytes 15728640 | tf_op jit(solution)/shard_map/dot_general | solution.py:21
  121.0 3.0 copy-done.5
  125.4 3.0 constant_dynamic-slice_fusion
  131.8 2.5 fusion.24
  135.1 14.3 %temporal_forward.1 = (bf16[1024,640]{1,0:T(8,128)(2,1)}, bf16[1024,640]{1,0:T(8,128)(2,1)}, f32[1024,640]{1,0:T(8,128)}, f32[1024,640]{1,0:T(8,128)}, f32[1024,...) custom-call(s32[1]{0:T(128)} %bitcast.6.off_ref, bf16[1024,768]{1,0:T(8,128)(2,1)} %slice.289.x_ref.x_far, ...), custom_call_target="tpu_custom_call" | custom-call | flops 1000 | bytes 1000 | tf_op jit(solution)/shard_map/temporal_forward/pallas_call | solution.py:139
  150.2 16.3 %all-gather.1 = f32[64,2,1,640]{3,1,2,0:T(2,128)S(1)} all-gather(f32[8,2,1,640]{3,1,2,0:T(2,128)S(1)} %copy.88), channel_id=3, replica_groups=mesh['seq'=4,'wide'=8] {'wide'}, dimensions={0}, use_global_device_ids=true | all-gather | bytes 368640 | tf_op jit(solution)/shard_map/all_gather | solution.py:1332
  166.6 6.4 fusion.50
  179.4 80.9 %stream_and_norm.1 = (f32[256,2048]{1,0:T(8,128)}, f32[256,2048]{1,0:T(8,128)}, bf16[4,256,2048]{2,1,0:T(8,128)(2,1)}) custom-call(bf16[1024,640]{1,0:T(8,128)(2,1)} %get-tuple-element.173.mixed_ref.mixed_far, bf16[640,2048]{1,0:T(8,128)(2,1)} %pad_maximum_fusion.weight_ref.out_far, bf16[256,2048]{1,0:T(8,128)(2,1)} %bitcast.362, f32[1,2048]{1,0:T(1,128)} %bitcast.386), custom_call_target="tpu_custom_call" | custom-call | flops 1000 | bytes 1000 | tf_op jit(solution)/shard_map/stream_and_norm/pallas_call | solution.py:353
  260.3 17.2 %fusion.52.gate_ref.up_ref = f32[1024,3072]{1,0:T(8,128)S(1)} fusion(bf16[1024,2048]{1,0:T(8,128)(2,1)} %bitcast.395, bf16[2048,3072]{1,0:T(8,128)(2,1)} %all-gather.11.cloned.1.call-done.weight_far), kind=kOutput, calls=%fused_computation.162 | convolution fusion | flops 12884901888 | bytes 29360128 | tf_op jit(solution)/shard_map/dot_general | solution.py:21
  283.7 10.9 %convolution_convert_fusion.1 = bf16[1536,2048]{1,0:T(8,128)(2,1)} fusion(bf16[1024,1536]{1,0:T(8,128)(2,1)S(1)} %fusion.10.hidden_far, bf16[1024,2048]{1,0:T(8,128)(2,1)} %constant_dynamic-update-slice_fusion.upstream_ref), kind=kOutput, calls=%fused_computation.6 | convolution fusion | flops 6445596672 | bytes 13631488 | tf_op jit(solution)/shard_map/dot_general | solution.py:29
  294.8 2.5 all-gather.13.cloned.1.call-done.down_ref.down_far
  297.4 17.7 %mlp_rows.1.rows_ref = bf16[1024,3072]{1,0:T(8,128)(2,1)} custom-call(bf16[1024,2048]{1,0:T(8,128)(2,1)} %constant_dynamic-update-slice_fusion.upstream_ref, bf16[1536,2048]{1,0:T(8,128)(2,1)} %all-gather.13.cloned.1.call-done.down_ref.down_far, f32[1024,3072]{1,0:T(8,128)} %copy-done.2, f32[1024,3072]{1,0:T(8,128)} %copy-done.2), custom_call_target="tpu_custom_call" | custom-call | flops 1000 | bytes 1000 | tf_op jit(solution)/shard_map/mlp_rows/pallas_call | solution.py:398
  315.1 19.5 %convolution_convert_fusion = bf16[2048,3072]{1,0:T(8,128)(2,1)} fusion(bf16[1024,2048]{1,0:T(8,128)(2,1)} %bitcast.396, bf16[1024,3072]{1,0:T(8,128)(2,1)} %mlp_rows.1.rows_ref), kind=kOutput, calls=%fused_computation | convolution fusion | flops 12891193344 | bytes 23068672 | tf_op jit(solution)/shard_map/dot_general | solution.py:29
  338.1 90.5 %stream_back.1 = (f32[256,2048]{1,0:T(8,128)}, bf16[4,256,2048]{2,1,0:T(8,128)(2,1)}, f32[8,2048]{1,0:T(8,128)}, bf16[4,256,2048]{2,1,0:T(8,128)(2,1)}, f32[4,256,640]{2,1,0:T(8,128)}) custom-call(bf16[1024,3072]{1,0:T(8,128)(2,1)} %mlp_rows.1.rows_ref, f32[256,2048]{1,0:T(8,128)} %get-tuple-element.111.stream_ref.stream_far, f32[1,2048]{1,0:T(1,128)} %bitcast.387, ...), custom_call_target="tpu_custom_call" | custom-call | flops 1000 | bytes 1000 | tf_op jit(solution)/shard_map/stream_back/pallas_call | solution.py:353
  429.5 48.1 %middle.1 = (bf16[1024,640]{1,0:T(8,128)(2,1)}, bf16[1024,768]{1,0:T(8,128)(2,1)}, bf16[1024,768]{1,0:T(8,128)(2,1)}, bf16[1024,768]{1,0:T(8,128)(2,1)}, f32[8,6...) custom-call(f32[1024,640]{1,0:T(8,128)} %bitcast.378, f32[1024,640]{1,0:T(8,128)} %get-tuple-element.172.y_ref, ...), custom_call_target="tpu_custom_call" | custom-call | flops 1000 | bytes 1000 | tf_op jit(solution)/shard_map/middle/pallas_call | solution.py:922
  477.6 19.2 %temporal_grads.1 = bf16[8,3136,128]{2,1,0:T(8,128)(2,1)} custom-call(bf16[1024,2048]{1,0:T(8,128)(2,1)} %fusion.1.normed_ref, bf16[1024,640]{1,0:T(8,128)(2,1)} %get-tuple-element.122.y_ref, bf16[1024,768]{1,0:T(8,128)(2,1)} %get-tuple-element.134.branch_ref, bf16[1024,768]{1,0:T(8,128)(2,1)} %slice.289.x_ref.x_far, ...), custom_call_target="tpu_custom_call" | custom-call | flops 1000 | bytes 1000 | tf_op jit(solution)/shard_map/temporal_grads/pallas_call | solution.py:1043
  498.7 2.7 reduce-scatter.7.cloned.1.call-done.mlp_ref
  502.7 70.1 %inputs_back.1 = (f32[256,2048]{1,0:T(8,128)}, f32[8,2048]{1,0:T(8,128)}, bf16[2560,512]{1,0:T(8,128)(2,1)}) custom-call(bf16[1024,768]{1,0:T(8,128)(2,1)} %get-tuple-element.134.branch_ref, bf16[1024,640]{1,0:T(8,128)(2,1)} %get-tuple-element.122.y_ref, bf16[256,2048]{1,0:T(8,128)(2,1)} %bitcast.363, f32[1,2048]{1,0:T(1,128)} %bitcast.389, ...), custom_call_target="tpu_custom_call" | custom-call | flops 1000 | bytes 1000 | tf_op jit(solution)/shard_map/inputs_back/pallas_call | solution.py:353
  574.3 36.6 %spread.1 = (bf16[256,2560]{1,0:T(8,128)(2,1)}, bf16[256,2560]{1,0:T(8,128)(2,1)}, bf16[320,512]{1,0:T(8,128)(2,1)}, f32[32,128]{1,0:T(8,128)}) custom-call(bf16[3136,128]{1,0:T(8,128)(2,1)} %bitcast.379, f32[8,24,128]{2,1,0:T(8,128)} %bitcast.380, f32[8,8,128]{2,1,0:T(8,128)} %bitcast.385), custom_call_target="tpu_custom_call" | custom-call | flops 1000 | bytes 1000 | tf_op jit(solution)/shard_map/spread/pallas_call | solution.py:353
  622.8 10.9 %finish.1 = (f32[256,1536]{1,0:T(8,128)}, f32[256,1536]{1,0:T(8,128)}, f32[1536,256]{1,0:T(8,128)}, f32[256,2048]{1,0:T(8,128)}, bf16[256,2048]{1,0:T(8,128)(2,1...) custom-call(bf16[256,3072]{1,0:T(8,128)(2,1)} %reduce-scatter.7.cloned.1.call-done.mlp_ref, ...), custom_call_target="tpu_custom_call" | custom-call | flops 4194304 | bytes 25165824 | tf_op jit(solution)/shard_map/finish/pallas_call | solution.py:1192
  (178 shorter events, 71.1 us)
Async XLA Ops:
  7.2 103.3 %all-gather.7.cloned.1.call-start = ((), (), s32[]{:S(2)}) async-start(), calls=%async_computation.4 | async-start | bytes 6488064 | tf_op jit(solution)/shard_map/all_gather | solution.py:1253
  9.8 115.6 %all-gather.9.cloned.1.call-start = ((), (), s32[]{:S(2)}) async-start(), calls=%async_computation.5 | async-start | bytes 2949120 | tf_op jit(solution)/shard_map/all_gather | solution.py:1284
  11.5 48.8 %copy-start.21 = (bf16[320]{0:T(512)(128)(2,1)S(1)}, bf16[320]{0:T(512)(128)(2,1)}, u32[]{:S(2)}) copy-start(bf16[320]{0:T(512)(128)(2,1)} %param.27) | copy-start | bytes 1924
  11.6 48.9 %copy-start.14 = (bf16[320,256]{1,0:T(8,128)(2,1)S(1)}, bf16[320,256]{1,0:T(8,128)(2,1)}, u32[]{:S(2)}) copy-start(bf16[320,256]{1,0:T(8,128)(2,1)} %param.23) | copy-start | bytes 491524
  11.6 48.9 %copy-start.15 = (bf16[320,256]{1,0:T(8,128)(2,1)S(1)}, bf16[320,256]{1,0:T(8,128)(2,1)}, u32[]{:S(2)}) copy-start(bf16[320,256]{1,0:T(8,128)(2,1)} %param.24) | copy-start | bytes 491524
  11.6 248.7 %all-gather.11.cloned.1.call-start = ((), (), s32[]{:S(2)}) async-start(), calls=%async_computation.6 | async-start | bytes 14155776 | tf_op jit(solution)/shard_map/all_gather | solution.py:1287
  13.1 284.3 %all-gather.13.cloned.1.call-start = ((), (), s32[]{:S(2)}) async-start(), calls=%async_computation.7 | async-start | bytes 7077888 | tf_op jit(solution)/shard_map/all_gather | solution.py:1290
  61.7 39.9 %collective-permute-start.1 = (bf16[256,2048]{1,0:T(8,128)(2,1)S(1)}, bf16[256,2048]{1,0:T(8,128)(2,1)}, u32[]{:S(2)}, u32[]{:S(2)}) collective-permute-start(bf16[256,2048]{1,0:T(8,128)(2,1)S(1)} %bitcast.366), channel_id=1, source_target_pairs={{0,16},{8,24},{16,0},{24,8},{1,17},{9,25},{17,1},{25,9},{2,18},{10... | collective-permute-start | bytes 3145736 | tf_op jit(solution)/shard_map/ppermute | solution.py:33
  62.5 39.1 %collective-permute-start = (bf16[256,2048]{1,0:T(8,128)(2,1)S(1)}, bf16[256,2048]{1,0:T(8,128)(2,1)}, u32[]{:S(2)}, u32[]{:S(2)}) collective-permute-start(bf16[256,2048]{1,0:T(8,128)(2,1)S(1)} %bitcast.367), channel_id=1, source_target_pairs={{0,8},{8,0},{16,24},{24,16},{1,9},{9,1},{17,25},{25,17},{2,10},{10... | collective-permute-start | bytes 3145736 | tf_op jit(solution)/shard_map/ppermute | solution.py:33
  83.4 16.1 %collective-permute-start.6 = (bf16[768,128]{1,0:T(8,128)(2,1)}, bf16[768,128]{1,0:T(8,128)(2,1)S(1)}, u32[]{:S(2)}, u32[]{:S(2)}) collective-permute-start(bf16[768,128]{1,0:T(8,128)(2,1)} %get-tuple-element.189), channel_id=1, source_target_pairs={{0,8},{8,0},{16,24},{24,16},{1,9},{9,1},{17,25},{25,17},{2,10},{10... | collective-permute-start | bytes 589832 | tf_op jit(solution)/shard_map/ppermute | solution.py:33
  83.9 15.5 %collective-permute-start.5 = (bf16[768,128]{1,0:T(8,128)(2,1)}, bf16[768,128]{1,0:T(8,128)(2,1)S(1)}, u32[]{:S(2)}, u32[]{:S(2)}) collective-permute-start(bf16[768,128]{1,0:T(8,128)(2,1)} %get-tuple-element.190), channel_id=1, source_target_pairs={{0,16},{8,24},{16,0},{24,8},{1,17},{9,25},{17,1},{25,9},{2,18},{10... | collective-permute-start | bytes 589832 | tf_op jit(solution)/shard_map/ppermute | solution.py:33
  85.4 14.1 %collective-permute-start.4 = (bf16[768,128]{1,0:T(8,128)(2,1)}, bf16[768,128]{1,0:T(8,128)(2,1)}, u32[]{:S(2)}, u32[]{:S(2)}) collective-permute-start(bf16[768,128]{1,0:T(8,128)(2,1)} %get-tuple-element.191), channel_id=1, source_target_pairs={{0,24},{8,16},{16,8},{24,0},{1,25},{9,17},{17,9},{25,1},{2,26},{10... | collective-permute-start | bytes 589832 | tf_op jit(solution)/shard_map/ppermute | solution.py:33
  86.9 342.6 %reduce-scatter.5.cloned.1.call-start = ((), (), s32[]{:S(2)}) async-start(), calls=%async_computation.8 | async-start | bytes 7077888 | tf_op jit(solution)/shard_map/reduce_scatter | solution.py:1354
  106.2 19.2 %collective-permute-start.3 = (bf16[128,2048]{1,0:T(8,128)(2,1)S(1)}, bf16[128,2048]{1,0:T(8,128)(2,1)S(1)}, u32[]{:S(2)}, u32[]{:S(2)}) collective-permute-start(bf16[128,2048]{1,0:T(8,128)(2,1)S(1)} %slice.147), channel_id=1, source_target_pairs={{0,8},{8,0},{16,24},{24,16},{1,9},{9,1},{17,25},{25,17},{2,10},{10... | collective-permute-start | bytes 1572872 | tf_op jit(solution)/shard_map/ppermute | solution.py:33
  106.8 18.5 %collective-permute-start.2 = (bf16[128,2048]{1,0:T(8,128)(2,1)S(1)}, bf16[128,2048]{1,0:T(8,128)(2,1)S(1)}, u32[]{:S(2)}, u32[]{:S(2)}) collective-permute-start(bf16[128,2048]{1,0:T(8,128)(2,1)S(1)} %slice.146), channel_id=1, source_target_pairs={{0,16},{8,24},{16,0},{24,8},{1,17},{9,25},{17,1},{25,9},{2,18},{10... | collective-permute-start | bytes 1572872 | tf_op jit(solution)/shard_map/ppermute | solution.py:33
  128.4 46.3 %collective-permute-start.9 = (bf16[640,512]{1,0:T(8,128)(2,1)}, bf16[640,512]{1,0:T(8,128)(2,1)S(1)}, u32[]{:S(2)}, u32[]{:S(2)}) collective-permute-start(bf16[640,512]{1,0:T(8,128)(2,1)} %get-tuple-element.178), channel_id=1, source_target_pairs={{0,8},{8,0},{16,24},{24,16},{1,9},{9,1},{17,25},{25,17},{2,10},{10... | collective-permute-start | bytes 1966088 | tf_op jit(solution)/shard_map/ppermute | solution.py:33
  128.9 45.8 %collective-permute-start.8 = (bf16[640,512]{1,0:T(8,128)(2,1)}, bf16[640,512]{1,0:T(8,128)(2,1)S(1)}, u32[]{:S(2)}, u32[]{:S(2)}) collective-permute-start(bf16[640,512]{1,0:T(8,128)(2,1)} %get-tuple-element.179), channel_id=1, source_target_pairs={{0,16},{8,24},{16,0},{24,8},{1,17},{9,25},{17,1},{25,9},{2,18},{10... | collective-permute-start | bytes 1966088 | tf_op jit(solution)/shard_map/ppermute | solution.py:33
  130.3 45.2 %collective-permute-start.7 = (bf16[640,512]{1,0:T(8,128)(2,1)}, bf16[640,512]{1,0:T(8,128)(2,1)}, u32[]{:S(2)}, u32[]{:S(2)}) collective-permute-start(bf16[640,512]{1,0:T(8,128)(2,1)} %get-tuple-element.180), channel_id=1, source_target_pairs={{0,24},{8,16},{16,8},{24,0},{1,25},{9,17},{17,9},{25,1},{2,26},{10... | collective-permute-start | bytes 1966088 | tf_op jit(solution)/shard_map/ppermute | solution.py:33
  294.6 206.8 %reduce-scatter.7.cloned.1.call-start = ((), (), s32[]{:S(2)}) async-start(), calls=%async_computation.9 | async-start | bytes 14155776 | tf_op jit(solution)/shard_map/reduce_scatter | solution.py:1358
  334.6 239.7 %reduce-scatter.9.cloned.1.call-start = ((), (), s32[]{:S(2)}) async-start(), calls=%async_computation.10 | async-start | bytes 7225344 | tf_op jit(solution)/shard_map/reduce_scatter | solution.py:1383
  501.4 113.0 %reduce-scatter.11.cloned.1.call-start = ((), (), s32[]{:S(2)}) async-start(), calls=%async_computation.11 | async-start | bytes 2949120 | tf_op jit(solution)/shard_map/reduce_scatter | solution.py:1383
  614.4 19.4 %collective-permute-start.12 = (bf16[320,512]{1,0:T(8,128)(2,1)}, bf16[320,512]{1,0:T(8,128)(2,1)S(1)}, u32[]{:S(2)}, u32[]{:S(2)}) collective-permute-start(bf16[320,512]{1,0:T(8,128)(2,1)} %reduce-scatter.11.cloned.1.call-done), channel_id=1, source_target_pairs={{0,8},{8,0},{16,24},{24,16},{1,9},{9,1},{17,25},{25,17},{2,10},{10... | collective-permute-start | bytes 983048 | tf_op jit(solution)/shard_map/ppermute | solution.py:33
  614.9 18.9 %collective-permute-start.11 = (bf16[320,512]{1,0:T(8,128)(2,1)}, bf16[320,512]{1,0:T(8,128)(2,1)S(1)}, u32[]{:S(2)}, u32[]{:S(2)}) collective-permute-start(bf16[320,512]{1,0:T(8,128)(2,1)} %reduce-scatter.11.cloned.1.call-done), channel_id=1, source_target_pairs={{0,16},{8,24},{16,0},{24,8},{1,17},{9,25},{17,1},{25,9},{2,18},{10... | collective-permute-start | bytes 983048 | tf_op jit(solution)/shard_map/ppermute | solution.py:33
  616.4 17.4 %collective-permute-start.10 = (bf16[320,512]{1,0:T(8,128)(2,1)}, bf16[320,512]{1,0:T(8,128)(2,1)S(1)}, u32[]{:S(2)}, u32[]{:S(2)}) collective-permute-start(bf16[320,512]{1,0:T(8,128)(2,1)} %reduce-scatter.11.cloned.1.call-done), channel_id=1, source_target_pairs={{0,24},{8,16},{16,8},{24,0},{1,25},{9,17},{17,9},{25,1},{2,26},{10... | collective-permute-start | bytes 983048 | tf_op jit(solution)/shard_map/ppermute | solution.py:33
  (23 other events, 436.0 us)
Sparse Core Ops, SparseCore 0:
  10.3 66.1 all-gather.6
  78.7 33.1 all-gather.8
  114.1 118.2 all-gather.10
  233.9 63.4 all-gather.12
  299.5 68.0 reduce-scatter.4
  369.8 131.5 reduce-scatter.6
  503.7 69.3 reduce-scatter.8
  575.5 36.0 reduce-scatter.10

commit v7 on v6

--- a/solution.py
+++ b/solution.py
@@ -314,8 +314,9 @@
 
 
 def stream_kernel(
-    mixed_ref, weight_ref, flat_ref, gain_ref,
-    stream_out, temporal_out, normed_out,
+    mixed_ref, weight_ref, flat_ref, gain_ref, own_ref,
+    near_low_ref, near_high_ref, side_low_ref, side_high_ref, far_low_ref, far_high_ref,
+    stream_out, temporal_out, normed_out, joined_out,
     acc, sent, got, sends, recvs,
 ):
     rows = flat_ref.shape[0]
@@ -333,7 +334,13 @@
         normed_out[0, r] = (stream * rms_parts(stream) * gain_ref[...]).astype(BF)
 
     over_chunks(rows, finish)
-    gathered = pass_on(send, 6, normed_out, both_ways(send, 6, normed_out.at[0], normed_out))
+    gathered = both_ways(send, 6, normed_out.at[0], normed_out)
+    joined_out[0] = own_ref[...]
+    halves = (near_low_ref, near_high_ref, side_low_ref, side_high_ref, far_low_ref, far_high_ref)
+    half = rows // 2
+    for i, part in enumerate(halves):
+        joined_out[1 + i // 2, (i % 2) * half : (i % 2 + 1) * half, :] = part[...]
+    gathered = pass_on(send, 6, normed_out, gathered)
     settle(gathered)
     for copy in copies:
         copy.wait_send()
@@ -365,15 +372,20 @@
     )(*operands)
 
 
-def stream_and_norm(mixed, weight, flat, gain):
+def stream_and_norm(mixed, weight, flat, gain, parts):
     rows, width = flat.shape
     groups = mixed.shape[0] // rows
     return remote_call(
         stream_kernel,
         "stream_and_norm",
         1,
-        [((rows, width), F32), ((rows, width), F32), ((groups, rows, width), BF)],
-        (mixed, weight, flat, gain),
+        [
+            ((rows, width), F32),
+            ((rows, width), F32),
+            ((groups, rows, width), BF),
+            ((groups, rows, width), BF),
+        ],
+        (mixed, weight, flat, gain, *parts),
         exchange_scratch(rows, width, 12),
     )
 
@@ -527,7 +539,9 @@
 
     def fetch(c):
         part = pl.ds(pl.multiple_of(c * tile, tile), tile)
-        return pltpu.make_async_copy(weight_far.at[part], weight_ref.at[part], fetches.at[c])
+        return pltpu.make_async_copy(
+            weight_far.at[part, : weight_ref.shape[1]], weight_ref.at[part], fetches.at[c]
+        )
 
     for c in range(parts):
         fetch(c).start()
@@ -611,7 +625,7 @@
         [((rows, width), F32), ((8, width), F32), ((4 * count, columns // 4), BF)],
         (branch_rows, y_rows, flat, gain, weight, mixed, low),
         [
-            pltpu.VMEM(weight.shape, BF),
+            pltpu.VMEM((width, branch_rows.shape[1] + y_rows.shape[1]), BF),
             pltpu.VMEM(mixed.shape, BF),
             pltpu.VMEM(low.shape, BF),
             pltpu.SemaphoreType.DMA((width // 512 + 2,)),
@@ -1250,11 +1264,19 @@
     all_low = all_low.reshape(total, width)
     edge_low = jnp.where(w == 0, 0.0, edge_low.reshape(all_seqs * ROWS16, width).astype(F32))
 
-    x_y_cols = lax.all_gather(
+    dw, rw = width // wide, channels // wide
+    out_part = lax.dynamic_slice_in_dim(out_weight, s * quarter, quarter, 1)
+    rest = rw - dw
+    rest_part = out_part[dw:]
+    temporal_cols = lax.all_gather(
         jnp.concatenate(
             [
                 lax.dynamic_slice_in_dim(branch_weight, base, window, 1),
                 lax.dynamic_slice_in_dim(gelu_weight, s * share, share, 1),
+                out_part[:dw],
+                jnp.concatenate(
+                    [rest_part[:, i : i + LANES] for i in range(0, quarter, LANES)], axis=0
+                ),
             ],
             axis=1,
         ),
@@ -1262,7 +1284,12 @@
         axis=0,
         tiled=True,
     )
-    dw, rw = width // wide, channels // wide
+    out_body = temporal_cols[:, window + share : window + share + quarter]
+    out_rest = temporal_cols[:, window + share + quarter :]
+    out_rest = out_rest.reshape(wide, quarter // LANES, rest, LANES).transpose(0, 2, 1, 3)
+    out_quarter = jnp.concatenate(
+        [out_body.reshape(wide, dw, quarter), out_rest.reshape(wide, rest, quarter)], axis=1
+    ).reshape(channels, quarter)
     small = jnp.concatenate(
         [norm_gain, mlp_gain, forget_bias, admit_bias, decay_rate, conv_bias, conv_weight.reshape(-1)]
     ).reshape(-1, gate_cols)
@@ -1271,8 +1298,9 @@
         [lax.dynamic_slice_in_dim(gates_quarter, s * gate_cols, gate_cols, 1), small], axis=0
     )
     small, edge_low, later_upstream = lax.optimization_barrier((small, edge_low, upstream))
-    upstream_near = swap(later_upstream, 1)
-    upstream_side = swap(later_upstream, 2)
+    half = rows // 2
+    upstream_near = [swap(later_upstream[:half], 1), swap(later_upstream[half:], 1)]
+    upstream_side = [swap(later_upstream[:half], 2), swap(later_upstream[half:], 2)]
     small = lax.all_gather(small, "wide")
     gates_quarter = small[:, :rw].reshape(channels, gate_cols)
     small = small[:, rw:].reshape(wide, -1).astype(F32)
@@ -1281,9 +1309,6 @@
     per_channel = small[:, 2 * dw :].reshape(wide, 8, rw).transpose(1, 0, 2).reshape(8, channels)
     per_channel = lax.dynamic_slice_in_dim(per_channel, s * share, share, 1)
 
-    out_quarter = lax.all_gather(
-        lax.dynamic_slice_in_dim(out_weight, s * quarter, quarter, 1), "wide", axis=0, tiled=True
-    )
     mlp_full = lax.all_gather(
         jnp.concatenate([gate_weight, up_weight], axis=1), "wide", axis=0, tiled=True
     )
@@ -1305,24 +1330,19 @@
     )
     normed_all = rms_norm(all_low.astype(F32), gain_one).astype(BF)
     normed_edge = rms_norm(edge_low, gain_one).astype(BF)
-    normed_all, upstream_near, upstream_side = lax.optimization_barrier(
-        (normed_all, upstream_near, upstream_side)
-    )
-    half = rows // 2
-    upstream_far = [swap(upstream_near[:half], 2), swap(upstream_side[half:], 1)]
-
-    x_y = dot(normed_all, x_y_cols)
+
+    x_y = dot(normed_all, temporal_cols[:, : window + share])
     x_win = x_y[:, :window].astype(BF)
     branch_y = x_y[:, window:]
-    x_win, out_quarter, *upstream_far = lax.optimization_barrier(
-        (x_win, out_quarter, *upstream_far)
-    )
-    upstream_all = jnp.concatenate([upstream, upstream_near, upstream_side, *upstream_far], axis=0)
+    x_win, out_quarter, *upstream_parts = lax.optimization_barrier(
+        (x_win, out_quarter, *upstream_near, *upstream_side)
+    )
+    upstream_parts += [swap(upstream_parts[0], 2), swap(upstream_parts[3], 1)]
     out_rows = jnp.concatenate(
         in_order(swapped(lambda j: lax.dynamic_slice_in_dim(out_quarter, j * share, share, 0))),
         axis=1,
     )
-    edge_win = dot(normed_edge, x_y_cols[:, :window]).astype(BF).astype(F32)
+    edge_win = dot(normed_edge, temporal_cols[:, :window]).astype(BF).astype(F32)
     edge_win = edge_win.reshape(all_seqs, ROWS16, window)[:, ROWS16 - HALO :]
     edge_win = edge_win.reshape(all_seqs * HALO, window)
     offset = off.reshape(1)
@@ -1330,6 +1350,7 @@
         offset, x_win, edge_win, gates, per_channel, tokens
     )
     ends = lax.all_gather(ends, "wide")[:, :, :, 0]
+    ends, *upstream_parts = lax.optimization_barrier((ends, *upstream_parts))
     carry = jnp.zeros((all_seqs, share), F32)
     for j in range(wide - 1):
         carry = jnp.where(j < w, ends[j, :, 0] * carry + ends[j, :, 1], carry)
@@ -1340,7 +1361,10 @@
 
     gelu_y = jax.nn.gelu(branch_y)
     mixed_low = (state * gelu_y).astype(BF)
-    stream, temporal, normed_two_all = stream_and_norm(mixed_low, out_rows, flat_low, gain_two)
+    stream, temporal, normed_two_all, upstream_all = stream_and_norm(
+        mixed_low, out_rows, flat_low, gain_two, [upstream, *upstream_parts]
+    )
+    upstream_all = upstream_all.reshape(total, width)
     normed_two_all = normed_two_all.reshape(total, width)
 
     gate_up = dot(normed_two_all, mlp_full)
@@ -1399,7 +1423,7 @@
     branch_late, early_sums, stacked = lax.optimization_barrier((branch_rows, early_sums, stacked))
     temporal_sum = sum_over_wide(stacked)
     first_back, gain_one_grad, out_cols = inputs_back(
-        branch_late, y_rows, x_y_cols, flat_low, gain_one, mixed_low, stream_low_all
+        branch_late, y_rows, temporal_cols, flat_low, gain_one, mixed_low, stream_low_all
     )
     out_sum = sum_over_wide(out_cols)
     late_sums = jnp.sum(gain_one_grad, axis=0).reshape(wide, dw)

time: 653 us -> 643 us (0.985)
  local copies, waits for them, and re-layouts: 40.3 us -> 30.2 us
    unnamed x66 -> x62, local copies, waits for them, and re-layouts: 19.5 us -> 8.99 us
    ppermute x13 -> x15, starting transfers between devices: 14.7 us -> 17.9 us  [swap(): lax.ppermute(values, 'seq', [(i, i ^ mask) for i in range(lax.axis_size('...]
  transfers between devices with their start and end apart: 21 -> 22, of which waited for: 2 -> 1; matrix products, arithmetic and copies ran while one was open for 19% -> 17% of each run, Pallas kernels for 68% -> 69%
where the time goes in v7:
time: 643 us; the launch traced here: 634 us
  Pallas kernels  436 us (68%)
  matrix products  59.7 us (9%)
  blocking collectives  38.4 us (6%)
  other arithmetic  32.2 us (5%)
  local copies, waits for them, and re-layouts  30.2 us (5%)
  starting transfers between devices  18.5 us (3%)
  between operations  16 us (2%)
    pallas_call x5, Pallas kernels, remote_call(): pl.pallas_call(kernel, in_specs=[pl.BlockSpec(memory_space=pltpu.VMEM)] *...  326 us
    pallas_call x1, Pallas kernels, middle(): pl.pallas_call(middle_kernel, in_specs=[vmem] * 12 + [anywhere] * 6, out_...  49.8 us
    dot_general x3, matrix products, dot(): return jnp.dot(left, right, preferred_element_type=F32)  31.4 us
    dot_general x2, matrix products, contract_rows(): lax.dot_general(left, right, (((0,), (0,)), ((), ())), preferred_element_...  28.3 us
    all_gather x1, blocking collectives, body(): small = lax.all_gather(small, 'wide')  20 us
    all_gather x1, blocking collectives, body(): ends = lax.all_gather(ends, 'wide')[:, :, :, 0]  18.4 us
    ppermute x15, starting transfers between devices, swap(): lax.ppermute(values, 'seq', [(i, i ^ mask) for i in range(lax.axis_size('...  17.9 us
    pallas_call x1, Pallas kernels, temporal_grads(): pl.pallas_call(functools.partial(grads_kernel, bases), grid=(width // BW,...  17.7 us
  transfers between devices with their start and end apart: 22, of which 1 were waited for; matrix products, arithmetic and copies ran while one was open for 17% of the time, Pallas kernels for 69%

profile of v7, /device:TPU:0, one launch (start us, length us, event | category | flops | bytes accessed | tf_op | source)
XLA Modules:
  0.0 634.1 jit_solution(3008355037294523908)
XLA Ops:
  13.2 47.1 %start.1 = (bf16[4,256,2048]{2,1,0:T(8,128)(2,1)}, bf16[4,32,2048]{2,1,0:T(8,128)(2,1)}) custom-call(bf16[256,2048]{1,0:T(8,128)(2,1)} %bitcast.343), custom_call_target="tpu_custom_call" | custom-call | flops 1000 | bytes 1000 | tf_op jit(solution)/shard_map/start/pallas_call | solution.py:360
  65.1 20.0 %all-gather = bf16[2752,128]{1,0:T(8,128)(2,1)S(1)} all-gather(bf16[344,128]{1,0:T(8,128)(2,1)S(1)} %pad_maximum_fusion.4), channel_id=2, replica_groups=mesh['seq'=4,'wide'=8] {'wide'}, dimensions={0}, use_global_device_ids=true | all-gather | bytes 792576 | tf_op jit(solution)/shard_map/all_gather | solution.py:1304
  89.6 3.3 multiply_reduce_fusion
  93.1 3.0 fusion.1.normed_ref
  102.5 11.8 %fusion.11 = f32[1024,1408]{1,0:T(8,128)} fusion(bf16[1024,2048]{1,0:T(8,128)(2,1)} %fusion.1.normed_ref, bf16[2048,2048]{1,0:T(8,128)(2,1)} %all-gather.6.cloned.1.call-done.weight_far), kind=kOutput, calls=%fused_computation.16 | convolution fusion | flops 5905580032 | bytes 15728640 | tf_op jit(solution)/shard_map/dot_general | solution.py:21
  114.9 3.2 slice.327.x_ref.x_far
  127.3 2.6 fusion.26
  130.6 14.3 %temporal_forward.1 = (bf16[1024,640]{1,0:T(8,128)(2,1)}, bf16[1024,640]{1,0:T(8,128)(2,1)}, f32[1024,640]{1,0:T(8,128)}, f32[1024,640]{1,0:T(8,128)}, f32[1024,...) custom-call(s32[1]{0:T(128)} %bitcast.6.off_ref, bf16[1024,768]{1,0:T(8,128)(2,1)} %slice.327.x_ref.x_far, ...), custom_call_target="tpu_custom_call" | custom-call | flops 1000 | bytes 1000 | tf_op jit(solution)/shard_map/temporal_forward/pallas_call | solution.py:139
  145.7 18.4 %all-gather.1 = f32[64,2,1,640]{3,1,2,0:T(2,128)S(1)} all-gather(f32[8,2,1,640]{3,1,2,0:T(2,128)S(1)} %copy.91), channel_id=3, replica_groups=mesh['seq'=4,'wide'=8] {'wide'}, dimensions={0}, use_global_device_ids=true | all-gather | bytes 368640 | tf_op jit(solution)/shard_map/all_gather | solution.py:1352
  164.2 6.4 %fusion.48 = (f32[1024,640]{1,0:T(8,128)}, bf16[1024,640]{1,0:T(8,128)(2,1)}) fusion(f32[1024,1408]{1,0:T(8,128)} %fusion.11, f32[1024,640]{1,0:T(8,128)} %get-tuple-element.106.local_ref, f32[1024,640]{1,0:T(8,128)} %get-tuple-element.107.reach_ref, f32[8,640]{1,0:T(8,128)S(1)} %fusion.40), kind=kLoop, calls=%fused_computation.157 | loop fusion | flops 9175040 | bytes 11816960 | tf_op jit(solution)/shard_map/slice | solution.py:1336
  174.2 84.6 %stream_and_norm.1 = (f32[256,2048]{1,0:T(8,128)}, f32[256,2048]{1,0:T(8,128)}, bf16[4,256,2048]{2,1,0:T(8,128)(2,1)}, bf16[4,256,2048]{2,1,0:T(8,128)(2,1)}) custom-call(bf16[1024,640]{1,0:T(8,128)(2,1)} %get-tuple-element.187.mixed_ref.mixed_far, bf16[640,2048]{1,0:T(8,128)(2,1)} %pad_maximum_fusion.1.weight_ref.out_far, bf16[256,2048]{1,0:T(8,128)(2,1)} %bitcast.344, ...), custom_call_target="tpu_custom_call" | custom-call | flops 1000 | bytes 1000 | tf_op jit(solution)/shard_map/stream_and_norm/pallas_call | solution.py:360
  258.8 17.0 %fusion.51.gate_ref.up_ref = f32[1024,3072]{1,0:T(8,128)S(1)} fusion(bf16[1024,2048]{1,0:T(8,128)(2,1)} %bitcast.376, bf16[2048,3072]{1,0:T(8,128)(2,1)} %all-gather.8.cloned.1.call-done.weight_far), kind=kOutput, calls=%fused_computation.160 | convolution fusion | flops 12884901888 | bytes 29360128 | tf_op jit(solution)/shard_map/dot_general | solution.py:21
  275.8 2.2 fusion.10.hidden_far
  278.1 3.5 copy-done.2
  283.2 8.7 %convolution_convert_fusion.1 = bf16[1536,2048]{1,0:T(8,128)(2,1)} fusion(bf16[1024,1536]{1,0:T(8,128)(2,1)S(1)} %fusion.10.hidden_far, bf16[1024,2048]{1,0:T(8,128)(2,1)S(1)} %bitcast.347), kind=kOutput, calls=%fused_computation.6 | convolution fusion | flops 6445596672 | bytes 13631488 | tf_op jit(solution)/shard_map/dot_general | solution.py:29
  292.2 17.2 %mlp_rows.1.rows_ref = bf16[1024,3072]{1,0:T(8,128)(2,1)} custom-call(bf16[1024,2048]{1,0:T(8,128)(2,1)} %bitcast.346, bf16[1536,2048]{1,0:T(8,128)(2,1)} %all-gather.10.cloned.1.call-done.down_ref.down_far, f32[1024,3072]{1,0:T(8,128)} %copy-done.2, f32[1024,3072]{1,0:T(8,128)} %copy-done.2), custom_call_target="tpu_custom_call" | custom-call | flops 1000 | bytes 1000 | tf_op jit(solution)/shard_map/mlp_rows/pallas_call | solution.py:410
  309.4 19.6 %convolution_convert_fusion = bf16[2048,3072]{1,0:T(8,128)(2,1)} fusion(bf16[1024,2048]{1,0:T(8,128)(2,1)} %bitcast.377, bf16[1024,3072]{1,0:T(8,128)(2,1)} %mlp_rows.1.rows_ref), kind=kOutput, calls=%fused_computation | convolution fusion | flops 12891193344 | bytes 23068672 | tf_op jit(solution)/shard_map/dot_general | solution.py:29
  332.5 87.5 %stream_back.1 = (f32[256,2048]{1,0:T(8,128)}, bf16[4,256,2048]{2,1,0:T(8,128)(2,1)}, f32[8,2048]{1,0:T(8,128)}, bf16[4,256,2048]{2,1,0:T(8,128)(2,1)}, f32[4,256,640]{2,1,0:T(8,128)}) custom-call(bf16[1024,3072]{1,0:T(8,128)(2,1)} %mlp_rows.1.rows_ref, f32[256,2048]{1,0:T(8,128)} %get-tuple-element.125.stream_ref.stream_far, f32[1,2048]{1,0:T(1,128)} %bitcast.368, ...), custom_call_target="tpu_custom_call" | custom-call | flops 1000 | bytes 1000 | tf_op jit(solution)/shard_map/stream_back/pallas_call | solution.py:360
  421.0 49.8 %middle.1 = (bf16[1024,640]{1,0:T(8,128)(2,1)}, bf16[1024,768]{1,0:T(8,128)(2,1)}, bf16[1024,768]{1,0:T(8,128)(2,1)}, bf16[1024,768]{1,0:T(8,128)(2,1)}, f32[8,6...) custom-call(f32[1024,640]{1,0:T(8,128)} %bitcast.358, f32[1024,640]{1,0:T(8,128)} %get-tuple-element.186.y_ref, ...), custom_call_target="tpu_custom_call" | custom-call | flops 1000 | bytes 1000 | tf_op jit(solution)/shard_map/middle/pallas_call | solution.py:936
  470.8 17.7 %temporal_grads.1 = bf16[8,3136,128]{2,1,0:T(8,128)(2,1)} custom-call(bf16[1024,2048]{1,0:T(8,128)(2,1)} %fusion.1.normed_ref, bf16[1024,640]{1,0:T(8,128)(2,1)} %get-tuple-element.136.y_ref, bf16[1024,768]{1,0:T(8,128)(2,1)} %get-tuple-element.148.branch_ref, bf16[1024,768]{1,0:T(8,128)(2,1)} %slice.327.x_ref.x_far, ...), custom_call_target="tpu_custom_call" | custom-call | flops 1000 | bytes 1000 | tf_op jit(solution)/shard_map/temporal_grads/pallas_call | solution.py:1057
  490.2 3.0 reduce-scatter.7.cloned.1.call-done.mlp_ref
  493.9 70.2 %inputs_back.1 = (f32[256,2048]{1,0:T(8,128)}, f32[8,2048]{1,0:T(8,128)}, bf16[2560,512]{1,0:T(8,128)(2,1)}) custom-call(bf16[1024,768]{1,0:T(8,128)(2,1)} %get-tuple-element.148.branch_ref, bf16[1024,640]{1,0:T(8,128)(2,1)} %get-tuple-element.136.y_ref, bf16[256,2048]{1,0:T(8,128)(2,1)} %bitcast.345, f32[1,2048]{1,0:T(1,128)} %bitcast.372, ...), custom_call_target="tpu_custom_call" | custom-call | flops 1000 | bytes 1000 | tf_op jit(solution)/shard_map/inputs_back/pallas_call | solution.py:360
  565.7 36.4 %spread.1 = (bf16[256,2560]{1,0:T(8,128)(2,1)}, bf16[256,2560]{1,0:T(8,128)(2,1)}, bf16[320,512]{1,0:T(8,128)(2,1)}, f32[32,128]{1,0:T(8,128)}) custom-call(bf16[3136,128]{1,0:T(8,128)(2,1)} %bitcast.360, f32[8,24,128]{2,1,0:T(8,128)} %bitcast.361, f32[8,8,128]{2,1,0:T(8,128)} %bitcast.366), custom_call_target="tpu_custom_call" | custom-call | flops 1000 | bytes 1000 | tf_op jit(solution)/shard_map/spread/pallas_call | solution.py:360
  613.9 10.9 %finish.1 = (f32[256,1536]{1,0:T(8,128)}, f32[256,1536]{1,0:T(8,128)}, f32[1536,256]{1,0:T(8,128)}, f32[256,2048]{1,0:T(8,128)}, bf16[256,2048]{1,0:T(8,128)(2,1...) custom-call(bf16[256,3072]{1,0:T(8,128)(2,1)} %reduce-scatter.7.cloned.1.call-done.mlp_ref, ...), custom_call_target="tpu_custom_call" | custom-call | flops 4194304 | bytes 25165824 | tf_op jit(solution)/shard_map/finish/pallas_call | solution.py:1206
  (181 shorter events, 59.6 us)
Async XLA Ops:
  7.2 95.3 %all-gather.6.cloned.1.call-start = ((), (), s32[]{:S(2)}) async-start(), calls=%async_computation.4 | async-start | bytes 9437184 | tf_op jit(solution)/shard_map/all_gather | solution.py:1271
  11.7 48.9 %copy-start.14 = (bf16[320,256]{1,0:T(8,128)(2,1)S(1)}, bf16[320,256]{1,0:T(8,128)(2,1)}, u32[]{:S(2)}) copy-start(bf16[320,256]{1,0:T(8,128)(2,1)} %param.23) | copy-start | bytes 491524
  11.7 48.9 %copy-start.15 = (bf16[320,256]{1,0:T(8,128)(2,1)S(1)}, bf16[320,256]{1,0:T(8,128)(2,1)}, u32[]{:S(2)}) copy-start(bf16[320,256]{1,0:T(8,128)(2,1)} %param.24) | copy-start | bytes 491524
  11.7 247.1 %all-gather.8.cloned.1.call-start = ((), (), s32[]{:S(2)}) async-start(), calls=%async_computation.5 | async-start | bytes 14155776 | tf_op jit(solution)/shard_map/all_gather | solution.py:1312
  13.1 279.0 %all-gather.10.cloned.1.call-start = ((), (), s32[]{:S(2)}) async-start(), calls=%async_computation.6 | async-start | bytes 7077888 | tf_op jit(solution)/shard_map/all_gather | solution.py:1315
  63.0 56.9 %collective-permute-start.3 = (bf16[128,2048]{1,0:T(8,128)(2,1)}, bf16[128,2048]{1,0:T(8,128)(2,1)}, u32[]{:S(2)}, u32[]{:S(2)}) collective-permute-start(bf16[128,2048]{1,0:T(8,128)(2,1)} %get-tuple-element.207), channel_id=1, source_target_pairs={{0,16},{8,24},{16,0},{24,8},{1,17},{9,25},{17,1},{25,9},{2,18},{10... | collective-permute-start | bytes 1572872 | tf_op jit(solution)/shard_map/ppermute | solution.py:33
  63.7 56.3 %collective-permute-start.1 = (bf16[128,2048]{1,0:T(8,128)(2,1)}, bf16[128,2048]{1,0:T(8,128)(2,1)}, u32[]{:S(2)}, u32[]{:S(2)}) collective-permute-start(bf16[128,2048]{1,0:T(8,128)(2,1)} %get-tuple-element.207), channel_id=1, source_target_pairs={{0,8},{8,0},{16,24},{24,16},{1,9},{9,1},{17,25},{25,17},{2,10},{10... | collective-permute-start | bytes 1572872 | tf_op jit(solution)/shard_map/ppermute | solution.py:33
  86.0 11.6 %collective-permute-start.6 = (bf16[768,128]{1,0:T(8,128)(2,1)}, bf16[768,128]{1,0:T(8,128)(2,1)S(1)}, u32[]{:S(2)}, u32[]{:S(2)}) collective-permute-start(bf16[768,128]{1,0:T(8,128)(2,1)} %get-tuple-element.209), channel_id=1, source_target_pairs={{0,8},{8,0},{16,24},{24,16},{1,9},{9,1},{17,25},{25,17},{2,10},{10... | collective-permute-start | bytes 589832 | tf_op jit(solution)/shard_map/ppermute | solution.py:33
  87.2 11.6 %collective-permute-start.5 = (bf16[768,128]{1,0:T(8,128)(2,1)S(1)}, bf16[768,128]{1,0:T(8,128)(2,1)S(1)}, u32[]{:S(2)}, u32[]{:S(2)}) collective-permute-start(bf16[768,128]{1,0:T(8,128)(2,1)S(1)} %get-tuple-element.210), channel_id=1, source_target_pairs={{0,16},{8,24},{16,0},{24,8},{1,17},{9,25},{17,1},{25,9},{2,18},{10... | collective-permute-start | bytes 589832 | tf_op jit(solution)/shard_map/ppermute | solution.py:33
  88.7 11.6 %collective-permute-start.4 = (bf16[768,128]{1,0:T(8,128)(2,1)S(1)}, bf16[768,128]{1,0:T(8,128)(2,1)}, u32[]{:S(2)}, u32[]{:S(2)}) collective-permute-start(bf16[768,128]{1,0:T(8,128)(2,1)S(1)} %get-tuple-element.211), channel_id=1, source_target_pairs={{0,24},{8,16},{16,8},{24,0},{1,25},{9,17},{17,9},{25,1},{2,26},{10... | collective-permute-start | bytes 589832 | tf_op jit(solution)/shard_map/ppermute | solution.py:33
  89.5 331.4 %reduce-scatter.5.cloned.1.call-start = ((), (), s32[]{:S(2)}) async-start(), calls=%async_computation.7 | async-start | bytes 7077888 | tf_op jit(solution)/shard_map/reduce_scatter | solution.py:1378
  97.6 22.3 %collective-permute-start.2 = (bf16[128,2048]{1,0:T(8,128)(2,1)}, bf16[128,2048]{1,0:T(8,128)(2,1)}, u32[]{:S(2)}, u32[]{:S(2)}) collective-permute-start(bf16[128,2048]{1,0:T(8,128)(2,1)} %get-tuple-element.208), channel_id=1, source_target_pairs={{0,16},{8,24},{16,0},{24,8},{1,17},{9,25},{17,1},{25,9},{2,18},{10... | collective-permute-start | bytes 1572872 | tf_op jit(solution)/shard_map/ppermute | solution.py:33
  98.9 21.1 %collective-permute-start = (bf16[128,2048]{1,0:T(8,128)(2,1)}, bf16[128,2048]{1,0:T(8,128)(2,1)}, u32[]{:S(2)}, u32[]{:S(2)}) collective-permute-start(bf16[128,2048]{1,0:T(8,128)(2,1)} %get-tuple-element.208), channel_id=1, source_target_pairs={{0,8},{8,0},{16,24},{24,16},{1,9},{9,1},{17,25},{25,17},{2,10},{10... | collective-permute-start | bytes 1572872 | tf_op jit(solution)/shard_map/ppermute | solution.py:33
  120.0 44.2 %collective-permute-start.7 = (bf16[128,2048]{1,0:T(8,128)(2,1)}, bf16[128,2048]{1,0:T(8,128)(2,1)}, u32[]{:S(2)}, u32[]{:S(2)}) collective-permute-start(bf16[128,2048]{1,0:T(8,128)(2,1)} %collective-permute-done.near_low_ref), channel_id=1, source_target_pairs={{0,16},{8,24},{16,0},{24,8},{1,17},{9,25},{17,1},{25,9},{2,18},{10... | collective-permute-start | bytes 1572872 | tf_op jit(solution)/shard_map/ppermute | solution.py:33
  121.1 43.0 %collective-permute-start.8 = (bf16[128,2048]{1,0:T(8,128)(2,1)}, bf16[128,2048]{1,0:T(8,128)(2,1)}, u32[]{:S(2)}, u32[]{:S(2)}) collective-permute-start(bf16[128,2048]{1,0:T(8,128)(2,1)} %collective-permute-done.3.side_high_ref), channel_id=1, source_target_pairs={{0,8},{8,0},{16,24},{24,16},{1,9},{9,1},{17,25},{25,17},{2,10},{10... | collective-permute-start | bytes 1572872 | tf_op jit(solution)/shard_map/ppermute | solution.py:33
  123.8 46.8 %collective-permute-start.11 = (bf16[640,512]{1,0:T(8,128)(2,1)}, bf16[640,512]{1,0:T(8,128)(2,1)S(1)}, u32[]{:S(2)}, u32[]{:S(2)}) collective-permute-start(bf16[640,512]{1,0:T(8,128)(2,1)} %get-tuple-element.192), channel_id=1, source_target_pairs={{0,8},{8,0},{16,24},{24,16},{1,9},{9,1},{17,25},{25,17},{2,10},{10... | collective-permute-start | bytes 1966088 | tf_op jit(solution)/shard_map/ppermute | solution.py:33
  124.3 46.3 %collective-permute-start.10 = (bf16[640,512]{1,0:T(8,128)(2,1)}, bf16[640,512]{1,0:T(8,128)(2,1)S(1)}, u32[]{:S(2)}, u32[]{:S(2)}) collective-permute-start(bf16[640,512]{1,0:T(8,128)(2,1)} %get-tuple-element.193), channel_id=1, source_target_pairs={{0,16},{8,24},{16,0},{24,8},{1,17},{9,25},{17,1},{25,9},{2,18},{10... | collective-permute-start | bytes 1966088 | tf_op jit(solution)/shard_map/ppermute | solution.py:33
  125.3 45.3 %collective-permute-start.9 = (bf16[640,512]{1,0:T(8,128)(2,1)S(1)}, bf16[640,512]{1,0:T(8,128)(2,1)S(1)}, u32[]{:S(2)}, u32[]{:S(2)}) collective-permute-start(bf16[640,512]{1,0:T(8,128)(2,1)S(1)} %get-tuple-element.194), channel_id=1, source_target_pairs={{0,24},{8,16},{16,8},{24,0},{1,25},{9,17},{17,9},{25,1},{2,26},{10... | collective-permute-start | bytes 1966088 | tf_op jit(solution)/shard_map/ppermute | solution.py:33
  291.9 201.3 %reduce-scatter.7.cloned.1.call-start = ((), (), s32[]{:S(2)}) async-start(), calls=%async_computation.8 | async-start | bytes 14155776 | tf_op jit(solution)/shard_map/reduce_scatter | solution.py:1382
  329.0 236.7 %reduce-scatter.9.cloned.1.call-start = ((), (), s32[]{:S(2)}) async-start(), calls=%async_computation.9 | async-start | bytes 7225344 | tf_op jit(solution)/shard_map/reduce_scatter | solution.py:1407
  493.3 112.2 %reduce-scatter.11.cloned.1.call-start = ((), (), s32[]{:S(2)}) async-start(), calls=%async_computation.10 | async-start | bytes 2949120 | tf_op jit(solution)/shard_map/reduce_scatter | solution.py:1407
  605.5 19.3 %collective-permute-start.14 = (bf16[320,512]{1,0:T(8,128)(2,1)}, bf16[320,512]{1,0:T(8,128)(2,1)S(1)}, u32[]{:S(2)}, u32[]{:S(2)}) collective-permute-start(bf16[320,512]{1,0:T(8,128)(2,1)} %reduce-scatter.11.cloned.1.call-done), channel_id=1, source_target_pairs={{0,8},{8,0},{16,24},{24,16},{1,9},{9,1},{17,25},{25,17},{2,10},{10... | collective-permute-start | bytes 983048 | tf_op jit(solution)/shard_map/ppermute | solution.py:33
  606.1 18.7 %collective-permute-start.13 = (bf16[320,512]{1,0:T(8,128)(2,1)}, bf16[320,512]{1,0:T(8,128)(2,1)S(1)}, u32[]{:S(2)}, u32[]{:S(2)}) collective-permute-start(bf16[320,512]{1,0:T(8,128)(2,1)} %reduce-scatter.11.cloned.1.call-done), channel_id=1, source_target_pairs={{0,16},{8,24},{16,0},{24,8},{1,17},{9,25},{17,1},{25,9},{2,18},{10... | collective-permute-start | bytes 983048 | tf_op jit(solution)/shard_map/ppermute | solution.py:33
  607.5 17.4 %collective-permute-start.12 = (bf16[320,512]{1,0:T(8,128)(2,1)}, bf16[320,512]{1,0:T(8,128)(2,1)S(1)}, u32[]{:S(2)}, u32[]{:S(2)}) collective-permute-start(bf16[320,512]{1,0:T(8,128)(2,1)} %reduce-scatter.11.cloned.1.call-done), channel_id=1, source_target_pairs={{0,24},{8,16},{16,8},{24,0},{1,25},{9,17},{17,9},{25,1},{2,26},{10... | collective-permute-start | bytes 983048 | tf_op jit(solution)/shard_map/ppermute | solution.py:33
  (26 other events, 531.6 us)
Sparse Core Ops, SparseCore 0:
  11.7 90.3 all-gather.5
  104.3 117.8 all-gather.7
  223.8 63.3 all-gather.9
  292.1 67.4 reduce-scatter.4
  361.7 131.5 reduce-scatter.6
  495.4 69.3 reduce-scatter.8
  567.3 35.8 reduce-scatter.10
